TPU v7x, 1024 devices: a whole 4x8x16 slice. The times are simulated.
1024 devices in a mesh: gx: 8 (over y), gy: 16 (over z), gz: 8 (over x, core).
Axes of the slice: x: 4, y: 8, z: 16, core: 2. Of those that a mesh axis runs over, the one named last changes fastest.
Arguments:
- populations: float32 [27, 64, 128, 1024], P(None, 'gx', 'gy', 'gz'), may hold values from 0 to 0.4, as said below
- solid_mask: int32 [64, 128, 1024], P('gx', 'gy', 'gz'), may hold values 0 or 1
- jet_mask: int32 [64, 128, 1024], P('gx', 'gy', 'gz'), may hold values 0 or 1
- visibility: int32 [8], replicated, may hold values from 0 to 7, each once
Outputs:
- advanced: float32 [27, 64, 128, 1024], P(None, 'gx', 'gy', 'gz')
- image: float32 [4, 256, 512], P(None, 'gx', ('gy', 'gz'))
Inputs may be any that keep to these rules, and one draw needn't show every extreme that they name: `populations`: each population is positive and below 1.6 times its direction's weight.
All inputs are finite; a program needn't handle non-finite values. No bound on the sum of `solid_mask` or of `jet_mask` on one device may be relied on, other than what follows from the above.
Results may differ from a plain program's by a relative error of at most 0.0001.
Values sent between devices are 32-bit elements; how exact they have to be, the bound alone decides.
No kernel may reach another device: no remote copies, remote signals or barrier semaphores. Data moves between devices by JAX's collectives and lax.ppermute only.
A program may use at most 32 MiB of HBM per device.

v0:
```python
import jax
import jax.numpy as jnp
import numpy as np
from jax import lax
from jax.sharding import PartitionSpec as P

STEPS = 2
UP = 4


omega_rate = 1.25
jet_speed = 0.12
alpha_top = 0.03
solid_alpha = 0.15
shade_scale = 0.002


def padded_2(block, sides, width):
    for axis, dim in sides:
        count = lax.axis_size(axis)
        forward = [(i, i + 1) for i in range(count - 1)]
        forward.append((count - 1, 0))
        backward = [(target, source) for source, target in forward]
        low = lax.ppermute(
            lax.slice_in_dim(block, block.shape[dim] - width, None, axis=dim), axis, forward
        )
        high = lax.ppermute(lax.slice_in_dim(block, 0, width, axis=dim), axis, backward)
        block = jnp.concatenate([low, block, high], axis=dim)
    return block


def lattice_tables():
    dirs = np.array(
        [(a, b, c) for a in (-1, 0, 1) for b in (-1, 0, 1) for c in (-1, 0, 1)], dtype=np.int64
    )
    table = np.array([8.0 / 27.0, 2.0 / 27.0, 1.0 / 54.0, 1.0 / 216.0])
    weights = table[np.abs(dirs).sum(axis=1)]
    return (dirs, weights)


def equilibrium(density, vel_first, vel_second, vel_third):
    dirs, weights = lattice_tables()
    cfirst = jnp.asarray(dirs[:, 0], jnp.float32).reshape(27, 1, 1, 1)
    csecond = jnp.asarray(dirs[:, 1], jnp.float32).reshape(27, 1, 1, 1)
    cthird = jnp.asarray(dirs[:, 2], jnp.float32).reshape(27, 1, 1, 1)
    wtable = jnp.asarray(weights, jnp.float32).reshape(27, 1, 1, 1)
    along = cfirst * vel_first + csecond * vel_second + cthird * vel_third
    square = vel_first * vel_first + vel_second * vel_second + vel_third * vel_third
    return wtable * density * (1.0 + 3.0 * along + 4.5 * along * along - 1.5 * square)


def moments(popul):
    dirs, weights = lattice_tables()
    density = jnp.sum(popul, axis=0)
    comps = []
    for axis_id in range(3):
        table = jnp.asarray(dirs[:, axis_id], jnp.float32).reshape(27, 1, 1, 1)
        comps.append(jnp.sum(table * popul, axis=0) / density)
    return (density, comps)


def collide(popul, solid_mask, jet_mask):
    density, comps = moments(popul)
    post = popul + omega_rate * (equilibrium(density, comps[0], comps[1], comps[2]) - popul)
    zeros_field = jnp.zeros_like(density)
    jet_state = equilibrium(density, zeros_field + jet_speed, zeros_field, zeros_field)
    post = jnp.where(jet_mask[None] == 1, jet_state, post)
    post = jnp.where(solid_mask[None] == 1, popul[::-1], post)
    return post


def shade(s_two, flow_first, solid_mask):
    ratio = s_two / (s_two + shade_scale)
    fluid_alpha = alpha_top * (1.0 - jnp.exp(-s_two / shade_scale))
    solid_on = solid_mask == 1
    alpha = jnp.where(solid_on, solid_alpha, fluid_alpha)
    red = jnp.where(solid_on, 0.6, 0.3 + 1.5 * ratio)
    green = jnp.where(solid_on, 0.6, 1.2 - 0.9 * ratio)
    blue = jnp.where(solid_on, 0.6, 0.8 + 0.4 * jnp.tanh(20.0 * flow_first))
    colour = jnp.stack([red, green, blue], axis=0) * alpha[None]
    return (alpha, colour)


def slab_pass(alpha, colour):
    logs = jnp.log1p(-alpha)
    running = jnp.cumsum(logs, axis=-1)
    weight = jnp.exp(running - logs)
    slab_colour = jnp.sum(colour * weight[None], axis=-1)
    return (running[..., -1], slab_colour)


def upsample(flat):
    chans, rows, cols = flat.shape
    wide = jnp.broadcast_to(flat[:, :, None, :, None], (chans, rows, UP, cols, UP))
    return wide.reshape(chans, rows * UP, cols * UP)


def body(populations, solid_mask, jet_mask, visibility):
    dirs, weights = lattice_tables()
    size_first, size_second, size_third = solid_mask.shape
    popul = populations
    for step in range(STEPS):
        post = collide(popul, solid_mask, jet_mask)
        padded = padded_2(post, (("gx", 1), ("gy", 2), ("gz", 3)), 1)
        moved = []
        for index in range(27):
            first = 1 - int(dirs[index, 0])
            second = 1 - int(dirs[index, 1])
            third = 1 - int(dirs[index, 2])
            moved.append(
                padded[
                    index,
                    first : first + size_first,
                    second : second + size_second,
                    third : third + size_third,
                ]
            )
        popul = jnp.stack(moved, axis=0)
    density, comps = moments(popul)
    fluid = 1.0 - solid_mask.astype(jnp.float32)
    flow = jnp.stack([comp * fluid for comp in comps], axis=0)
    rim = padded_2(flow, (("gx", 1), ("gy", 2), ("gz", 3)), 1)

    def derive(comp, axis_id):
        if axis_id == 0:
            return 0.5 * (rim[comp, 2:, 1:-1, 1:-1] - rim[comp, :-2, 1:-1, 1:-1])
        if axis_id == 1:
            return 0.5 * (rim[comp, 1:-1, 2:, 1:-1] - rim[comp, 1:-1, :-2, 1:-1])
        return 0.5 * (rim[comp, 1:-1, 1:-1, 2:] - rim[comp, 1:-1, 1:-1, :-2])

    vort_first = derive(2, 1) - derive(1, 2)
    vort_second = derive(0, 2) - derive(2, 0)
    vort_third = derive(1, 0) - derive(0, 1)
    s_two = vort_first * vort_first + vort_second * vort_second + vort_third * vort_third
    alpha, colour = shade(s_two, flow[0], solid_mask)
    slab_log, slab_colour = slab_pass(alpha, colour)
    depth_count = lax.axis_size("gz")
    stripe = size_second // depth_count
    logs_all = lax.all_gather(slab_log[None], "gz", axis=0, tiled=True)
    position = lax.axis_index("gz")
    own_rank = lax.dynamic_index_in_dim(visibility, position, 0, keepdims=False)
    front_mask = (visibility < own_rank).astype(jnp.float32)
    front = jnp.sum(front_mask[:, None, None] * logs_all, axis=0)
    term = jnp.exp(front)[None] * slab_colour
    rgb = lax.psum_scatter(term, "gz", scatter_dimension=2, tiled=True)
    total = jnp.sum(logs_all, axis=0)
    opacity = 1.0 - jnp.exp(lax.dynamic_slice_in_dim(total, position * stripe, stripe, 1))
    flat = jnp.concatenate([rgb, opacity[None]], axis=0)
    return (popul, upsample(flat))


def solution(mesh):
    return jax.shard_map(
        body,
        mesh=mesh,
        in_specs=(P(None, "gx", "gy", "gz"), P("gx", "gy", "gz"), P("gx", "gy", "gz"), P()),
        out_specs=(P(None, "gx", "gy", "gz"), P(None, "gx", ("gy", "gz"))),
        check_vma=False,
    )
```

profile of v0, /device:TPU:1, one launch (start us, length us, event | category | flops | bytes accessed | tf_op | source)
XLA Modules:
  0.0 206.1 jit_solution(17898201569385696164)
XLA Ops:
  2.9 2.9 %fusion.1 = f32[27,8,8,128]{3,2,1,0:T(8,128)S(1)} fusion(f32[27,8,8,128]{3,2,1,0:T(8,128)} %param.29, f32[8,8,128]{2,1,0:T(8,128)S(1)} %get-tuple-element.124, f32[8,8,128]{2,1,0:T(8,128)S(1)} %get-tuple-element.127, f32[27]{0:T(128)} %constant.73.clone, f32[8,8,128]{2,1,0:T(8,128)S(1)} %get-tuple-element.126, f32[27]{0:T(128)} %constant.72.clone, ...), kind=kLoop, calls=%fused_computation.9 | loop fusion | flops 4202496 | bytes 1950236 | tf_op jit(solution)/shard_map/jit(_where)/select_n | solution.py:68
  5.9 4.0 %collective-permute-start = (f32[27,1,8,128]{3,2,1,0:T(8,128)S(1)}, f32[27,1,8,128]{3,2,1,0:T(8,128)S(1)}, u32[]{:S(2)}, u32[]{:S(2)}) collective-permute-start(f32[27,1,8,128]{3,2,1,0:T(8,128)S(1)} %get-tuple-element.138), channel_id=1, source_target_pairs={{0,128},{128,256},{256,384},{384,512},{512,640},{640,768},{768,896... | collective-permute-start | bytes 331784 | tf_op jit(solution)/shard_map/ppermute | solution.py:24
  9.9 3.8 %collective-permute-start.1 = (f32[27,1,8,128]{3,2,1,0:T(8,128)S(1)}, f32[27,1,8,128]{3,2,1,0:T(8,128)S(1)}, u32[]{:S(2)}, u32[]{:S(2)}) collective-permute-start(f32[27,1,8,128]{3,2,1,0:T(8,128)S(1)} %get-tuple-element.139), channel_id=1, source_target_pairs={{128,0},{256,128},{384,256},{512,384},{640,512},{768,640},{896,768... | collective-permute-start | bytes 331784 | tf_op jit(solution)/shard_map/ppermute | solution.py:27
  15.6 4.0 %collective-permute-start.2 = (f32[27,10,1,128]{3,2,1,0:T(1,128)S(1)}, f32[27,10,1,128]{3,2,1,0:T(1,128)S(1)}, u32[]{:S(2)}, u32[]{:S(2)}) collective-permute-start(f32[27,10,1,128]{3,2,1,0:T(1,128)S(1)} %get-tuple-element.134), channel_id=1, source_target_pairs={{0,8},{8,16},{16,24},{24,32},{32,40},{40,48},{48,56},{56,64},{64,7... | collective-permute-start | bytes 414728 | tf_op jit(solution)/shard_map/ppermute | solution.py:24
  19.6 15.9 %collective-permute-start.3 = (f32[27,10,1,128]{3,2,1,0:T(1,128)S(1)}, f32[27,10,1,128]{3,2,1,0:T(1,128)S(1)}, u32[]{:S(2)}, u32[]{:S(2)}) collective-permute-start(f32[27,10,1,128]{3,2,1,0:T(1,128)S(1)} %get-tuple-element.135), channel_id=1, source_target_pairs={{8,0},{16,8},{24,16},{32,24},{40,32},{48,40},{56,48},{64,56},{72,6... | collective-permute-start | bytes 414728 | tf_op jit(solution)/shard_map/ppermute | solution.py:27
  38.6 2.2 %fusion.39 = (f32[27,10,10,1]{3,2,1,0:T(8,128)S(1)}, f32[27,10,10,1]{3,2,1,0:T(8,128)}) fusion(f32[27,10,10,128]{3,2,1,0:T(8,128)S(1)} %pad_maximum_fusion), kind=kLoop, calls=%fused_computation.258 | loop fusion | bytes 43200 | tf_op jit(solution)/shard_map/slice | solution.py:25
  40.8 2.5 %copy.46 = f32[27,10,10,1]{0,3,2,1:T(1,128)S(1)} copy(f32[27,10,10,1]{3,2,1,0:T(8,128)} %get-tuple-element.131) | data formatting | bytes 21600 | tf_op jit(solution)/shard_map/slice | solution.py:27
  43.3 2.9 %collective-permute-start.4 = (f32[27,10,10,1]{0,3,2,1:T(1,128)S(1)}, f32[27,10,10,1]{0,3,2,1:T(1,128)}, u32[]{:S(2)}, u32[]{:S(2)}) collective-permute-start(f32[27,10,10,1]{0,3,2,1:T(1,128)S(1)} %copy.46), channel_id=1, source_target_pairs={{1,0},{2,1},{3,2},{4,3},{5,4},{6,5},{7,6},{0,7},{9,8},{10,9},{11,1... | collective-permute-start | bytes 32408 | tf_op jit(solution)/shard_map/ppermute | solution.py:27
  46.2 1.6 copy.48
  49.2 2.7 %copy.47 = f32[27,10,10,1]{3,2,1,0:T(8,128)S(1)} copy(f32[27,10,10,1]{0,3,2,1:T(1,128)} %collective-permute-done.4) | data formatting | bytes 21600 | tf_op jit(solution)/shard_map/ppermute | solution.py:27
  54.0 3.9 %copy.49 = f32[27,10,10,1]{3,2,1,0:T(8,128)} copy(f32[27,10,10,1]{0,3,2,1:T(1,128)} %collective-permute-done.5) | data formatting | bytes 21600 | tf_op jit(solution)/shard_map/ppermute | solution.py:24
  79.2 3.2 %collective-permute-start.6 = (f32[27,1,8,128]{3,2,1,0:T(8,128)S(1)}, f32[27,1,8,128]{3,2,1,0:T(8,128)S(1)}, u32[]{:S(2)}, u32[]{:S(2)}) collective-permute-start(f32[27,1,8,128]{3,2,1,0:T(8,128)S(1)} %get-tuple-element.136), channel_id=1, source_target_pairs={{0,128},{128,256},{256,384},{384,512},{512,640},{640,768},{768,896... | collective-permute-start | bytes 331784 | tf_op jit(solution)/shard_map/ppermute | solution.py:24
  82.4 3.5 %collective-permute-start.7 = (f32[27,1,8,128]{3,2,1,0:T(8,128)S(1)}, f32[27,1,8,128]{3,2,1,0:T(8,128)S(1)}, u32[]{:S(2)}, u32[]{:S(2)}) collective-permute-start(f32[27,1,8,128]{3,2,1,0:T(8,128)S(1)} %get-tuple-element.137), channel_id=1, source_target_pairs={{128,0},{256,128},{384,256},{512,384},{640,512},{768,640},{896,768... | collective-permute-start | bytes 331784 | tf_op jit(solution)/shard_map/ppermute | solution.py:27
  86.8 2.8 %collective-permute-done.7 = f32[27,1,8,128]{3,2,1,0:T(8,128)S(1)} collective-permute-done((f32[27,1,8,128]{3,2,1,0:T(8,128)S(1)}, f32[27,1,8,128]{3,2,1,0:T(8,128)S(1)}, u32[]{:S(2)}, u32[]{:S(2)}) %collective-permute-start.7) | collective-permute-done | bytes 110624 | tf_op jit(solution)/shard_map/ppermute | solution.py:27
  89.8 1.9 collective-permute-start.8
  91.8 5.2 %collective-permute-start.9 = (f32[27,10,1,128]{3,2,1,0:T(1,128)S(1)}, f32[27,10,1,128]{3,2,1,0:T(1,128)S(1)}, u32[]{:S(2)}, u32[]{:S(2)}) collective-permute-start(f32[27,10,1,128]{3,2,1,0:T(1,128)S(1)} %get-tuple-element.133), channel_id=1, source_target_pairs={{8,0},{16,8},{24,16},{32,24},{40,32},{48,40},{56,48},{64,56},{72,6... | collective-permute-start | bytes 414728 | tf_op jit(solution)/shard_map/ppermute | solution.py:27
  100.5 2.2 %fusion.38 = (f32[27,10,10,1]{3,2,1,0:T(8,128)S(1)}, f32[27,10,10,1]{3,2,1,0:T(8,128)}) fusion(f32[27,10,10,128]{3,2,1,0:T(8,128)S(1)} %pad_maximum_fusion.1), kind=kLoop, calls=%fused_computation.257 | loop fusion | bytes 43200 | tf_op jit(solution)/shard_map/slice | solution.py:25
  102.7 2.5 %copy.50 = f32[27,10,10,1]{0,3,2,1:T(1,128)S(1)} copy(f32[27,10,10,1]{3,2,1,0:T(8,128)} %get-tuple-element.129) | data formatting | bytes 21600 | tf_op jit(solution)/shard_map/slice | solution.py:27
  106.4 1.6 copy.52
  109.4 2.7 %copy.51 = f32[27,10,10,1]{3,2,1,0:T(8,128)S(1)} copy(f32[27,10,10,1]{0,3,2,1:T(1,128)} %collective-permute-done.10) | data formatting | bytes 21600 | tf_op jit(solution)/shard_map/ppermute | solution.py:27
  114.2 3.9 %copy.53 = f32[27,10,10,1]{3,2,1,0:T(8,128)} copy(f32[27,10,10,1]{0,3,2,1:T(1,128)} %collective-permute-done.11) | data formatting | bytes 21600 | tf_op jit(solution)/shard_map/ppermute | solution.py:24
  138.0 4.8 %collective-permute-start.12 = (f32[3,1,8,128]{3,2,1,0:T(8,128)S(1)}, f32[3,1,8,128]{3,2,1,0:T(8,128)S(1)}, u32[]{:S(2)}, u32[]{:S(2)}) collective-permute-start(f32[3,1,8,128]{3,2,1,0:T(8,128)S(1)} %get-tuple-element.146), channel_id=1, source_target_pairs={{0,128},{128,256},{256,384},{384,512},{512,640},{640,768},{768,896... | collective-permute-start | bytes 36872 | tf_op jit(solution)/shard_map/ppermute | solution.py:24
  142.8 1.9 collective-permute-start.13
  144.7 3.0 %collective-permute-done.13 = f32[3,1,8,128]{3,2,1,0:T(8,128)S(1)} collective-permute-done((f32[3,1,8,128]{3,2,1,0:T(8,128)S(1)}, f32[3,1,8,128]{3,2,1,0:T(8,128)S(1)}, u32[]{:S(2)}, u32[]{:S(2)}) %collective-permute-start.13) | collective-permute-done | bytes 12320 | tf_op jit(solution)/shard_map/ppermute | solution.py:27
  147.7 5.3 %collective-permute-start.14 = (f32[3,10,1,128]{3,2,1,0:T(1,128)S(1)}, f32[3,10,1,128]{3,2,1,0:T(1,128)S(1)}, u32[]{:S(2)}, u32[]{:S(2)}) collective-permute-start(f32[3,10,1,128]{3,2,1,0:T(1,128)S(1)} %get-tuple-element.144), channel_id=1, source_target_pairs={{8,0},{16,8},{24,16},{32,24},{40,32},{48,40},{56,48},{64,56},{72,6... | collective-permute-start | bytes 46088 | tf_op jit(solution)/shard_map/ppermute | solution.py:27
  153.0 1.9 collective-permute-start.15
  155.6 3.1 %collective-permute-done.15 = f32[3,10,1,128]{3,2,1,0:T(1,128)S(1)} collective-permute-done((f32[3,10,1,128]{3,2,1,0:T(1,128)S(1)}, f32[3,10,1,128]{3,2,1,0:T(1,128)S(1)}, u32[]{:S(2)}, u32[]{:S(2)}) %collective-permute-start.15) | collective-permute-done | bytes 15392 | tf_op jit(solution)/shard_map/ppermute | solution.py:24
  158.9 1.7 collective-permute-start.16
  163.7 2.2 %collective-permute-done.16 = f32[3,10,10,1]{3,2,1,0:T(8,128)S(1)} collective-permute-done((f32[3,10,10,1]{3,2,1,0:T(8,128)S(1)}, f32[3,10,10,1]{3,2,1,0:T(8,128)S(1)}, u32[]{:S(2)}, u32[]{:S(2)}) %collective-permute-start.16) | collective-permute-done | bytes 1232 | tf_op jit(solution)/shard_map/ppermute | solution.py:27
  166.4 2.3 %reduce_window_sum.11 = f32[8,8,128]{2,1,0:T(8,128)S(1)} reduce-window(f32[8,8,128]{2,1,0:T(8,128)S(1)} %get-tuple-element.16, f32[]{:T(128)} %constant.29.clone.1), window={size=1x1x128 pad=0_0x0_0x127_0}, to_apply=%region_10.11 | reduce-window | flops 1040384 | bytes 65540 | tf_op jit(solution)/shard_map/jit(cumsum)/reduce_window_sum | solution.py:86
  168.9 14.6 %all-gather = f32[64,8,1]{1,2,0:T(1,128)S(1)} all-gather(f32[8,8,1]{1,2,0:T(1,128)S(1)} %copy.54), channel_id=2, replica_groups=mesh['gx'=8,'gy'=16,'gz'=8] {'gz'}, dimensions={0}, use_global_device_ids=true | all-gather | bytes 2304 | tf_op jit(solution)/shard_map/all_gather | solution.py:139
  184.1 20.5 %all-reduce = f32[3,8,8]{1,0,2:T(4,128)S(1)} all-reduce(f32[3,8,8]{1,0,2:T(4,128)S(1)} %copy.57), channel_id=3, replica_groups=mesh['gx'=8,'gy'=16,'gz'=8] {'gz'}, use_global_device_ids=true, to_apply=%region_13.14.clone | all-reduce | flops 192 | bytes 1536
  (148 shorter events, 67.5 us)
Async XLA Ops:
  5.9 8.1 %collective-permute-start = (f32[27,1,8,128]{3,2,1,0:T(8,128)S(1)}, f32[27,1,8,128]{3,2,1,0:T(8,128)S(1)}, u32[]{:S(2)}, u32[]{:S(2)}) collective-permute-start(f32[27,1,8,128]{3,2,1,0:T(8,128)S(1)} %get-tuple-element.138), channel_id=1, source_target_pairs={{0,128},{128,256},{256,384},{384,512},{512,640},{640,768},{768,896... | collective-permute-start | bytes 331784 | tf_op jit(solution)/shard_map/ppermute | solution.py:24
  9.9 5.6 %collective-permute-start.1 = (f32[27,1,8,128]{3,2,1,0:T(8,128)S(1)}, f32[27,1,8,128]{3,2,1,0:T(8,128)S(1)}, u32[]{:S(2)}, u32[]{:S(2)}) collective-permute-start(f32[27,1,8,128]{3,2,1,0:T(8,128)S(1)} %get-tuple-element.139), channel_id=1, source_target_pairs={{128,0},{256,128},{384,256},{512,384},{640,512},{768,640},{896,768... | collective-permute-start | bytes 331784 | tf_op jit(solution)/shard_map/ppermute | solution.py:27
  15.6 20.4 %collective-permute-start.2 = (f32[27,10,1,128]{3,2,1,0:T(1,128)S(1)}, f32[27,10,1,128]{3,2,1,0:T(1,128)S(1)}, u32[]{:S(2)}, u32[]{:S(2)}) collective-permute-start(f32[27,10,1,128]{3,2,1,0:T(1,128)S(1)} %get-tuple-element.134), channel_id=1, source_target_pairs={{0,8},{8,16},{16,24},{24,32},{32,40},{40,48},{48,56},{56,64},{64,7... | collective-permute-start | bytes 414728 | tf_op jit(solution)/shard_map/ppermute | solution.py:24
  19.6 17.9 %collective-permute-start.3 = (f32[27,10,1,128]{3,2,1,0:T(1,128)S(1)}, f32[27,10,1,128]{3,2,1,0:T(1,128)S(1)}, u32[]{:S(2)}, u32[]{:S(2)}) collective-permute-start(f32[27,10,1,128]{3,2,1,0:T(1,128)S(1)} %get-tuple-element.135), channel_id=1, source_target_pairs={{8,0},{16,8},{24,16},{32,24},{40,32},{48,40},{56,48},{64,56},{72,6... | collective-permute-start | bytes 414728 | tf_op jit(solution)/shard_map/ppermute | solution.py:27
  43.3 5.9 %collective-permute-start.4 = (f32[27,10,10,1]{0,3,2,1:T(1,128)S(1)}, f32[27,10,10,1]{0,3,2,1:T(1,128)}, u32[]{:S(2)}, u32[]{:S(2)}) collective-permute-start(f32[27,10,10,1]{0,3,2,1:T(1,128)S(1)} %copy.46), channel_id=1, source_target_pairs={{1,0},{2,1},{3,2},{4,3},{5,4},{6,5},{7,6},{0,7},{9,8},{10,9},{11,1... | collective-permute-start | bytes 32408 | tf_op jit(solution)/shard_map/ppermute | solution.py:27
  47.8 6.2 %collective-permute-start.5 = (f32[27,10,10,1]{0,3,2,1:T(1,128)}, f32[27,10,10,1]{0,3,2,1:T(1,128)}, u32[]{:S(2)}, u32[]{:S(2)}) collective-permute-start(f32[27,10,10,1]{0,3,2,1:T(1,128)} %copy.48), channel_id=1, source_target_pairs={{0,1},{1,2},{2,3},{3,4},{4,5},{5,6},{6,7},{7,0},{8,9},{9,10},{10,1... | collective-permute-start | bytes 32408 | tf_op jit(solution)/shard_map/ppermute | solution.py:24
  51.9 1.5 copy-start.3
  57.9 1.6 copy-start.4
  59.5 1.6 copy-start
  74.8 1.3 copy-start.10
  74.8 1.3 copy-start.11
  74.8 1.3 copy-start.12
  75.5 2.3 %copy-start.13 = (f32[27]{0:T(128)S(1)}, f32[27]{0:T(128)}, u32[]{:S(2)}) copy-start(f32[27]{0:T(128)} %constant.74.clone) | copy-start | bytes 328
  75.5 2.3 %copy-start.14 = (f32[27]{0:T(128)S(1)}, f32[27]{0:T(128)}, u32[]{:S(2)}) copy-start(f32[27]{0:T(128)} %constant.88) | copy-start | bytes 328
  76.2 1.6 copy-start.8
  79.2 7.6 %collective-permute-start.6 = (f32[27,1,8,128]{3,2,1,0:T(8,128)S(1)}, f32[27,1,8,128]{3,2,1,0:T(8,128)S(1)}, u32[]{:S(2)}, u32[]{:S(2)}) collective-permute-start(f32[27,1,8,128]{3,2,1,0:T(8,128)S(1)} %get-tuple-element.136), channel_id=1, source_target_pairs={{0,128},{128,256},{256,384},{384,512},{512,640},{640,768},{768,896... | collective-permute-start | bytes 331784 | tf_op jit(solution)/shard_map/ppermute | solution.py:24
  82.4 7.2 %collective-permute-start.7 = (f32[27,1,8,128]{3,2,1,0:T(8,128)S(1)}, f32[27,1,8,128]{3,2,1,0:T(8,128)S(1)}, u32[]{:S(2)}, u32[]{:S(2)}) collective-permute-start(f32[27,1,8,128]{3,2,1,0:T(8,128)S(1)} %get-tuple-element.137), channel_id=1, source_target_pairs={{128,0},{256,128},{384,256},{512,384},{640,512},{768,640},{896,768... | collective-permute-start | bytes 331784 | tf_op jit(solution)/shard_map/ppermute | solution.py:27
  89.8 8.7 %collective-permute-start.8 = (f32[27,10,1,128]{3,2,1,0:T(1,128)S(1)}, f32[27,10,1,128]{3,2,1,0:T(1,128)S(1)}, u32[]{:S(2)}, u32[]{:S(2)}) collective-permute-start(f32[27,10,1,128]{3,2,1,0:T(1,128)S(1)} %get-tuple-element.132), channel_id=1, source_target_pairs={{0,8},{8,16},{16,24},{24,32},{32,40},{40,48},{48,56},{56,64},{64,7... | collective-permute-start | bytes 414728 | tf_op jit(solution)/shard_map/ppermute | solution.py:24
  91.8 7.7 %collective-permute-start.9 = (f32[27,10,1,128]{3,2,1,0:T(1,128)S(1)}, f32[27,10,1,128]{3,2,1,0:T(1,128)S(1)}, u32[]{:S(2)}, u32[]{:S(2)}) collective-permute-start(f32[27,10,1,128]{3,2,1,0:T(1,128)S(1)} %get-tuple-element.133), channel_id=1, source_target_pairs={{8,0},{16,8},{24,16},{32,24},{40,32},{48,40},{56,48},{64,56},{72,6... | collective-permute-start | bytes 414728 | tf_op jit(solution)/shard_map/ppermute | solution.py:27
  105.2 4.2 %collective-permute-start.10 = (f32[27,10,10,1]{0,3,2,1:T(1,128)S(1)}, f32[27,10,10,1]{0,3,2,1:T(1,128)}, u32[]{:S(2)}, u32[]{:S(2)}) collective-permute-start(f32[27,10,10,1]{0,3,2,1:T(1,128)S(1)} %copy.50), channel_id=1, source_target_pairs={{1,0},{2,1},{3,2},{4,3},{5,4},{6,5},{7,6},{0,7},{9,8},{10,9},{11,1... | collective-permute-start | bytes 32408 | tf_op jit(solution)/shard_map/ppermute | solution.py:27
  108.0 6.2 %collective-permute-start.11 = (f32[27,10,10,1]{0,3,2,1:T(1,128)}, f32[27,10,10,1]{0,3,2,1:T(1,128)}, u32[]{:S(2)}, u32[]{:S(2)}) collective-permute-start(f32[27,10,10,1]{0,3,2,1:T(1,128)} %copy.52), channel_id=1, source_target_pairs={{0,1},{1,2},{2,3},{3,4},{4,5},{5,6},{6,7},{7,0},{8,9},{9,10},{10,1... | collective-permute-start | bytes 32408 | tf_op jit(solution)/shard_map/ppermute | solution.py:24
  112.1 1.5 copy-start.6
  118.2 1.6 copy-start.7
  119.8 1.6 copy-start.1
  135.7 2.1 %copy-start.9 = (s32[8,8,128]{2,1,0:T(8,128)S(1)}, s32[8,8,128]{2,1,0:T(8,128)}, u32[]{:S(2)}) copy-start(s32[8,8,128]{2,1,0:T(8,128)} %param.30) | copy-start | bytes 98308
  136.4 18.6 %copy-start.15 = (s32[8]{0:T(128)S(1)}, s32[8]{0:T(128)}, u32[]{:S(2)}) copy-start(s32[8]{0:T(128)} %param.32) | copy-start | bytes 100
  138.0 6.7 %collective-permute-start.12 = (f32[3,1,8,128]{3,2,1,0:T(8,128)S(1)}, f32[3,1,8,128]{3,2,1,0:T(8,128)S(1)}, u32[]{:S(2)}, u32[]{:S(2)}) collective-permute-start(f32[3,1,8,128]{3,2,1,0:T(8,128)S(1)} %get-tuple-element.146), channel_id=1, source_target_pairs={{0,128},{128,256},{256,384},{384,512},{512,640},{640,768},{768,896... | collective-permute-start | bytes 36872 | tf_op jit(solution)/shard_map/ppermute | solution.py:24
  142.8 4.9 %collective-permute-start.13 = (f32[3,1,8,128]{3,2,1,0:T(8,128)S(1)}, f32[3,1,8,128]{3,2,1,0:T(8,128)S(1)}, u32[]{:S(2)}, u32[]{:S(2)}) collective-permute-start(f32[3,1,8,128]{3,2,1,0:T(8,128)S(1)} %get-tuple-element.147), channel_id=1, source_target_pairs={{128,0},{256,128},{384,256},{512,384},{640,512},{768,640},{896,768... | collective-permute-start | bytes 36872 | tf_op jit(solution)/shard_map/ppermute | solution.py:27
  147.7 7.9 %collective-permute-start.14 = (f32[3,10,1,128]{3,2,1,0:T(1,128)S(1)}, f32[3,10,1,128]{3,2,1,0:T(1,128)S(1)}, u32[]{:S(2)}, u32[]{:S(2)}) collective-permute-start(f32[3,10,1,128]{3,2,1,0:T(1,128)S(1)} %get-tuple-element.144), channel_id=1, source_target_pairs={{8,0},{16,8},{24,16},{32,24},{40,32},{48,40},{56,48},{64,56},{72,6... | collective-permute-start | bytes 46088 | tf_op jit(solution)/shard_map/ppermute | solution.py:27
  153.0 5.7 %collective-permute-start.15 = (f32[3,10,1,128]{3,2,1,0:T(1,128)S(1)}, f32[3,10,1,128]{3,2,1,0:T(1,128)S(1)}, u32[]{:S(2)}, u32[]{:S(2)}) collective-permute-start(f32[3,10,1,128]{3,2,1,0:T(1,128)S(1)} %get-tuple-element.145), channel_id=1, source_target_pairs={{0,8},{8,16},{16,24},{24,32},{32,40},{40,48},{48,56},{56,64},{64,7... | collective-permute-start | bytes 46088 | tf_op jit(solution)/shard_map/ppermute | solution.py:24
  158.9 7.0 %collective-permute-start.16 = (f32[3,10,10,1]{3,2,1,0:T(8,128)S(1)}, f32[3,10,10,1]{3,2,1,0:T(8,128)S(1)}, u32[]{:S(2)}, u32[]{:S(2)}) collective-permute-start(f32[3,10,10,1]{3,2,1,0:T(8,128)S(1)} %get-tuple-element.140), channel_id=1, source_target_pairs={{1,0},{2,1},{3,2},{4,3},{5,4},{6,5},{7,6},{0,7},{9,8},{10,9},{11,1... | collective-permute-start | bytes 3608 | tf_op jit(solution)/shard_map/ppermute | solution.py:27
  160.7 5.3 %collective-permute-start.17 = (f32[3,10,10,1]{3,2,1,0:T(8,128)S(1)}, f32[3,10,10,1]{3,2,1,0:T(8,128)S(1)}, u32[]{:S(2)}, u32[]{:S(2)}) collective-permute-start(f32[3,10,10,1]{3,2,1,0:T(8,128)S(1)} %get-tuple-element.141), channel_id=1, source_target_pairs={{0,1},{1,2},{2,3},{3,4},{4,5},{5,6},{6,7},{7,0},{8,9},{9,10},{10,1... | collective-permute-start | bytes 3608 | tf_op jit(solution)/shard_map/ppermute | solution.py:24
  (2 other events, 1.3 us)
where the time goes:
time: 209 us; the launch traced here: 206 us
  starting transfers between devices  64.7 us (31%)
  other arithmetic  53.4 us (26%)
  blocking collectives  35.1 us (17%)
  local copies, waits for them, and re-layouts  33 us (16%)
  waiting for transfers between devices  18.7 us (9%)
    ppermute x9, starting transfers between devices, padded_2(): lax.ppermute(lax.slice_in_dim(block, 0, width, axis=dim), axis, backward)  41.5 us
    unnamed x50, other arithmetic  37.3 us
    ppermute x9, starting transfers between devices, padded_2(): lax.ppermute(lax.slice_in_dim(block, block.shape[dim] - width, None, axis...  23.2 us
    unnamed x1, blocking collectives  20.5 us
    all_gather x1, blocking collectives, body(): logs_all = lax.all_gather(slab_log[None], 'gz', axis=0, tiled=True)  14.6 us
    ppermute x9, waiting for transfers between devices, padded_2(): lax.ppermute(lax.slice_in_dim(block, 0, width, axis=dim), axis, backward)  12.4 us
    ppermute x2, local copies, waits for them, and re-layouts, padded_2(): lax.ppermute(lax.slice_in_dim(block, block.shape[dim] - width, None, axis...  7.86 us
    slice x6, local copies, waits for them, and re-layouts, padded_2(): lax.slice_in_dim(block, block.shape[dim] - width, None, axis=dim)  7.66 us
  transfers between devices with their start and end apart: 18, of which 13 were waited for; matrix products, arithmetic and copies ran while one was open for 7% of the time, Pallas kernels for 0%

commit v1 on v0

v1 whole, which is shorter than its diff:
```python
import jax
import jax.numpy as jnp
import numpy as np
from jax import lax
from jax.experimental import pallas as pl
from jax.experimental.pallas import tpu as pltpu
from jax.sharding import PartitionSpec as P

UP = 4
CELLS = 8
LANES = 128
REACH = 3
SPAN = CELLS + 2 * REACH
RING = 16
GROUP = 8

omega_rate = 1.25
jet_speed = 0.12
alpha_top = 0.03
solid_alpha = 0.15
shade_scale = 0.002

DIRS = [(a, b, c) for a in (-1, 0, 1) for b in (-1, 0, 1) for c in (-1, 0, 1)]
WEIGHTS = [(8.0 / 27.0, 2.0 / 27.0, 1.0 / 54.0, 1.0 / 216.0)[abs(a) + abs(b) + abs(c)] for a, b, c in DIRS]
SOLID, JET = 27, 28
MASKS = (SOLID, JET)


def axis_list(axis, inward):
    out = []
    for dist, allowed in ((1, (-1, 0, 1)), (2, (0, inward)), (3, (inward,))):
        out += [(i, dist) for i in range(27) if DIRS[i][axis] in allowed]
    out += [(m, dist) for m in MASKS for dist in (1, 2)]
    return out


def held(key, x):
    dist, inward = (-x, 1) if x < 0 else (x - CELLS + 1, -1)
    if dist <= 0:
        return True
    return (key, dist) in axis_list(0, inward)


def corner_list(inward):
    out = []
    for key, dist in axis_list(1, inward):
        for x in (-3, -2, -1, 8, 9, 10):
            if held(key, x) and not (dist == 3 and x in (-3, 10)):
                out.append((key, dist, x))
    return out


X_COUNT = len(axis_list(0, 1))
Y_OWN = len(axis_list(1, 1)) * CELLS
Y_COUNT = Y_OWN + -(-len(corner_list(1)) // 8) * 8


def moments(f):
    third = None
    parts = []
    for a in range(3):
        row = []
        for b in range(3):
            lo, mid, hi = f[9 * a + 3 * b], f[9 * a + 3 * b + 1], f[9 * a + 3 * b + 2]
            row.append((lo + hi) + mid)
            diff = hi - lo
            third = diff if third is None else third + diff
        parts.append(row)
    sums = [(row[0] + row[2]) + row[1] for row in parts]
    second = (parts[0][2] - parts[0][0]) + (parts[1][2] - parts[1][0]) + (parts[2][2] - parts[2][0])
    return (sums[0] + sums[2]) + sums[1], sums[2] - sums[0], second, third


def collide(f, solid, jet):
    density, first, second, third = moments(f)
    scale = 1.0 / density
    ux = jnp.where(jet, jet_speed, first * scale)
    uy = jnp.where(jet, 0.0, second * scale)
    uz = jnp.where(jet, 0.0, third * scale)
    gain = jnp.where(jet, 1.0, omega_rate) * density
    keep = jnp.where(jet, 0.0, 1.0 - omega_rate)
    base = 1.0 - 1.5 * (ux * ux + uy * uy + uz * uz)
    strength = {w: gain * w for w in set(WEIGHTS)}
    post = [None] * 27
    comps = (ux, uy, uz)
    for i in range(14):
        w = strength[WEIGHTS[i]]
        if i == 13:
            post[i] = jnp.where(solid, f[i], w * base + keep * f[i])
            continue
        along = None
        for c, u in zip(DIRS[i], comps):
            if c == 0:
                continue
            if along is None:
                along = u if c > 0 else -u
            else:
                along = along + u if c > 0 else along - u
        even = w * (base + 4.5 * (along * along))
        odd = w * (3.0 * along)
        j = 26 - i
        post[i] = jnp.where(solid, f[j], (even + odd) + keep * f[i])
        post[j] = jnp.where(solid, f[i], (even - odd) + keep * f[j])
    return post


def lanes_of(rows):
    return lax.broadcasted_iota(jnp.int32, (rows, LANES), 1)


def turn(value, shift, axis):
    size = value.shape[axis]
    if isinstance(shift, int):
        shift = shift % size
        if shift == 0:
            return value
    return pltpu.roll(value, shift, axis)


def first_kernel(f_ref, solid_ref, jet_ref, p_ref, lo_ref, hi_ref):
    def plane(x, carry):
        start = pl.multiple_of(x * CELLS, CELLS)
        rows = pl.ds(start, CELLS)
        f = [f_ref[i, rows, :] for i in range(27)]
        post = collide(f, solid_ref[rows, :] == 1, jet_ref[rows, :] == 1)
        for i in range(27):
            p_ref[i, rows, :] = post[i]
        return carry

    lax.fori_loop(0, CELLS, plane, 0)

    def plane_of(key, x):
        rows = pl.ds(x * CELLS, CELLS)
        if key == SOLID:
            return solid_ref[rows, :].astype(jnp.float32)
        if key == JET:
            return jet_ref[rows, :].astype(jnp.float32)
        return p_ref[key, rows, :]

    for k, (key, dist) in enumerate(axis_list(0, -1)):
        lo_ref[k] = plane_of(key, dist - 1)
    for k, (key, dist) in enumerate(axis_list(0, 1)):
        hi_ref[k] = plane_of(key, CELLS - dist)


def second_kernel(p_ref, solid_ref, jet_ref, xlo_ref, xhi_ref, lo_ref, hi_ref):
    low_at = {entry: k for k, entry in enumerate(axis_list(0, 1))}
    high_at = {entry: k for k, entry in enumerate(axis_list(0, -1))}

    def own_rows(key, row):
        rows = pl.ds(row, CELLS, stride=CELLS)
        if key == SOLID:
            return solid_ref[rows, :].astype(jnp.float32)
        if key == JET:
            return jet_ref[rows, :].astype(jnp.float32)
        return p_ref[key, rows, :]

    for inward, out_ref in ((-1, lo_ref), (1, hi_ref)):
        for k, (key, dist) in enumerate(axis_list(1, inward)):
            row = dist - 1 if inward < 0 else CELLS - dist
            out_ref[pl.ds(k * CELLS, CELLS), :] = own_rows(key, row)
        for k, (key, dist, x) in enumerate(corner_list(inward)):
            row = dist - 1 if inward < 0 else CELLS - dist
            if x < 0:
                value = xlo_ref[low_at[(key, -x)], pl.ds(row, 1), :]
            else:
                value = xhi_ref[high_at[(key, x - CELLS + 1)], pl.ds(row, 1), :]
            out_ref[pl.ds(Y_OWN + k, 1), :] = value


def third_kernel(p_ref, solid_ref, jet_ref, xlo_ref, xhi_ref, ylo_ref, yhi_ref, e_ref, z_ref):
    for x in range(CELLS):
        rows = pl.ds((x + REACH) * RING, CELLS)
        for i in range(27):
            e_ref[i, rows, :] = p_ref[i, pl.ds(x * CELLS, CELLS), :]
        e_ref[SOLID, rows, :] = solid_ref[pl.ds(x * CELLS, CELLS), :].astype(jnp.float32)
        e_ref[JET, rows, :] = jet_ref[pl.ds(x * CELLS, CELLS), :].astype(jnp.float32)
    for k, (key, dist) in enumerate(axis_list(0, 1)):
        e_ref[key, pl.ds((REACH - dist) * RING, CELLS), :] = xlo_ref[k]
    for k, (key, dist) in enumerate(axis_list(0, -1)):
        e_ref[key, pl.ds((REACH + CELLS - 1 + dist) * RING, CELLS), :] = xhi_ref[k]
    for inward, in_ref in ((1, ylo_ref), (-1, yhi_ref)):
        for k, (key, dist) in enumerate(axis_list(1, inward)):
            ring = RING - dist if inward > 0 else CELLS - 1 + dist
            e_ref[key, pl.ds(REACH * RING + ring, CELLS, stride=RING), :] = in_ref[pl.ds(k * CELLS, CELLS), :]
        for k, (key, dist, x) in enumerate(corner_list(inward)):
            ring = RING - dist if inward > 0 else CELLS - 1 + dist
            e_ref[key, pl.ds((x + REACH) * RING + ring, 1), :] = in_ref[pl.ds(Y_OWN + k, 1), :]
    group = lanes_of(RING) // GROUP

    def pack(key, carry):
        acc = jnp.zeros((RING, LANES), jnp.float32)
        for plane in range(SPAN):
            value = turn(e_ref[key, pl.ds(plane * RING, RING), :], GROUP * plane + 3, 1)
            acc = jnp.where(group == plane, value, acc)
        z_ref[key] = acc
        return carry

    lax.fori_loop(0, 29, pack, 0)


def fourth_kernel(e_ref, z_ref, zlo_ref, zhi_ref, adv_ref, out_ref, g_ref, ge_ref, h_ref, flow_ref):
    lane = lanes_of(RING)
    slot = lane % GROUP

    def edges(key, own):
        mixed = jnp.where(slot < 3, zlo_ref[key], own)
        return jnp.where(slot >= 5, turn(zhi_ref[key], 2, 1), mixed)

    for i in range(27):
        own = z_ref[i]
        if DIRS[i][2] == 1:
            own = turn(own, 2, 1)
        ge_ref[i] = edges(i, own)
    nothing = jnp.zeros((RING, LANES), jnp.float32)
    edge_solid = edges(SOLID, nothing)
    edge_jet = edges(JET, nothing)

    def stream_edges():
        out = []
        for i, (a, b, c) in enumerate(DIRS):
            out.append(turn(turn(ge_ref[i], b, 0), GROUP * a + c, 1))
        return out

    def stream(load, plane):
        out = []
        for i, (a, b, c) in enumerate(DIRS):
            source = plane - a
            value = load(i, source)
            if c == 1:
                value = jnp.where(lane == LANES - 1, turn(ge_ref[i], LANES - 1 - 2 - GROUP * source, 1), value)
            elif c == -1:
                value = jnp.where(lane == 0, turn(ge_ref[i], LANES - 5 - GROUP * source, 1), value)
            out.append(turn(turn(value, b, 0), c, 1))
        return out

    def rows_of(plane):
        return pl.ds(pl.multiple_of(plane * RING, RING), RING)

    def from_block(i, plane):
        return e_ref[i, rows_of(plane), :]

    def from_step(i, plane):
        return g_ref[i, rows_of(plane), :]

    edge_post = collide(stream_edges(), edge_solid > 0.5, edge_jet > 0.5)
    for i in range(27):
        h_ref[i] = edge_post[i]

    def step_one(plane, carry):
        f = stream(from_block, plane)
        post = collide(f, e_ref[SOLID, rows_of(plane), :] > 0.5, e_ref[JET, rows_of(plane), :] > 0.5)
        for i in range(27):
            g_ref[i, rows_of(plane), :] = post[i]
            c = DIRS[i][2]
            if c == -1:
                h_ref[i] = jnp.where(lane == GROUP * plane + 3, turn(post[i], GROUP * plane + 3, 1), h_ref[i])
            elif c == 1:
                h_ref[i] = jnp.where(lane == GROUP * plane + 4, turn(post[i], GROUP * plane + 5, 1), h_ref[i])
        return carry

    lax.fori_loop(1, SPAN - 1, step_one, 0)
    for i in range(27):
        ge_ref[i] = h_ref[i]

    def velocity(f, solid):
        density, first, second, third = moments(f)
        scale = (1.0 - solid) / density
        return first * scale, second * scale, third * scale

    edge_flow = velocity(stream_edges(), edge_solid)

    def step_two(plane, keep):
        f = stream(from_step, plane)
        if keep:
            for i in range(27):
                adv_ref[i, plane - REACH] = f[i][:CELLS]
        for c, value in enumerate(velocity(f, e_ref[SOLID, rows_of(plane), :])):
            flow_ref[c, rows_of(plane), :] = value

    step_two(REACH - 1, False)
    step_two(REACH + CELLS, False)

    def step_two_own(plane, carry):
        step_two(plane, True)
        return carry

    lax.fori_loop(REACH, REACH + CELLS, step_two_own, 0)

    short = lanes_of(CELLS)

    def render(x, acc):
        plane = x + REACH
        flow = [flow_ref[c, rows_of(plane), :] for c in range(3)]
        ahead = [flow_ref[c, rows_of(plane + 1), :][:CELLS] for c in range(3)]
        behind = [flow_ref[c, rows_of(plane - 1), :][:CELLS] for c in range(3)]

        def along_first(c):
            return 0.5 * (ahead[c] - behind[c])

        def along_second(c):
            return 0.5 * (turn(flow[c], -1, 0) - turn(flow[c], 1, 0))[:CELLS]

        def along_third(c):
            here = flow[c][:CELLS]
            edge = edge_flow[c][:CELLS]
            low = jnp.where(short == 0, turn(edge, LANES - 2 - GROUP * plane, 1), turn(here, 1, 1))
            high = jnp.where(
                short == LANES - 1, turn(edge, LANES - 1 - 5 - GROUP * plane, 1), turn(here, -1, 1)
            )
            return 0.5 * (high - low)

        vort_first = along_second(2) - along_third(1)
        vort_second = along_third(0) - along_first(2)
        vort_third = along_first(1) - along_second(0)
        s_two = vort_first * vort_first + vort_second * vort_second + vort_third * vort_third
        solid_on = e_ref[SOLID, pl.ds(pl.multiple_of(plane * RING, RING), CELLS), :] > 0.5
        ratio = s_two / (s_two + shade_scale)
        alpha = jnp.where(solid_on, solid_alpha, alpha_top * (1.0 - jnp.exp(-s_two / shade_scale)))
        red = jnp.where(solid_on, 0.6, 0.3 + 1.5 * ratio)
        green = jnp.where(solid_on, 0.6, 1.2 - 0.9 * ratio)
        blue = jnp.where(solid_on, 0.6, 0.8 + 0.4 * jnp.tanh(20.0 * flow[0][:CELLS]))
        logs = jnp.log1p(-alpha)
        running = logs
        for step in (1, 2, 4, 8, 16, 32, 64):
            running = running + jnp.where(short >= step, turn(running, step, 1), 0.0)
        weight = alpha * jnp.exp(running - logs)
        for ch, value in enumerate((red * weight, green * weight, blue * weight, logs)):
            total = jnp.sum(value, axis=1, keepdims=True)
            acc = jnp.where(short // UP == ch * CELLS + x, total, acc)
        return acc

    out_ref[...] = lax.fori_loop(0, CELLS, render, jnp.zeros((CELLS, LANES), jnp.float32))


def last_kernel(slab_ref, rank_ref, out_ref):
    slabs = slab_ref[...]
    rank = rank_ref[...]
    channel = lanes_of(CELLS) // (CELLS * UP)
    logs = slabs
    for ch in range(3):
        logs = jnp.where(channel == ch, turn(slabs, (ch + 1) * CELLS * UP, 1), logs)
    front = jnp.zeros_like(slabs)
    for s in range(CELLS):
        front = front + jnp.where(rank[s : s + 1] < rank, logs[s : s + 1], 0.0)
    colour = jnp.sum(jnp.exp(front) * slabs, axis=0, keepdims=True)
    opacity = 1.0 - jnp.exp(jnp.sum(logs, axis=0, keepdims=True))
    row = jnp.where(channel[:1] == 3, opacity, colour)
    for ch in range(4):
        out_ref[ch] = jnp.broadcast_to(turn(row, -ch * CELLS * UP, 1)[:, : CELLS * UP], (UP, CELLS * UP))


def call(kernel, outs, scratch=()):
    shapes = tuple(jax.ShapeDtypeStruct(shape, jnp.float32) for shape in outs)
    return pl.pallas_call(
        kernel,
        out_shape=shapes,
        scratch_shapes=[pltpu.VMEM(shape, jnp.float32) for shape in scratch],
        compiler_params=pltpu.CompilerParams(vmem_limit_bytes=24 * 1024 * 1024),
    )


def both_ways(lo, hi, axis):
    count = lax.axis_size(axis)
    forward = [(i, (i + 1) % count) for i in range(count)]
    backward = [(target, source) for source, target in forward]
    return lax.ppermute(hi, axis, forward), lax.ppermute(lo, axis, backward)


def body(populations, solid_mask, jet_mask, visibility):
    cells = CELLS * CELLS
    f = populations.reshape(27, cells, LANES)
    solid = solid_mask.reshape(cells, LANES)
    jet = jet_mask.reshape(cells, LANES)
    x_shape = (X_COUNT, CELLS, LANES)
    post, lo, hi = call(first_kernel, ((27, cells, LANES), x_shape, x_shape))(f, solid, jet)
    xlo, xhi = both_ways(lo, hi, "gx")
    y_shape = (Y_COUNT, LANES)
    lo, hi = call(second_kernel, (y_shape, y_shape))(post, solid, jet, xlo, xhi)
    ylo, yhi = both_ways(lo, hi, "gy")
    block, face = call(third_kernel, ((29, SPAN * RING, LANES), (29, RING, LANES)))(
        post, solid, jet, xlo, xhi, ylo, yhi
    )
    zlo, zhi = both_ways(face, face, "gz")
    advanced, slabs = call(
        fourth_kernel,
        ((27, CELLS, CELLS, LANES), (CELLS, LANES)),
        (
            (27, SPAN * RING, LANES),
            (27, RING, LANES),
            (27, RING, LANES),
            (3, SPAN * RING, LANES),
        ),
    )(block, face, zlo, zhi)
    slabs = lax.all_to_all(slabs, "gz", 0, 0, tiled=True)
    rank = jnp.broadcast_to(visibility[:, None], (CELLS, LANES))
    (image,) = call(last_kernel, ((4, UP, CELLS * UP),))(slabs, rank)
    return advanced, jnp.swapaxes(image, 1, 2)


def solution(mesh):
    return jax.shard_map(
        body,
        mesh=mesh,
        in_specs=(P(None, "gx", "gy", "gz"), P("gx", "gy", "gz"), P("gx", "gy", "gz"), P()),
        out_specs=(P(None, "gx", "gy", "gz"), P(None, "gx", ("gy", "gz"))),
        check_vma=False,
    )
```

time: 209 us -> 80.7 us (0.39)
  the two profiles are of different devices: /device:TPU:1 before, /device:TPU:24 now
where the time goes in v1:
time: 80.7 us; the launch traced here: 80.2 us
  starting transfers between devices  29.7 us (37%)
  waiting for transfers between devices  18.6 us (23%)
  Pallas kernels  17.6 us (22%)
  blocking collectives  9.28 us (11%)
  local copies, waits for them, and re-layouts  4.27 us (5%)
    ppermute x6, starting transfers between devices, both_ways(): return (lax.ppermute(hi, axis, forward), lax.ppermute(lo, axis, backward))  29.7 us
    ppermute x6, waiting for transfers between devices, both_ways(): return (lax.ppermute(hi, axis, forward), lax.ppermute(lo, axis, backward))  18.6 us
    pallas_call x1, Pallas kernels, body(): call(fourth_kernel, ((27, CELLS, CELLS, LANES), (CELLS, LANES)), ((27, SP...  12.7 us
    all_to_all x1, blocking collectives, body(): slabs = lax.all_to_all(slabs, 'gz', 0, 0, tiled=True)  9.28 us
    unnamed x12, local copies, waits for them, and re-layouts  4.2 us
    pallas_call x1, Pallas kernels, body(): call(third_kernel, ((29, SPAN * RING, LANES), (29, RING, LANES)))  3.38 us
  transfers between devices with their start and end apart: 6, of which 5 were waited for; matrix products, arithmetic and copies ran while one was open for 0% of the time, Pallas kernels for 0%

profile of v1, /device:TPU:24, one launch (start us, length us, event | category | flops | bytes accessed | tf_op | source)
XLA Modules:
  0.0 80.2 jit_solution(5386675993350949330)
XLA Ops:
  0.6 0.0 copy-start
  0.6 1.2 %copy-done = f32[27,8,8,128]{3,2,1,0:T(8,128)S(1)} copy-done((f32[27,8,8,128]{3,2,1,0:T(8,128)S(1)}, f32[27,8,8,128]{3,2,1,0:T(8,128)}, u32[]{:S(2)}) %copy-start) | copy-done | bytes 884760
  1.8 0.0 copy-start.1
  1.8 0.8 copy-done.1
  2.6 0.0 copy-start.3
  2.6 0.8 copy-done.3
  3.3 0.5 shard_map.59
  3.8 4.7 %collective-permute-start = (f32[58,8,128]{2,1,0:T(8,128)S(1)}, f32[58,8,128]{2,1,0:T(8,128)S(1)}, u32[]{:S(2)}, u32[]{:S(2)}) collective-permute-start(f32[58,8,128]{2,1,0:T(8,128)S(1)} %get-tuple-element.12), channel_id=1, source_target_pairs={{0,128},{128,256},{256,384},{384,512},{512,640},{640,768},{768,896... | collective-permute-start | bytes 712712 | tf_op jit(solution)/shard_map/ppermute | solution.py:367
  8.5 1.9 %collective-permute-start.1 = (f32[58,8,128]{2,1,0:T(8,128)S(1)}, f32[58,8,128]{2,1,0:T(8,128)S(1)}, u32[]{:S(2)}, u32[]{:S(2)}) collective-permute-start(f32[58,8,128]{2,1,0:T(8,128)S(1)} %get-tuple-element.13), channel_id=1, source_target_pairs={{128,0},{256,128},{384,256},{512,384},{640,512},{768,640},{896,768... | collective-permute-start | bytes 712712 | tf_op jit(solution)/shard_map/ppermute | solution.py:367
  10.5 3.1 %collective-permute-done.xlo_ref = f32[58,8,128]{2,1,0:T(8,128)S(1)} collective-permute-done((f32[58,8,128]{2,1,0:T(8,128)S(1)}, f32[58,8,128]{2,1,0:T(8,128)S(1)}, u32[]{:S(2)}, u32[]{:S(2)}) %collective-permute-start) | collective-permute-done | bytes 237600 | tf_op jit(solution)/shard_map/ppermute | solution.py:367
  13.5 5.3 %collective-permute-done.1.xhi_ref = f32[58,8,128]{2,1,0:T(8,128)S(1)} collective-permute-done((f32[58,8,128]{2,1,0:T(8,128)S(1)}, f32[58,8,128]{2,1,0:T(8,128)S(1)}, u32[]{:S(2)}, u32[]{:S(2)}) %collective-permute-start.1) | collective-permute-done | bytes 237600 | tf_op jit(solution)/shard_map/ppermute | solution.py:367
  18.9 0.3 shard_map.60
  19.1 0.0 copy-start.5
  19.1 4.3 %collective-permute-start.2 = (f32[696,128]{1,0:T(8,128)S(1)}, f32[696,128]{1,0:T(8,128)S(1)}, u32[]{:S(2)}, u32[]{:S(2)}) collective-permute-start(f32[696,128]{1,0:T(8,128)S(1)} %get-tuple-element.14), channel_id=1, source_target_pairs={{0,8},{8,16},{16,24},{24,32},{32,40},{40,48},{48,56},{56,64},{64,7... | collective-permute-start | bytes 1069064 | tf_op jit(solution)/shard_map/ppermute | solution.py:367
  23.4 15.9 %collective-permute-start.3 = (f32[696,128]{1,0:T(8,128)S(1)}, f32[696,128]{1,0:T(8,128)S(1)}, u32[]{:S(2)}, u32[]{:S(2)}) collective-permute-start(f32[696,128]{1,0:T(8,128)S(1)} %get-tuple-element.15), channel_id=1, source_target_pairs={{8,0},{16,8},{24,16},{32,24},{40,32},{48,40},{56,48},{64,56},{72,6... | collective-permute-start | bytes 1069064 | tf_op jit(solution)/shard_map/ppermute | solution.py:367
  39.3 5.2 %collective-permute-done.2.ylo_ref = f32[696,128]{1,0:T(8,128)S(1)} collective-permute-done((f32[696,128]{1,0:T(8,128)S(1)}, f32[696,128]{1,0:T(8,128)S(1)}, u32[]{:S(2)}, u32[]{:S(2)}) %collective-permute-start.2) | collective-permute-done | bytes 356384 | tf_op jit(solution)/shard_map/ppermute | solution.py:367
  44.5 1.2 %collective-permute-done.3.yhi_ref = f32[696,128]{1,0:T(8,128)S(1)} collective-permute-done((f32[696,128]{1,0:T(8,128)S(1)}, f32[696,128]{1,0:T(8,128)S(1)}, u32[]{:S(2)}, u32[]{:S(2)}) %collective-permute-start.3) | collective-permute-done | bytes 356384 | tf_op jit(solution)/shard_map/ppermute | solution.py:367
  45.7 0.0 copy-start.2
  45.7 0.8 copy-done.2
  46.4 0.0 copy-start.4
  46.4 0.8 copy-done.4
  47.2 3.4 %shard_map.61 = (f32[29,224,128]{2,1,0:T(8,128)S(1)}, f32[29,16,128]{2,1,0:T(8,128)S(1)}) custom-call(f32[27,64,128]{2,1,0:T(8,128)S(1)} %get-tuple-element.11.p_ref, s32[64,128]{1,0:T(8,128)S(1)} %bitcast.11, s32[64,128]{1,0:T(8,128)S(1)} %bitcast.14, f32[58,8,128]{2,1,0:T(8,128)S(1)} %collective-permute-done.xlo_ref, ...), custom_call_target="tpu_custom_call" | custom-call | tf_op jit(solution)/shard_map/pallas_call | solution.py:381
  50.6 0.0 collective-permute-start.4
  50.6 2.9 %collective-permute-start.5 = (f32[29,16,128]{2,1,0:T(8,128)S(1)}, f32[29,16,128]{2,1,0:T(8,128)S(1)}, u32[]{:S(2)}, u32[]{:S(2)}) collective-permute-start(f32[29,16,128]{2,1,0:T(8,128)S(1)} %get-tuple-element.17.z_ref), channel_id=1, source_target_pairs={{1,0},{2,1},{3,2},{4,3},{5,4},{6,5},{7,6},{0,7},{9,8},{10,9},{11,1... | collective-permute-start | bytes 712712 | tf_op jit(solution)/shard_map/ppermute | solution.py:367
  53.6 3.8 %collective-permute-done.4.zlo_ref = f32[29,16,128]{2,1,0:T(8,128)S(1)} collective-permute-done((f32[29,16,128]{2,1,0:T(8,128)S(1)}, f32[29,16,128]{2,1,0:T(8,128)S(1)}, u32[]{:S(2)}, u32[]{:S(2)}) %collective-permute-start.4) | collective-permute-done | bytes 237600 | tf_op jit(solution)/shard_map/ppermute | solution.py:367
  57.3 0.0 collective-permute-done.5.zhi_ref
  57.3 12.7 %shard_map.62 = (f32[27,8,8,128]{3,2,1,0:T(8,128)}, f32[8,128]{1,0:T(8,128)S(1)}) custom-call(f32[29,224,128]{2,1,0:T(8,128)S(1)} %get-tuple-element.16.e_ref, f32[29,16,128]{2,1,0:T(8,128)S(1)} %get-tuple-element.17.z_ref, f32[29,16,128]{2,1,0:T(8,128)S(1)} %collective-permute-done.4.zlo_ref, f32[29,16,128]{2,1,0:T(8,128)S(1)} %collective-permute-done.5.zhi_ref), custom_call_target="tpu_custom_call" | custom-call | tf_op jit(solution)/shard_map/pallas_call | solution.py:385
  70.0 9.3 %all_to_all.11 = f32[8,1,128]{2,1,0:T(1,128)S(1)} all-to-all(f32[8,1,128]{2,1,0:T(1,128)S(1)} %bitcast.16), channel_id=1, replica_groups=mesh['gx'=8,'gy'=16,'gz'=8] {'gz'}, dimensions={0} | all-to-all | bytes 8192 | tf_op jit(solution)/shard_map/all_to_all | solution.py:395
  79.3 0.0 copy-done.5
  79.3 0.1 broadcast_in_dim.2.rank_ref
  79.4 0.8 shard_map.63
Async XLA Ops:
  0.6 1.2 %copy-start = (f32[27,8,8,128]{3,2,1,0:T(8,128)S(1)}, f32[27,8,8,128]{3,2,1,0:T(8,128)}, u32[]{:S(2)}) copy-start(f32[27,8,8,128]{3,2,1,0:T(8,128)} %param.4) | copy-start | bytes 2654212
  1.8 0.8 copy-start.1
  2.6 0.8 copy-start.3
  3.8 9.7 %collective-permute-start = (f32[58,8,128]{2,1,0:T(8,128)S(1)}, f32[58,8,128]{2,1,0:T(8,128)S(1)}, u32[]{:S(2)}, u32[]{:S(2)}) collective-permute-start(f32[58,8,128]{2,1,0:T(8,128)S(1)} %get-tuple-element.12), channel_id=1, source_target_pairs={{0,128},{128,256},{256,384},{384,512},{512,640},{640,768},{768,896... | collective-permute-start | bytes 712712 | tf_op jit(solution)/shard_map/ppermute | solution.py:367
  8.5 10.3 %collective-permute-start.1 = (f32[58,8,128]{2,1,0:T(8,128)S(1)}, f32[58,8,128]{2,1,0:T(8,128)S(1)}, u32[]{:S(2)}, u32[]{:S(2)}) collective-permute-start(f32[58,8,128]{2,1,0:T(8,128)S(1)} %get-tuple-element.13), channel_id=1, source_target_pairs={{128,0},{256,128},{384,256},{512,384},{640,512},{768,640},{896,768... | collective-permute-start | bytes 712712 | tf_op jit(solution)/shard_map/ppermute | solution.py:367
  19.1 60.2 %copy-start.5 = (s32[8]{0:T(128)S(1)}, s32[8]{0:T(128)}, u32[]{:S(2)}) copy-start(s32[8]{0:T(128)} %param.7) | copy-start | bytes 100
  19.1 25.4 %collective-permute-start.2 = (f32[696,128]{1,0:T(8,128)S(1)}, f32[696,128]{1,0:T(8,128)S(1)}, u32[]{:S(2)}, u32[]{:S(2)}) collective-permute-start(f32[696,128]{1,0:T(8,128)S(1)} %get-tuple-element.14), channel_id=1, source_target_pairs={{0,8},{8,16},{16,24},{24,32},{32,40},{40,48},{48,56},{56,64},{64,7... | collective-permute-start | bytes 1069064 | tf_op jit(solution)/shard_map/ppermute | solution.py:367
  23.4 22.2 %collective-permute-start.3 = (f32[696,128]{1,0:T(8,128)S(1)}, f32[696,128]{1,0:T(8,128)S(1)}, u32[]{:S(2)}, u32[]{:S(2)}) collective-permute-start(f32[696,128]{1,0:T(8,128)S(1)} %get-tuple-element.15), channel_id=1, source_target_pairs={{8,0},{16,8},{24,16},{32,24},{40,32},{48,40},{56,48},{64,56},{72,6... | collective-permute-start | bytes 1069064 | tf_op jit(solution)/shard_map/ppermute | solution.py:367
  45.7 0.8 copy-start.2
  46.4 0.8 copy-start.4
  50.6 6.8 %collective-permute-start.4 = (f32[29,16,128]{2,1,0:T(8,128)S(1)}, f32[29,16,128]{2,1,0:T(8,128)S(1)}, u32[]{:S(2)}, u32[]{:S(2)}) collective-permute-start(f32[29,16,128]{2,1,0:T(8,128)S(1)} %get-tuple-element.17.z_ref), channel_id=1, source_target_pairs={{0,1},{1,2},{2,3},{3,4},{4,5},{5,6},{6,7},{7,0},{8,9},{9,10},{10,1... | collective-permute-start | bytes 712712 | tf_op jit(solution)/shard_map/ppermute | solution.py:367
  50.6 6.7 %collective-permute-start.5 = (f32[29,16,128]{2,1,0:T(8,128)S(1)}, f32[29,16,128]{2,1,0:T(8,128)S(1)}, u32[]{:S(2)}, u32[]{:S(2)}) collective-permute-start(f32[29,16,128]{2,1,0:T(8,128)S(1)} %get-tuple-element.17.z_ref), channel_id=1, source_target_pairs={{1,0},{2,1},{3,2},{4,3},{5,4},{6,5},{7,6},{0,7},{9,8},{10,9},{11,1... | collective-permute-start | bytes 712712 | tf_op jit(solution)/shard_map/ppermute | solution.py:367

commit v2 on v1

v2 whole, which is shorter than its diff:
```python
import jax
import jax.numpy as jnp
import numpy as np
from jax import lax
from jax.experimental import pallas as pl
from jax.experimental.pallas import tpu as pltpu
from jax.sharding import PartitionSpec as P

UP = 4
CELLS = 8
LANES = 128
REACH = 3
SPAN = CELLS + 2 * REACH
LAST = SPAN - 1
ROWS = 16
HALF = 15
GROUP = 8

omega_rate = 1.25
jet_speed = 0.12
alpha_top = 0.03
solid_alpha = 0.15
shade_scale = 0.002

DIRS = [(a, b, c) for a in (-1, 0, 1) for b in (-1, 0, 1) for c in (-1, 0, 1)]
WEIGHTS = [(8.0 / 27.0, 2.0 / 27.0, 1.0 / 54.0, 1.0 / 216.0)[abs(a) + abs(b) + abs(c)] for a, b, c in DIRS]
SOLID, JET = 27, 28
MASKS = (SOLID, JET)


def axis_list(axis, inward):
    out = []
    for dist, allowed in ((1, (-1, 0, 1)), (2, (0, inward)), (3, (inward,))):
        out += [(i, dist) for i in range(27) if DIRS[i][axis] in allowed]
    out += [(m, dist) for m in MASKS for dist in (1, 2)]
    return out


def held(key, x):
    dist, inward = (-x, 1) if x < 0 else (x - CELLS + 1, -1)
    if dist <= 0:
        return True
    return (key, dist) in axis_list(0, inward)


def corner_list(inward):
    out = []
    for key, dist in axis_list(1, inward):
        for x in (-3, -2, -1, 8, 9, 10):
            if held(key, x) and not (dist == 3 and x in (-3, 10)):
                out.append((key, dist, x))
    return out


X_COUNT = len(axis_list(0, 1))
Y_OWN = len(axis_list(1, 1)) * CELLS
Y_COUNT = Y_OWN + -(-len(corner_list(1)) // 8) * 8


def moments(f):
    third = None
    parts = []
    for a in range(3):
        row = []
        for b in range(3):
            lo, mid, hi = f[9 * a + 3 * b], f[9 * a + 3 * b + 1], f[9 * a + 3 * b + 2]
            row.append((lo + hi) + mid)
            diff = hi - lo
            third = diff if third is None else third + diff
        parts.append(row)
    sums = [(row[0] + row[2]) + row[1] for row in parts]
    second = (parts[0][2] - parts[0][0]) + (parts[1][2] - parts[1][0]) + (parts[2][2] - parts[2][0])
    return (sums[0] + sums[2]) + sums[1], sums[2] - sums[0], second, third


def collide(f, solid, jet):
    density, first, second, third = moments(f)
    scale = 1.0 / density
    ux = jnp.where(jet, jet_speed, first * scale)
    uy = jnp.where(jet, 0.0, second * scale)
    uz = jnp.where(jet, 0.0, third * scale)
    gain = jnp.where(jet, 1.0, omega_rate) * density
    keep = jnp.where(jet, 0.0, 1.0 - omega_rate)
    base = 1.0 - 1.5 * (ux * ux + uy * uy + uz * uz)
    strength = {w: gain * w for w in set(WEIGHTS)}
    post = [None] * 27
    comps = (ux, uy, uz)
    for i in range(14):
        w = strength[WEIGHTS[i]]
        if i == 13:
            post[i] = jnp.where(solid, f[i], w * base + keep * f[i])
            continue
        along = None
        for c, u in zip(DIRS[i], comps):
            if c == 0:
                continue
            if along is None:
                along = u if c > 0 else -u
            else:
                along = along + u if c > 0 else along - u
        even = w * (base + 4.5 * (along * along))
        odd = w * (3.0 * along)
        j = 26 - i
        post[i] = jnp.where(solid, f[j], (even + odd) + keep * f[i])
        post[j] = jnp.where(solid, f[i], (even - odd) + keep * f[j])
    return post


def lanes_of(rows):
    return lax.broadcasted_iota(jnp.int32, (rows, LANES), 1)


def turn(value, shift, axis):
    size = value.shape[axis]
    if isinstance(shift, int):
        shift = shift % size
        if shift == 0:
            return value
    return pltpu.roll(value, shift, axis)


def first_kernel(f_hbm, solid_hbm, jet_hbm, p_ref, lo_ref, hi_ref, f_ref, solid_ref, jet_ref, sems):
    masks = [
        pltpu.make_async_copy(solid_hbm, solid_ref, sems.at[CELLS]),
        pltpu.make_async_copy(jet_hbm, jet_ref, sems.at[CELLS + 1]),
    ]
    copies = []
    for x in range(CELLS):
        rows = pl.ds(x * CELLS, CELLS)
        copies.append(pltpu.make_async_copy(f_hbm.at[:, rows, :], f_ref.at[:, rows, :], sems.at[x]))
    for copy in masks + copies:
        copy.start()
    for copy in masks:
        copy.wait()
    p_ref[SOLID] = solid_ref[...].astype(jnp.float32)
    p_ref[JET] = jet_ref[...].astype(jnp.float32)

    def plane(x):
        rows = pl.ds(x * CELLS, CELLS)
        f = [f_ref[i, rows, :] for i in range(27)]
        post = collide(f, solid_ref[rows, :] == 1, jet_ref[rows, :] == 1)
        for i in range(27):
            p_ref[i, rows, :] = post[i]

    for x in range(CELLS):
        copies[x].wait()
        plane(x)
    for k, (key, dist) in enumerate(axis_list(0, -1)):
        lo_ref[k] = p_ref[key, pl.ds((dist - 1) * CELLS, CELLS), :]
    for k, (key, dist) in enumerate(axis_list(0, 1)):
        hi_ref[k] = p_ref[key, pl.ds((CELLS - dist) * CELLS, CELLS), :]


LOW_AT = {entry: k for k, entry in enumerate(axis_list(0, 1))}
HIGH_AT = {entry: k for k, entry in enumerate(axis_list(0, -1))}


def plane_ref(key, x, p_ref, xlo_ref, xhi_ref):
    if x < 0:
        return xlo_ref.at[LOW_AT[(key, -x)]]
    if x >= CELLS:
        return xhi_ref.at[HIGH_AT[(key, x - CELLS + 1)]]
    return p_ref.at[key, pl.ds(x * CELLS, CELLS), :]


def second_kernel(p_ref, xlo_ref, xhi_ref, lo_ref, hi_ref):
    for inward, out_ref in ((-1, lo_ref), (1, hi_ref)):
        for k, (key, dist) in enumerate(axis_list(1, inward)):
            row = dist - 1 if inward < 0 else CELLS - dist
            out_ref[pl.ds(k * CELLS, CELLS), :] = p_ref[key, pl.ds(row, CELLS, stride=CELLS), :]
        for k, (key, dist, x) in enumerate(corner_list(inward)):
            row = dist - 1 if inward < 0 else CELLS - dist
            out_ref[pl.ds(Y_OWN + k, 1), :] = plane_ref(key, x, p_ref, xlo_ref, xhi_ref)[pl.ds(row, 1), :]


def faces_kernel(p_ref, xlo_ref, xhi_ref, z_ref):
    group = lanes_of(CELLS) // GROUP
    for key in range(29):
        acc = jnp.zeros((CELLS, LANES), jnp.float32)
        for plane in range(SPAN):
            if held(key, plane - REACH):
                value = plane_ref(key, plane - REACH, p_ref, xlo_ref, xhi_ref)[...]
                acc = jnp.where(group == LAST - plane, turn(value, GROUP * (LAST - plane) + 3, 1), acc)
        z_ref[key] = acc


def third_kernel(ylo_ref, yhi_ref, zmain_ref, h_ref, z_ref, lo_ref, hi_ref):
    for inward, in_ref in ((1, ylo_ref), (-1, yhi_ref)):
        for k, (key, dist) in enumerate(axis_list(1, inward)):
            start = CELLS * REACH + CELLS - dist if inward > 0 else CELLS * (REACH + 1) + dist - 1
            h_ref[key, pl.ds(start, CELLS, stride=CELLS), :] = in_ref[pl.ds(k * CELLS, CELLS), :]
        for k, (key, dist, x) in enumerate(corner_list(inward)):
            plane = x + REACH
            row = CELLS * plane + CELLS - dist if inward > 0 else CELLS * (plane + 1) + dist - 1
            h_ref[key, pl.ds(row, 1), :] = in_ref[pl.ds(Y_OWN + k, 1), :]
    lane = lanes_of(CELLS)
    group = lane // GROUP
    upper = lax.broadcasted_iota(jnp.int32, (CELLS, LANES), 0) < CELLS // 2
    for key in range(29):
        acc = jnp.zeros((CELLS, LANES), jnp.float32)
        for tile in range(SPAN + 1):
            value = turn(h_ref[key, pl.ds(tile * CELLS, CELLS), :], GROUP * (LAST - tile) + 3, 1)
            acc = jnp.where(group == (LAST - tile) % (LANES // GROUP), value, acc)
        z_ref[key, pl.ds(0, CELLS), :] = zmain_ref[key]
        z_ref[key, pl.ds(CELLS, CELLS), :] = jnp.where(upper, turn(acc, GROUP, 1), acc)
    early = lanes_of(2 * CELLS) % GROUP < REACH
    for k in range(HALF):
        first = z_ref[k]
        if k + HALF < 29:
            second = z_ref[k + HALF]
            lo_ref[k] = jnp.where(early, turn(second, -REACH, 1), first)
            hi_ref[k] = jnp.where(early, first, turn(second, REACH, 1))
        else:
            lo_ref[k] = first
            hi_ref[k] = first


def block_kernel(p_ref, xlo_ref, xhi_ref, h_ref, e_ref):
    for plane in range(SPAN):
        for key in range(29):
            if held(key, plane - REACH):
                e_ref[key, pl.ds(plane * ROWS + CELLS, CELLS), :] = plane_ref(
                    key, plane - REACH, p_ref, xlo_ref, xhi_ref
                )[...]
    for tile in range(SPAN + 1):
        for key in range(29):
            e_ref[key, pl.ds(tile * ROWS, CELLS), :] = h_ref[key, pl.ds(tile * CELLS, CELLS), :]


def face_sums(values):
    rows = [(row[0] + row[2]) + row[1] for row in values]
    second = (values[0][2] - values[0][0]) + (values[1][2] - values[1][0]) + (values[2][2] - values[2][0])
    return (rows[0] + rows[2]) + rows[1], rows[2] - rows[0], second


def fourth_kernel(e_ref, z_ref, zlo_ref, zhi_ref, adv_hbm, out_ref, g_ref, ge_ref, he_ref, flow_ref, adv_ref, sem):
    lane = lanes_of(CELLS)
    slot = lane % GROUP

    wide_slot = lanes_of(2 * CELLS) % GROUP
    for key in range(29):
        if key < HALF:
            low, high = zlo_ref[key], turn(zhi_ref[key], 2, 1)
        else:
            low, high = turn(zlo_ref[key - HALF], -REACH, 1), turn(zhi_ref[key - HALF], REACH + 2, 1)
        value = jnp.where(wide_slot < 3, low, high)
        if key < 27 and DIRS[key][2] == -1:
            value = jnp.where(wide_slot == 3, z_ref[key], value)
        elif key < 27 and DIRS[key][2] == 1:
            value = jnp.where(wide_slot == 4, turn(z_ref[key], 2, 1), value)
        ge_ref[key, pl.ds(CELLS, 2 * CELLS), :] = value
        ge_ref[key, pl.ds(0, CELLS), :] = value[CELLS:]

    def edge_stream(ref, y):
        return [
            turn(ref[i, pl.ds(CELLS + y - b, CELLS), :], c - GROUP * a, 1) for i, (a, b, c) in enumerate(DIRS)
        ]

    for y in (-2, 6):
        rows = pl.ds(CELLS + y, CELLS)
        post = collide(edge_stream(ge_ref, y), ge_ref[SOLID, rows, :] > 0.5, ge_ref[JET, rows, :] > 0.5)
        for i in range(27):
            he_ref[i, rows, :] = post[i]

    def settle(c, value, edge):
        return jnp.where(lane == (0 if c > 0 else LANES - 1), edge, turn(value, c, 1))

    def shift_to_end(c, plane):
        return (LANES - 2 if c > 0 else LANES - 6) - GROUP * (LAST - plane)

    def plane_rows(plane, y):
        return pl.ds(plane * ROWS + CELLS + y, CELLS)

    def plane_stream(ref, edge_ref, plane, y):
        still, out = [], []
        for i, (a, b, c) in enumerate(DIRS):
            value = ref[i, plane_rows(plane - a, y - b), :]
            still.append(value)
            if c != 0:
                edge = edge_ref[i, pl.ds(CELLS + y - b, CELLS), :]
                value = settle(c, value, turn(edge, shift_to_end(c, plane - a), 1))
            out.append(value)
        return still, out

    def row_slice(plane, y):
        return pl.ds(plane * ROWS + CELLS + y, CELLS, stride=ROWS)

    def row_stream(ref, edge_ref, y):
        out = []
        for i, (a, b, c) in enumerate(DIRS):
            value = ref[i, row_slice(REACH - a, y - b), :]
            if c != 0:
                edge = jnp.broadcast_to(edge_ref[i, pl.ds(CELLS + y - b, 1), :], (CELLS, LANES))
                edge = pltpu.roll(
                    edge, shift_to_end(c, REACH - a), 1, stride=GROUP, stride_axis=0
                )
                value = settle(c, value, edge)
            out.append(value)
        return out

    def step_one(plane, y):
        rows = plane_rows(plane, y)
        post = collide(
            plane_stream(e_ref, ge_ref, plane, y)[1], e_ref[SOLID, rows, :] > 0.5, e_ref[JET, rows, :] > 0.5
        )
        for i in range(27):
            g_ref[i, rows, :] = post[i]

    def step_one_own(k, carry):
        step_one(REACH + 2 * k, 0)
        step_one(REACH + 2 * k + 1, 0)
        return carry

    def step_one_halo(k, carry):
        plane = k + 1 + CELLS * (k // 2)
        step_one(plane, -2)
        step_one(plane, 6)
        return carry

    lax.fori_loop(0, CELLS // 2, step_one_own, 0)
    lax.fori_loop(0, 4, step_one_halo, 0)
    for y in (-2, -1, CELLS, CELLS + 1):
        rows = row_slice(REACH, y)
        post = collide(row_stream(e_ref, ge_ref, y), e_ref[SOLID, rows, :] > 0.5, e_ref[JET, rows, :] > 0.5)
        for i in range(27):
            g_ref[i, rows, :] = post[i]

    def velocity(f, solid):
        density, first, second, third = moments(f)
        scale = (1.0 - solid) / density
        return first * scale, second * scale, third * scale

    def store_flow(rows, f):
        for c, value in enumerate(velocity(f, e_ref[SOLID, rows, :])):
            flow_ref[c, rows, :] = value

    def by_pair(values, c):
        return [[values[9 * a + 3 * b + c + 1] for b in range(3)] for a in range(3)]

    def step_two(plane, acc):
        still, f = plane_stream(g_ref, he_ref, plane, 0)
        rows = pl.ds(pl.multiple_of((plane - REACH) * CELLS, CELLS), CELLS)
        for i in range(27):
            adv_ref[i, rows, :] = f[i]
        store_flow(plane_rows(plane, 0), f)
        place = (lane // GROUP == LAST - plane) & ((slot == 2) | (slot == 3))
        out = []
        for total, down, up in zip(acc, face_sums(by_pair(still, -1)), face_sums(by_pair(still, 1))):
            mixed = turn(jnp.where(lane == 0, down, up), GROUP * (LAST - plane) + 3, 1)
            out.append(jnp.where(place, mixed, total))
        return tuple(out)

    def step_two_own(k, acc):
        return step_two(REACH + 2 * k + 1, step_two(REACH + 2 * k, acc))

    acc = lax.fori_loop(0, CELLS // 2, step_two_own, tuple(jnp.zeros((CELLS, LANES), jnp.float32) for _ in range(3)))
    save = pltpu.make_async_copy(adv_ref, adv_hbm, sem)
    save.start()
    for plane in (REACH - 1, REACH + CELLS):
        store_flow(plane_rows(plane, 0), plane_stream(g_ref, he_ref, plane, 0)[1])
    for y in (-1, CELLS):
        store_flow(row_slice(REACH, y), row_stream(g_ref, he_ref, y))
    f = edge_stream(he_ref, 0)
    sums = [face_sums(by_pair(f, c)) for c in (-1, 0, 1)]
    high = slot == 5
    density, first, second = [
        middle + jnp.where(high, down, up) + jnp.where(high, turn(total, 3, 1), turn(total, -1, 1))
        for down, middle, up, total in zip(sums[0], sums[1], sums[2], acc)
    ]
    scale = (1.0 - ge_ref[SOLID, pl.ds(CELLS, CELLS), :]) / density
    edge_flow = (first * scale, second * scale)

    acc = jnp.zeros((CELLS, LANES), jnp.float32)
    for x in range(CELLS):
        plane = x + REACH
        here = [flow_ref[c, plane_rows(plane, 0), :] for c in range(3)]

        def along_first(c):
            return 0.5 * (flow_ref[c, plane_rows(plane + 1, 0), :] - flow_ref[c, plane_rows(plane - 1, 0), :])

        def along_second(c):
            return 0.5 * (flow_ref[c, plane_rows(plane, 1), :] - flow_ref[c, plane_rows(plane, -1), :])

        def along_third(c):
            low = settle(1, here[c], turn(edge_flow[c], shift_to_end(1, plane), 1))
            high = settle(-1, here[c], turn(edge_flow[c], shift_to_end(-1, plane), 1))
            return 0.5 * (high - low)

        vort_first = along_second(2) - along_third(1)
        vort_second = along_third(0) - along_first(2)
        vort_third = along_first(1) - along_second(0)
        s_two = vort_first * vort_first + vort_second * vort_second + vort_third * vort_third
        solid_on = e_ref[SOLID, plane_rows(plane, 0), :] > 0.5
        ratio = s_two / (s_two + shade_scale)
        alpha = jnp.where(solid_on, solid_alpha, alpha_top * (1.0 - jnp.exp(-s_two / shade_scale)))
        red = jnp.where(solid_on, 0.6, 0.3 + 1.5 * ratio)
        green = jnp.where(solid_on, 0.6, 1.2 - 0.9 * ratio)
        blue = jnp.where(solid_on, 0.6, 0.8 + 0.4 * jnp.tanh(20.0 * here[0]))
        logs = jnp.log1p(-alpha)
        running = logs
        for step in (1, 2, 4, 8, 16, 32, 64):
            running = running + jnp.where(lane >= step, turn(running, step, 1), 0.0)
        weight = alpha * jnp.exp(running - logs)
        for ch, value in enumerate((red * weight, green * weight, blue * weight, logs)):
            total = jnp.sum(value, axis=1, keepdims=True)
            acc = jnp.where(lane // UP == ch * CELLS + x, total, acc)
    out_ref[...] = acc
    save.wait()


def last_kernel(slab_ref, rank_ref, out_ref):
    slabs = slab_ref[...]
    rank = rank_ref[...]
    channel = lanes_of(CELLS) // (CELLS * UP)
    logs = slabs
    for ch in range(3):
        logs = jnp.where(channel == ch, turn(slabs, (ch + 1) * CELLS * UP, 1), logs)
    front = jnp.zeros_like(slabs)
    for s in range(CELLS):
        front = front + jnp.where(rank[s : s + 1] < rank, logs[s : s + 1], 0.0)
    colour = jnp.sum(jnp.exp(front) * slabs, axis=0, keepdims=True)
    opacity = 1.0 - jnp.exp(jnp.sum(logs, axis=0, keepdims=True))
    row = jnp.where(channel[:1] == 3, opacity, colour)
    for ch in range(4):
        out_ref[ch] = jnp.broadcast_to(turn(row, -ch * CELLS * UP, 1)[:, : CELLS * UP], (UP, CELLS * UP))


def call(kernel, outs, scratch=(), in_hbm=False, first_out_hbm=False):
    shapes = tuple(jax.ShapeDtypeStruct(shape, jnp.float32) for shape in outs)
    extra = {}
    if in_hbm:
        extra["in_specs"] = [pl.BlockSpec(memory_space=pltpu.HBM)] * 3
    if first_out_hbm:
        spaces = [pltpu.HBM] + [pltpu.VMEM] * (len(outs) - 1)
        extra["out_specs"] = tuple(pl.BlockSpec(memory_space=space) for space in spaces)
    return pl.pallas_call(
        kernel,
        out_shape=shapes,
        scratch_shapes=scratch,
        compiler_params=pltpu.CompilerParams(vmem_limit_bytes=24 * 1024 * 1024),
        **extra,
    )


def both_ways(lo, hi, axis):
    count = lax.axis_size(axis)
    forward = [(i, (i + 1) % count) for i in range(count)]
    backward = [(target, source) for source, target in forward]
    return lax.ppermute(hi, axis, forward), lax.ppermute(lo, axis, backward)


def body(populations, solid_mask, jet_mask, visibility):
    cells = CELLS * CELLS
    f = populations.reshape(27, cells, LANES)
    solid = solid_mask.reshape(cells, LANES)
    jet = jet_mask.reshape(cells, LANES)
    x_shape = (X_COUNT, CELLS, LANES)
    post, lo, hi = call(
        first_kernel,
        ((29, cells, LANES), x_shape, x_shape),
        (
            pltpu.VMEM((27, cells, LANES), jnp.float32),
            pltpu.VMEM((cells, LANES), jnp.int32),
            pltpu.VMEM((cells, LANES), jnp.int32),
            pltpu.SemaphoreType.DMA((CELLS + 2,)),
        ),
        in_hbm=True,
    )(f, solid, jet)
    xlo, xhi = both_ways(lo, hi, "gx")
    y_shape = (Y_COUNT, LANES)
    lo, hi = call(second_kernel, (y_shape, y_shape))(post, xlo, xhi)
    ylo, yhi = both_ways(lo, hi, "gy")
    (main,) = call(faces_kernel, ((29, CELLS, LANES),))(post, xlo, xhi)
    half_shape = (HALF, 2 * CELLS, LANES)
    halo, face, lo, hi = call(
        third_kernel, ((29, (SPAN + 1) * CELLS, LANES), (29, 2 * CELLS, LANES), half_shape, half_shape)
    )(ylo, yhi, main)
    zlo, zhi = both_ways(lo, hi, "gz")
    height = SPAN * ROWS + CELLS
    (block,) = call(block_kernel, ((29, height, LANES),))(post, xlo, xhi, halo)
    advanced, slabs = call(
        fourth_kernel,
        ((27, cells, LANES), (CELLS, LANES)),
        (
            pltpu.VMEM((27, height, LANES), jnp.float32),
            pltpu.VMEM((29, 3 * CELLS, LANES), jnp.float32),
            pltpu.VMEM((27, 3 * CELLS, LANES), jnp.float32),
            pltpu.VMEM((3, height, LANES), jnp.float32),
            pltpu.VMEM((27, cells, LANES), jnp.float32),
            pltpu.SemaphoreType.DMA,
        ),
        first_out_hbm=True,
    )(block, face, zlo, zhi)
    slabs = lax.all_to_all(slabs, "gz", 0, 0, tiled=True)
    rank = jnp.broadcast_to(visibility[:, None], (CELLS, LANES))
    (image,) = call(last_kernel, ((4, UP, CELLS * UP),))(slabs, rank)
    return advanced.reshape(27, CELLS, CELLS, LANES), jnp.swapaxes(image, 1, 2)


def solution(mesh):
    return jax.shard_map(
        body,
        mesh=mesh,
        in_specs=(P(None, "gx", "gy", "gz"), P("gx", "gy", "gz"), P("gx", "gy", "gz"), P()),
        out_specs=(P(None, "gx", "gy", "gz"), P(None, "gx", ("gy", "gz"))),
        check_vma=False,
    )
```

time: 80.7 us -> 68.6 us (0.85)
  Pallas kernels: 17.6 us -> 9 us
  waiting for transfers between devices: 18.6 us -> 16.7 us
  local copies, waits for them, and re-layouts: 4.27 us -> 2.75 us
    pallas_call x4 -> x6, Pallas kernels: 16.8 us -> 8.23 us  [the longest x1 4.26 us: body(): call(fourth_kernel, ((27, cells, LANES), (CELLS, LANES)), (pltpu.VMEM((27...]
    ppermute x6, waiting for transfers between devices: 18.6 us -> 16.7 us  [both_ways(): return (lax.ppermute(hi, axis, forward), lax.ppermute(lo, axis, backward))]
    unnamed x12 -> x8, local copies, waits for them, and re-layouts: 4.2 us -> 2.68 us
  transfers between devices with their start and end apart: 6 -> 6, of which waited for: 5 -> 5; matrix products, arithmetic and copies ran while one was open for 0% -> 0% of each run, Pallas kernels for 0% -> 1%
where the time goes in v2:
time: 68.6 us; the launch traced here: 68.2 us
  starting transfers between devices  29.7 us (43%)
  waiting for transfers between devices  16.7 us (24%)
  blocking collectives  9.29 us (14%)
  Pallas kernels  9 us (13%)
  local copies, waits for them, and re-layouts  2.75 us (4%)
  between operations  0.72 us (1%)
    ppermute x6, starting transfers between devices, both_ways(): return (lax.ppermute(hi, axis, forward), lax.ppermute(lo, axis, backward))  29.7 us
    ppermute x6, waiting for transfers between devices, both_ways(): return (lax.ppermute(hi, axis, forward), lax.ppermute(lo, axis, backward))  16.7 us
    all_to_all x1, blocking collectives, body(): slabs = lax.all_to_all(slabs, 'gz', 0, 0, tiled=True)  9.29 us
    pallas_call x1, Pallas kernels, body(): call(fourth_kernel, ((27, cells, LANES), (CELLS, LANES)), (pltpu.VMEM((27...  4.26 us
    unnamed x8, local copies, waits for them, and re-layouts  2.68 us
    pallas_call x1, Pallas kernels, body(): call(third_kernel, ((29, (SPAN + 1) * CELLS, LANES), (29, 2 * CELLS, LANE...  2.24 us
  transfers between devices with their start and end apart: 6, of which 5 were waited for; matrix products, arithmetic and copies ran while one was open for 0% of the time, Pallas kernels for 1%

profile of v2, /device:TPU:24, one launch (start us, length us, event | category | flops | bytes accessed | tf_op | source)
XLA Modules:
  0.0 68.2 jit_solution(11028729124286270936)
XLA Ops:
  0.6 0.0 copy-start
  0.6 1.2 %copy-done = f32[27,8,8,128]{3,2,1,0:T(8,128)S(1)} copy-done((f32[27,8,8,128]{3,2,1,0:T(8,128)S(1)}, f32[27,8,8,128]{3,2,1,0:T(8,128)}, u32[]{:S(2)}) %copy-start) | copy-done | bytes 884760
  1.8 0.0 copy-start.1
  1.8 0.8 %copy-done.1 = s32[8,8,128]{2,1,0:T(8,128)S(1)} copy-done((s32[8,8,128]{2,1,0:T(8,128)S(1)}, s32[8,8,128]{2,1,0:T(8,128)}, u32[]{:S(2)}) %copy-start.1) | copy-done | bytes 32792
  2.6 0.0 copy-start.2
  2.6 0.8 %copy-done.2 = s32[8,8,128]{2,1,0:T(8,128)S(1)} copy-done((s32[8,8,128]{2,1,0:T(8,128)S(1)}, s32[8,8,128]{2,1,0:T(8,128)}, u32[]{:S(2)}) %copy-start.2) | copy-done | bytes 32792
  3.3 0.8 %shard_map.59 = (f32[29,64,128]{2,1,0:T(8,128)S(1)}, f32[58,8,128]{2,1,0:T(8,128)S(1)}, f32[58,8,128]{2,1,0:T(8,128)S(1)}) custom-call(f32[27,64,128]{2,1,0:T(8,128)S(1)} %bitcast.9, s32[64,128]{1,0:T(8,128)S(1)} %bitcast.10, s32[64,128]{1,0:T(8,128)S(1)} %bitcast.11), custom_call_target="tpu_custom_call" | custom-call | tf_op jit(solution)/shard_map/pallas_call | solution.py:458
  4.2 4.7 %collective-permute-start = (f32[58,8,128]{2,1,0:T(8,128)S(1)}, f32[58,8,128]{2,1,0:T(8,128)S(1)}, u32[]{:S(2)}, u32[]{:S(2)}) collective-permute-start(f32[58,8,128]{2,1,0:T(8,128)S(1)} %get-tuple-element.14), channel_id=1, source_target_pairs={{0,128},{128,256},{256,384},{384,512},{512,640},{640,768},{768,896... | collective-permute-start | bytes 712712 | tf_op jit(solution)/shard_map/ppermute | solution.py:449
  8.9 1.9 %collective-permute-start.1 = (f32[58,8,128]{2,1,0:T(8,128)S(1)}, f32[58,8,128]{2,1,0:T(8,128)S(1)}, u32[]{:S(2)}, u32[]{:S(2)}) collective-permute-start(f32[58,8,128]{2,1,0:T(8,128)S(1)} %get-tuple-element.15), channel_id=1, source_target_pairs={{128,0},{256,128},{384,256},{512,384},{640,512},{768,640},{896,768... | collective-permute-start | bytes 712712 | tf_op jit(solution)/shard_map/ppermute | solution.py:449
  10.8 3.1 %collective-permute-done.xlo_ref = f32[58,8,128]{2,1,0:T(8,128)S(1)} collective-permute-done((f32[58,8,128]{2,1,0:T(8,128)S(1)}, f32[58,8,128]{2,1,0:T(8,128)S(1)}, u32[]{:S(2)}, u32[]{:S(2)}) %collective-permute-start) | collective-permute-done | bytes 237600 | tf_op jit(solution)/shard_map/ppermute | solution.py:449
  13.9 5.3 %collective-permute-done.1.xhi_ref = f32[58,8,128]{2,1,0:T(8,128)S(1)} collective-permute-done((f32[58,8,128]{2,1,0:T(8,128)S(1)}, f32[58,8,128]{2,1,0:T(8,128)S(1)}, u32[]{:S(2)}, u32[]{:S(2)}) %collective-permute-start.1) | collective-permute-done | bytes 237600 | tf_op jit(solution)/shard_map/ppermute | solution.py:449
  19.2 0.2 shard_map.60
  19.5 4.3 %collective-permute-start.2 = (f32[696,128]{1,0:T(8,128)S(1)}, f32[696,128]{1,0:T(8,128)S(1)}, u32[]{:S(2)}, u32[]{:S(2)}) collective-permute-start(f32[696,128]{1,0:T(8,128)S(1)} %get-tuple-element.16), channel_id=1, source_target_pairs={{0,8},{8,16},{16,24},{24,32},{32,40},{40,48},{48,56},{56,64},{64,7... | collective-permute-start | bytes 1069064 | tf_op jit(solution)/shard_map/ppermute | solution.py:449
  23.7 15.9 %collective-permute-start.3 = (f32[696,128]{1,0:T(8,128)S(1)}, f32[696,128]{1,0:T(8,128)S(1)}, u32[]{:S(2)}, u32[]{:S(2)}) collective-permute-start(f32[696,128]{1,0:T(8,128)S(1)} %get-tuple-element.17), channel_id=1, source_target_pairs={{8,0},{16,8},{24,16},{32,24},{40,32},{48,40},{56,48},{64,56},{72,6... | collective-permute-start | bytes 1069064 | tf_op jit(solution)/shard_map/ppermute | solution.py:449
  39.6 0.4 shard_map.61.zmain_ref
  40.1 4.8 %collective-permute-done.2.ylo_ref = f32[696,128]{1,0:T(8,128)S(1)} collective-permute-done((f32[696,128]{1,0:T(8,128)S(1)}, f32[696,128]{1,0:T(8,128)S(1)}, u32[]{:S(2)}, u32[]{:S(2)}) %collective-permute-start.2) | collective-permute-done | bytes 356384 | tf_op jit(solution)/shard_map/ppermute | solution.py:449
  44.8 1.2 %collective-permute-done.3.yhi_ref = f32[696,128]{1,0:T(8,128)S(1)} collective-permute-done((f32[696,128]{1,0:T(8,128)S(1)}, f32[696,128]{1,0:T(8,128)S(1)}, u32[]{:S(2)}, u32[]{:S(2)}) %collective-permute-start.3) | collective-permute-done | bytes 356384 | tf_op jit(solution)/shard_map/ppermute | solution.py:449
  46.0 2.2 %shard_map.62 = (f32[29,120,128]{2,1,0:T(8,128)S(1)}, f32[29,16,128]{2,1,0:T(8,128)S(1)}, f32[15,16,128]{2,1,0:T(8,128)S(1)}, f32[15,16,128]{2,1,0:T(8,128)S(1)}) custom-call(f32[696,128]{1,0:T(8,128)S(1)} %collective-permute-done.2.ylo_ref, f32[696,128]{1,0:T(8,128)S(1)} %collective-permute-done.3.yhi_ref, f32[29,8,128]{2,1,0:T(8,128)S(1)} %shard_map.61.zmain_ref), custom_call_target="tpu_custom_call" | custom-call | tf_op jit(solution)/shard_map/pallas_call | solution.py:475
  48.2 0.0 collective-permute-start.4
  48.3 2.9 %collective-permute-start.5 = (f32[15,16,128]{2,1,0:T(8,128)S(1)}, f32[15,16,128]{2,1,0:T(8,128)S(1)}, u32[]{:S(2)}, u32[]{:S(2)}) collective-permute-start(f32[15,16,128]{2,1,0:T(8,128)S(1)} %get-tuple-element.21), channel_id=1, source_target_pairs={{1,0},{2,1},{3,2},{4,3},{5,4},{6,5},{7,6},{0,7},{9,8},{10,9},{11,1... | collective-permute-start | bytes 368648 | tf_op jit(solution)/shard_map/ppermute | solution.py:449
  51.2 0.2 shard_map.63.e_ref
  51.4 0.0 copy-start.3
  51.4 2.3 %collective-permute-done.4.zlo_ref = f32[15,16,128]{2,1,0:T(8,128)S(1)} collective-permute-done((f32[15,16,128]{2,1,0:T(8,128)S(1)}, f32[15,16,128]{2,1,0:T(8,128)S(1)}, u32[]{:S(2)}, u32[]{:S(2)}) %collective-permute-start.4) | collective-permute-done | bytes 122912 | tf_op jit(solution)/shard_map/ppermute | solution.py:449
  53.8 0.0 collective-permute-done.5.zhi_ref
  53.8 4.3 %shard_map.64 = (f32[27,64,128]{2,1,0:T(8,128)}, f32[8,128]{1,0:T(8,128)S(1)}) custom-call(f32[29,232,128]{2,1,0:T(8,128)S(1)} %shard_map.63.e_ref, f32[29,16,128]{2,1,0:T(8,128)S(1)} %get-tuple-element.19.z_ref, f32[15,16,128]{2,1,0:T(8,128)S(1)} %collective-permute-done.4.zlo_ref, f32[15,16,128]{2,1,0:T(8,128)S(1)} %collective-permute-done.5.zhi_ref), custom_call_target="tpu_custom_call" | custom-call | tf_op jit(solution)/shard_map/pallas_call | solution.py:481
  58.0 9.3 %all_to_all.11 = f32[8,1,128]{2,1,0:T(1,128)S(1)} all-to-all(f32[8,1,128]{2,1,0:T(1,128)S(1)} %bitcast.13), channel_id=1, replica_groups=mesh['gx'=8,'gy'=16,'gz'=8] {'gz'}, dimensions={0} | all-to-all | bytes 8192 | tf_op jit(solution)/shard_map/all_to_all | solution.py:494
  67.3 0.0 copy-done.3
  67.3 0.1 broadcast_in_dim.2.rank_ref
  67.4 0.8 %shard_map.65 = f32[4,4,32]{2,1,0:T(4,128)} custom-call(f32[8,128]{1,0:T(8,128)S(1)} %bitcast.12, s32[8,128]{1,0:T(8,128)S(1)} %broadcast_in_dim.2.rank_ref), custom_call_target="tpu_custom_call" | custom-call | tf_op jit(solution)/shard_map/pallas_call | solution.py:496
Async XLA Ops:
  0.6 1.2 %copy-start = (f32[27,8,8,128]{3,2,1,0:T(8,128)S(1)}, f32[27,8,8,128]{3,2,1,0:T(8,128)}, u32[]{:S(2)}) copy-start(f32[27,8,8,128]{3,2,1,0:T(8,128)} %param.4) | copy-start | bytes 2654212
  1.8 0.8 %copy-start.1 = (s32[8,8,128]{2,1,0:T(8,128)S(1)}, s32[8,8,128]{2,1,0:T(8,128)}, u32[]{:S(2)}) copy-start(s32[8,8,128]{2,1,0:T(8,128)} %param.5) | copy-start | bytes 98308
  2.6 0.8 %copy-start.2 = (s32[8,8,128]{2,1,0:T(8,128)S(1)}, s32[8,8,128]{2,1,0:T(8,128)}, u32[]{:S(2)}) copy-start(s32[8,8,128]{2,1,0:T(8,128)} %param.6) | copy-start | bytes 98308
  4.2 9.7 %collective-permute-start = (f32[58,8,128]{2,1,0:T(8,128)S(1)}, f32[58,8,128]{2,1,0:T(8,128)S(1)}, u32[]{:S(2)}, u32[]{:S(2)}) collective-permute-start(f32[58,8,128]{2,1,0:T(8,128)S(1)} %get-tuple-element.14), channel_id=1, source_target_pairs={{0,128},{128,256},{256,384},{384,512},{512,640},{640,768},{768,896... | collective-permute-start | bytes 712712 | tf_op jit(solution)/shard_map/ppermute | solution.py:449
  8.9 10.3 %collective-permute-start.1 = (f32[58,8,128]{2,1,0:T(8,128)S(1)}, f32[58,8,128]{2,1,0:T(8,128)S(1)}, u32[]{:S(2)}, u32[]{:S(2)}) collective-permute-start(f32[58,8,128]{2,1,0:T(8,128)S(1)} %get-tuple-element.15), channel_id=1, source_target_pairs={{128,0},{256,128},{384,256},{512,384},{640,512},{768,640},{896,768... | collective-permute-start | bytes 712712 | tf_op jit(solution)/shard_map/ppermute | solution.py:449
  19.5 25.4 %collective-permute-start.2 = (f32[696,128]{1,0:T(8,128)S(1)}, f32[696,128]{1,0:T(8,128)S(1)}, u32[]{:S(2)}, u32[]{:S(2)}) collective-permute-start(f32[696,128]{1,0:T(8,128)S(1)} %get-tuple-element.16), channel_id=1, source_target_pairs={{0,8},{8,16},{16,24},{24,32},{32,40},{40,48},{48,56},{56,64},{64,7... | collective-permute-start | bytes 1069064 | tf_op jit(solution)/shard_map/ppermute | solution.py:449
  23.7 22.2 %collective-permute-start.3 = (f32[696,128]{1,0:T(8,128)S(1)}, f32[696,128]{1,0:T(8,128)S(1)}, u32[]{:S(2)}, u32[]{:S(2)}) collective-permute-start(f32[696,128]{1,0:T(8,128)S(1)} %get-tuple-element.17), channel_id=1, source_target_pairs={{8,0},{16,8},{24,16},{32,24},{40,32},{48,40},{56,48},{64,56},{72,6... | collective-permute-start | bytes 1069064 | tf_op jit(solution)/shard_map/ppermute | solution.py:449
  48.2 5.5 %collective-permute-start.4 = (f32[15,16,128]{2,1,0:T(8,128)S(1)}, f32[15,16,128]{2,1,0:T(8,128)S(1)}, u32[]{:S(2)}, u32[]{:S(2)}) collective-permute-start(f32[15,16,128]{2,1,0:T(8,128)S(1)} %get-tuple-element.20), channel_id=1, source_target_pairs={{0,1},{1,2},{2,3},{3,4},{4,5},{5,6},{6,7},{7,0},{8,9},{9,10},{10,1... | collective-permute-start | bytes 368648 | tf_op jit(solution)/shard_map/ppermute | solution.py:449
  48.3 5.5 %collective-permute-start.5 = (f32[15,16,128]{2,1,0:T(8,128)S(1)}, f32[15,16,128]{2,1,0:T(8,128)S(1)}, u32[]{:S(2)}, u32[]{:S(2)}) collective-permute-start(f32[15,16,128]{2,1,0:T(8,128)S(1)} %get-tuple-element.21), channel_id=1, source_target_pairs={{1,0},{2,1},{3,2},{4,3},{5,4},{6,5},{7,6},{0,7},{9,8},{10,9},{11,1... | collective-permute-start | bytes 368648 | tf_op jit(solution)/shard_map/ppermute | solution.py:449
  51.4 15.9 %copy-start.3 = (s32[8]{0:T(128)S(1)}, s32[8]{0:T(128)}, u32[]{:S(2)}) copy-start(s32[8]{0:T(128)} %param.7) | copy-start | bytes 100

commit v3 on v2

v3 whole, which is shorter than its diff:
```python
import jax
import jax.numpy as jnp
import numpy as np
from jax import lax
from jax.experimental import pallas as pl
from jax.experimental.pallas import tpu as pltpu
from jax.sharding import PartitionSpec as P

UP = 4
CELLS = 8
LANES = 128
REACH = 3
SPAN = CELLS + 2 * REACH
LAST = SPAN - 1
ROWS = 16
HALF = 15
GROUP = 8

omega_rate = 1.25
jet_speed = 0.12
alpha_top = 0.03
solid_alpha = 0.15
shade_scale = 0.002

DIRS = [(a, b, c) for a in (-1, 0, 1) for b in (-1, 0, 1) for c in (-1, 0, 1)]
WEIGHTS = [(8.0 / 27.0, 2.0 / 27.0, 1.0 / 54.0, 1.0 / 216.0)[abs(a) + abs(b) + abs(c)] for a, b, c in DIRS]
SOLID, JET = 27, 28
MASKS = (SOLID, JET)


def axis_list(axis, inward):
    out = []
    for dist, allowed in ((1, (-1, 0, 1)), (2, (0, inward)), (3, (inward,))):
        out += [(i, dist) for i in range(27) if DIRS[i][axis] in allowed]
    out += [(m, dist) for m in MASKS for dist in (1, 2)]
    return out


def held(key, x):
    dist, inward = (-x, 1) if x < 0 else (x - CELLS + 1, -1)
    if dist <= 0:
        return True
    return (key, dist) in axis_list(0, inward)


def corner_list(inward):
    out = []
    for key, dist in axis_list(1, inward):
        first, second = (0, 0) if key in MASKS else DIRS[key][:2]
        for x in (-3, -2, -1, 8, 9, 10):
            far = -(x + first) if x < 0 else x + first - CELLS + 1
            if held(key, x) and not (far >= 2 and dist - inward * second >= 2):
                out.append((key, dist, x))
    return out


X_COUNT = len(axis_list(0, 1))
Y_OWN = len(axis_list(1, 1)) * CELLS
Y_COUNT = Y_OWN + -(-len(corner_list(1)) // 8) * 8


def moments(f):
    third = None
    parts = []
    for a in range(3):
        row = []
        for b in range(3):
            lo, mid, hi = f[9 * a + 3 * b], f[9 * a + 3 * b + 1], f[9 * a + 3 * b + 2]
            row.append((lo + hi) + mid)
            diff = hi - lo
            third = diff if third is None else third + diff
        parts.append(row)
    sums = [(row[0] + row[2]) + row[1] for row in parts]
    second = (parts[0][2] - parts[0][0]) + (parts[1][2] - parts[1][0]) + (parts[2][2] - parts[2][0])
    return (sums[0] + sums[2]) + sums[1], sums[2] - sums[0], second, third


def collide(f, solid, jet):
    density, first, second, third = moments(f)
    scale = 1.0 / density
    ux = jnp.where(jet, jet_speed, first * scale)
    uy = jnp.where(jet, 0.0, second * scale)
    uz = jnp.where(jet, 0.0, third * scale)
    gain = jnp.where(jet, 1.0, omega_rate) * density
    keep = jnp.where(jet, 0.0, 1.0 - omega_rate)
    base = 1.0 - 1.5 * (ux * ux + uy * uy + uz * uz)
    strength = {w: gain * w for w in set(WEIGHTS)}
    post = [None] * 27
    comps = (ux, uy, uz)
    for i in range(14):
        w = strength[WEIGHTS[i]]
        if i == 13:
            post[i] = jnp.where(solid, f[i], w * base + keep * f[i])
            continue
        along = None
        for c, u in zip(DIRS[i], comps):
            if c == 0:
                continue
            if along is None:
                along = u if c > 0 else -u
            else:
                along = along + u if c > 0 else along - u
        even = w * (base + 4.5 * (along * along))
        odd = w * (3.0 * along)
        j = 26 - i
        post[i] = jnp.where(solid, f[j], (even + odd) + keep * f[i])
        post[j] = jnp.where(solid, f[i], (even - odd) + keep * f[j])
    return post


def lanes_of(rows):
    return lax.broadcasted_iota(jnp.int32, (rows, LANES), 1)


def turn(value, shift, axis):
    size = value.shape[axis]
    if isinstance(shift, int):
        shift = shift % size
        if shift == 0:
            return value
    return pltpu.roll(value, shift, axis)


def first_kernel(f_ref, mask_ref, p_ref, lo_ref, hi_ref):
    for k, key in enumerate(MASKS):
        p_ref[key] = mask_ref[k]
    for x in range(CELLS):
        rows = pl.ds(x * CELLS, CELLS)
        f = [f_ref[i, rows, :] for i in range(27)]
        post = collide(f, mask_ref[0, rows, :] > 0.5, mask_ref[1, rows, :] > 0.5)
        for i in range(27):
            p_ref[i, rows, :] = post[i]
    for k, (key, dist) in enumerate(axis_list(0, -1)):
        lo_ref[k] = p_ref[key, pl.ds((dist - 1) * CELLS, CELLS), :]
    for k, (key, dist) in enumerate(axis_list(0, 1)):
        hi_ref[k] = p_ref[key, pl.ds((CELLS - dist) * CELLS, CELLS), :]


LOW_AT = {entry: k for k, entry in enumerate(axis_list(0, 1))}
HIGH_AT = {entry: k for k, entry in enumerate(axis_list(0, -1))}


def plane_ref(key, x, p_ref, xlo_ref, xhi_ref):
    if x < 0:
        return xlo_ref.at[LOW_AT[(key, -x)]]
    if x >= CELLS:
        return xhi_ref.at[HIGH_AT[(key, x - CELLS + 1)]]
    return p_ref.at[key, pl.ds(x * CELLS, CELLS), :]


def second_kernel(p_ref, xlo_ref, xhi_ref, lo_ref, hi_ref):
    for inward, out_ref in ((-1, lo_ref), (1, hi_ref)):
        for k, (key, dist) in enumerate(axis_list(1, inward)):
            row = dist - 1 if inward < 0 else CELLS - dist
            out_ref[pl.ds(k * CELLS, CELLS), :] = p_ref[key, pl.ds(row, CELLS, stride=CELLS), :]
        for k, (key, dist, x) in enumerate(corner_list(inward)):
            row = dist - 1 if inward < 0 else CELLS - dist
            out_ref[pl.ds(Y_OWN + k, 1), :] = plane_ref(key, x, p_ref, xlo_ref, xhi_ref)[pl.ds(row, 1), :]


def pack(tiles):
    group = lanes_of(CELLS) // GROUP
    acc = [jnp.zeros((CELLS, LANES), jnp.float32)] * 29
    for place, shift, load in tiles:
        here = group == place % (LANES // GROUP)
        for key in range(29):
            value = load(key)
            if value is not None:
                acc[key] = jnp.where(here, turn(value, shift, 1), acc[key])
    return acc


def faces_kernel(p_ref, xlo_ref, xhi_ref, low_ref, high_ref):
    def load(key, plane):
        if held(key, plane - REACH):
            return plane_ref(key, plane - REACH, p_ref, xlo_ref, xhi_ref)[...]

    for out_ref, start in ((low_ref, 3), (high_ref, 5)):
        tiles = [
            (LAST - plane, GROUP * (LAST - plane) + start, lambda key, plane=plane: load(key, plane))
            for plane in range(SPAN)
        ]
        for key, value in enumerate(pack(tiles)):
            out_ref[key] = value


def pack_halo(h_ref, start):
    upper = lax.broadcasted_iota(jnp.int32, (CELLS, LANES), 0) < CELLS // 2
    tiles = [
        (
            LAST - tile,
            GROUP * (LAST - tile) + start,
            lambda key, tile=tile: h_ref[key, pl.ds(tile * CELLS, CELLS), :],
        )
        for tile in range(SPAN + 1)
    ]
    return [jnp.where(upper, turn(value, GROUP, 1), value) for value in pack(tiles)]


def third_kernel(ylo_ref, yhi_ref, main_ref, h_ref, z_ref, lo_ref, hi_ref):
    for inward, in_ref in ((1, ylo_ref), (-1, yhi_ref)):
        for k, (key, dist) in enumerate(axis_list(1, inward)):
            start = CELLS * REACH + CELLS - dist if inward > 0 else CELLS * (REACH + 1) + dist - 1
            h_ref[key, pl.ds(start, CELLS, stride=CELLS), :] = in_ref[pl.ds(k * CELLS, CELLS), :]
        for k, (key, dist, x) in enumerate(corner_list(inward)):
            plane = x + REACH
            row = CELLS * plane + CELLS - dist if inward > 0 else CELLS * (plane + 1) + dist - 1
            h_ref[key, pl.ds(row, 1), :] = in_ref[pl.ds(Y_OWN + k, 1), :]
    halo = pack_halo(h_ref, 3)
    early = lanes_of(CELLS) % GROUP < REACH
    for key in range(29):
        z_ref[key] = halo[key]
    for part, values in enumerate(([main_ref[key] for key in range(29)], halo)):
        rows = pl.ds(part * CELLS, CELLS)
        for out_ref, shift in ((lo_ref, -REACH), (hi_ref, REACH)):
            for k in range(HALF):
                value = values[k]
                if k + HALF < 29:
                    other = turn(values[k + HALF], shift, 1)
                    value = jnp.where(early, other, value) if shift < 0 else jnp.where(early, value, other)
                out_ref[k, rows, :] = value


def plane_rows(plane, y):
    return pl.ds(plane * ROWS + CELLS + y, CELLS)


def row_slice(plane, y):
    return pl.ds(plane * ROWS + CELLS + y, CELLS, stride=ROWS)


def velocity(f, solid):
    density, first, second, third = moments(f)
    scale = (1.0 - solid) / density
    return first * scale, second * scale, third * scale


def steps_kernel(p_ref, xlo_ref, xhi_ref, h_ref, adv_ref, flow_ref, high_ref, e_ref, g_ref):
    for plane in range(SPAN):
        for key in range(29):
            if held(key, plane - REACH):
                e_ref[key, plane_rows(plane, 0), :] = plane_ref(key, plane - REACH, p_ref, xlo_ref, xhi_ref)[...]
    for tile in range(SPAN + 1):
        for key in range(29):
            e_ref[key, pl.ds(tile * ROWS, CELLS), :] = h_ref[key, pl.ds(tile * CELLS, CELLS), :]

    def stream(ref, rows):
        out = [None] * 27
        for move in (-1, 1, 0):
            for i, (a, b, c) in enumerate(DIRS):
                if c == move:
                    out[i] = turn(ref[i, rows(a, b), :], c, 1)
        return out

    def plane_stream(ref, plane, y):
        return stream(ref, lambda a, b: plane_rows(plane - a, y - b))

    def row_stream(ref, y):
        return stream(ref, lambda a, b: row_slice(REACH - a, y - b))

    def settle(rows, f):
        post = collide(f, e_ref[SOLID, rows, :] > 0.5, e_ref[JET, rows, :] > 0.5)
        for i in range(27):
            g_ref[i, rows, :] = post[i]

    def step_one(plane, y):
        settle(plane_rows(plane, y), plane_stream(e_ref, plane, y))

    def step_one_own(k, carry):
        step_one(REACH + 2 * k, 0)
        step_one(REACH + 2 * k + 1, 0)
        return carry

    def step_one_halo(k, carry):
        plane = k + 1 + CELLS * (k // 2)
        step_one(plane, -2)
        step_one(plane, 6)
        return carry

    lax.fori_loop(0, CELLS // 2, step_one_own, 0)
    lax.fori_loop(0, 4, step_one_halo, 0)
    for y in (-2, -1, CELLS, CELLS + 1):
        settle(row_slice(REACH, y), row_stream(e_ref, y))

    def store_flow(rows, f):
        for c, value in enumerate(velocity(f, e_ref[SOLID, rows, :])):
            flow_ref[c, rows, :] = value

    def step_two(plane):
        f = plane_stream(g_ref, plane, 0)
        rows = pl.ds(pl.multiple_of((plane - REACH) * CELLS, CELLS), CELLS)
        for i in range(27):
            adv_ref[i, rows, :] = f[i]
        store_flow(plane_rows(plane, 0), f)

    def step_two_own(k, carry):
        step_two(REACH + 2 * k)
        step_two(REACH + 2 * k + 1)
        return carry

    lax.fori_loop(0, CELLS // 2, step_two_own, 0)
    for plane in (REACH - 1, REACH + CELLS):
        store_flow(plane_rows(plane, 0), plane_stream(g_ref, plane, 0))
    for y in (-1, CELLS):
        store_flow(row_slice(REACH, y), row_stream(g_ref, y))
    for key, value in enumerate(pack_halo(h_ref, 5)):
        high_ref[key] = value


def render_kernel(
    p_ref, adv_ref, flow_ref, lmain_ref, lhalo_ref, hmain_ref, hhalo_ref, zlo_ref, zhi_ref,
    adv_hbm, out_ref, low_ref, high_ref, lpost_ref, hpost_ref, done_ref, rim_ref, sem,
):
    lane = lanes_of(CELLS)
    slot = lane % GROUP
    ends = (lane < 2) | (lane >= LANES - 2)

    for part in range(2):
        rows = pl.ds(part * CELLS, CELLS)
        own_low, own_high = (lmain_ref, hmain_ref) if part == 0 else (lhalo_ref, hhalo_ref)
        low = [zlo_ref[key, rows, :] for key in range(HALF)]
        low += [turn(zlo_ref[key, rows, :], -REACH, 1) for key in range(29 - HALF)]
        high = [turn(zhi_ref[key, rows, :], 2, 1) for key in range(HALF)]
        high += [turn(zhi_ref[key, rows, :], REACH + 2, 1) for key in range(29 - HALF)]
        for key in range(29):
            first = jnp.where(slot < 3, low[key], own_low[key])
            second = jnp.where(slot >= 5, high[key], own_high[key])
            for start in (CELLS,) if part == 0 else (0, 2 * CELLS):
                low_ref[key, pl.ds(start, CELLS), :] = first
                high_ref[key, pl.ds(start, CELLS), :] = second

    def edge_stream(ref, rows):
        out = [None] * 27
        for a in (-1, 0, 1):
            for c in (-1, 0, 1):
                for b in (-1, 0, 1):
                    i = 9 * a + 3 * b + c + 13
                    out[i] = turn(ref[i, rows(b), :], c - GROUP * a, 1)
        return out

    for y in (-2, 6):
        for ref, post_ref in ((low_ref, lpost_ref), (high_ref, hpost_ref)):
            rows = pl.ds(CELLS + y, CELLS)
            f = edge_stream(ref, lambda b: pl.ds(CELLS + y - b, CELLS))
            post = collide(f, ref[SOLID, rows, :] > 0.5, ref[JET, rows, :] > 0.5)
            for i in range(27):
                post_ref[i, rows, :] = post[i]

    def join(low, high):
        return jnp.where(lanes_of(low.shape[0]) % GROUP < 3, turn(high, -2, 1), low)

    f_low = edge_stream(lpost_ref, lambda b: pl.ds(CELLS - b, CELLS))
    flow_low = velocity(f_low, low_ref[SOLID, pl.ds(CELLS, CELLS), :])
    f_high = edge_stream(hpost_ref, lambda b: pl.ds(CELLS - b, CELLS))
    flow_high = velocity(f_high, high_ref[SOLID, pl.ds(CELLS, CELLS), :])
    joined = [join(low, high) for low, high in zip(f_low, f_high)]
    for x in range(CELLS):
        rows = pl.ds(x * CELLS, CELLS)
        shift = -(GROUP * (LAST - REACH - x) + 3)
        for i in range(27):
            done_ref[i, rows, :] = jnp.where(ends, turn(joined[i], shift, 1), adv_ref[i, rows, :])
    save = pltpu.make_async_copy(done_ref, adv_hbm, sem)
    save.start()
    joined = [join(low, high) for low, high in zip(flow_low, flow_high)]
    for plane in range(REACH - 1, REACH + CELLS + 1):
        rows = plane_rows(plane, 0)
        shift = -(GROUP * (LAST - plane) + 3)
        for c in range(3):
            rim_ref[c, rows, :] = jnp.where(ends, turn(joined[c], shift, 1), flow_ref[c, rows, :])
    beside = pl.ds(CELLS - 1, 2, stride=CELLS + 1)
    side_low = velocity(
        edge_stream(lpost_ref, lambda b: pl.ds(CELLS - 1 - b, 2, stride=CELLS + 1)), low_ref[SOLID, beside, :]
    )
    side_high = velocity(
        edge_stream(hpost_ref, lambda b: pl.ds(CELLS - 1 - b, 2, stride=CELLS + 1)), high_ref[SOLID, beside, :]
    )
    for c in range(3):
        joined = join(side_low[c], side_high[c])
        for k, y in enumerate((-1, CELLS)):
            rows = row_slice(REACH, y)
            spread = pltpu.roll(
                jnp.broadcast_to(joined[k : k + 1], (CELLS, LANES)),
                LANES - (GROUP * (LAST - REACH) + 3),
                1,
                stride=GROUP,
                stride_axis=0,
            )
            rim_ref[c, rows, :] = jnp.where(ends, spread, flow_ref[c, rows, :])

    own = range(REACH, REACH + CELLS)

    def here(c):
        return [rim_ref[c, plane_rows(plane, 0), :] for plane in own]

    def along_first(c):
        return [
            0.5 * (rim_ref[c, plane_rows(plane + 1, 0), :] - rim_ref[c, plane_rows(plane - 1, 0), :]) for plane in own
        ]

    def along_second(c):
        return [0.5 * (rim_ref[c, plane_rows(plane, 1), :] - rim_ref[c, plane_rows(plane, -1), :]) for plane in own]

    def along_third(c):
        low = [turn(value, 1, 1) for value in here(c)]
        high = [turn(value, -1, 1) for value in here(c)]
        out = []
        for k, plane in enumerate(own):
            base = GROUP * (LAST - plane)
            first = jnp.where(lane == 0, turn(flow_low[c], -2 - base, 1), low[k])
            second = jnp.where(lane == LANES - 1, turn(flow_high[c], -6 - base, 1), high[k])
            out.append(0.5 * (second - first))
        return out

    def minus(first, second):
        return [a - b for a, b in zip(first, second)]

    vort = (
        minus(along_second(2), along_third(1)),
        minus(along_third(0), along_first(2)),
        minus(along_first(1), along_second(0)),
    )
    s_two = jnp.concatenate([a * a + b * b + c * c for a, b, c in zip(*vort)], axis=0)
    flow_first = jnp.concatenate(here(0), axis=0)
    solid_on = p_ref[SOLID] > 0.5
    ratio = s_two / (s_two + shade_scale)
    alpha = jnp.where(solid_on, solid_alpha, alpha_top * (1.0 - jnp.exp(-s_two / shade_scale)))
    red = jnp.where(solid_on, 0.6, 0.3 + 1.5 * ratio)
    green = jnp.where(solid_on, 0.6, 1.2 - 0.9 * ratio)
    blue = jnp.where(solid_on, 0.6, 0.8 + 0.4 * jnp.tanh(20.0 * flow_first))
    logs = jnp.log1p(-alpha)
    running = logs
    wide = lanes_of(CELLS * CELLS)
    for step in (1, 2, 4, 8, 16, 32, 64):
        running = running + jnp.where(wide >= step, turn(running, step, 1), 0.0)
    weight = alpha * jnp.exp(running - logs)
    acc = jnp.zeros((CELLS, LANES), jnp.float32)
    for ch, value in enumerate((red * weight, green * weight, blue * weight, logs)):
        total = jnp.sum(value, axis=1, keepdims=True)
        for x in range(CELLS):
            acc = jnp.where(lane // UP == ch * CELLS + x, total[x * CELLS : (x + 1) * CELLS], acc)
    out_ref[...] = acc
    save.wait()


def last_kernel(slab_ref, rank_ref, out_ref):
    slabs = slab_ref[...]
    rank = rank_ref[...]
    channel = lanes_of(CELLS) // (CELLS * UP)
    logs = slabs
    for ch in range(3):
        logs = jnp.where(channel == ch, turn(slabs, (ch + 1) * CELLS * UP, 1), logs)
    front = jnp.zeros_like(slabs)
    for s in range(CELLS):
        front = front + jnp.where(rank[s : s + 1] < rank, logs[s : s + 1], 0.0)
    colour = jnp.sum(jnp.exp(front) * slabs, axis=0, keepdims=True)
    opacity = 1.0 - jnp.exp(jnp.sum(logs, axis=0, keepdims=True))
    row = jnp.where(channel[:1] == 3, opacity, colour)
    for ch in range(4):
        out_ref[ch] = jnp.broadcast_to(turn(row, -ch * CELLS * UP, 1)[:, : CELLS * UP], (UP, CELLS * UP))


def call(kernel, outs, scratch=(), first_out_hbm=False):
    shapes = tuple(jax.ShapeDtypeStruct(shape, jnp.float32) for shape in outs)
    extra = {}
    if first_out_hbm:
        spaces = [pltpu.HBM] + [pltpu.VMEM] * (len(outs) - 1)
        extra["out_specs"] = tuple(pl.BlockSpec(memory_space=space) for space in spaces)
    return pl.pallas_call(
        kernel,
        out_shape=shapes,
        scratch_shapes=scratch,
        compiler_params=pltpu.CompilerParams(vmem_limit_bytes=24 * 1024 * 1024),
        **extra,
    )


def both_ways(lo, hi, axis):
    count = lax.axis_size(axis)
    forward = [(i, (i + 1) % count) for i in range(count)]
    backward = [(target, source) for source, target in forward]
    return lax.ppermute(hi, axis, forward), lax.ppermute(lo, axis, backward)


def body(populations, solid_mask, jet_mask, visibility):
    cells = CELLS * CELLS
    f = populations.reshape(27, cells, LANES)
    masks = jnp.stack([solid_mask, jet_mask]).astype(jnp.float32).reshape(2, cells, LANES)
    x_shape = (X_COUNT, CELLS, LANES)
    post, lo, hi = call(first_kernel, ((29, cells, LANES), x_shape, x_shape))(f, masks)
    xlo, xhi = both_ways(lo, hi, "gx")
    y_shape = (Y_COUNT, LANES)
    lo, hi = call(second_kernel, (y_shape, y_shape))(post, xlo, xhi)
    ylo, yhi = both_ways(lo, hi, "gy")
    tile_shape = (29, CELLS, LANES)
    low, high = call(faces_kernel, (tile_shape, tile_shape))(post, xlo, xhi)
    half_shape = (HALF, 2 * CELLS, LANES)
    halo, low_halo, lo, hi = call(
        third_kernel, ((29, (SPAN + 1) * CELLS, LANES), tile_shape, half_shape, half_shape)
    )(ylo, yhi, low)
    zlo, zhi = both_ways(lo, hi, "gz")
    height = SPAN * ROWS + CELLS
    moved, flow, high_halo = call(
        steps_kernel,
        ((27, cells, LANES), (3, height, LANES), tile_shape),
        (pltpu.VMEM((29, height, LANES), jnp.float32), pltpu.VMEM((27, height, LANES), jnp.float32)),
    )(post, xlo, xhi, halo)
    edge = pltpu.VMEM((29, 3 * CELLS, LANES), jnp.float32)
    edge_post = pltpu.VMEM((27, 3 * CELLS, LANES), jnp.float32)
    advanced, slabs = call(
        render_kernel,
        ((27, cells, LANES), (CELLS, LANES)),
        (
            edge,
            edge,
            edge_post,
            edge_post,
            pltpu.VMEM((27, cells, LANES), jnp.float32),
            pltpu.VMEM((3, height, LANES), jnp.float32),
            pltpu.SemaphoreType.DMA,
        ),
        first_out_hbm=True,
    )(post, moved, flow, low, low_halo, high, high_halo, zlo, zhi)
    slabs = lax.all_to_all(slabs, "gz", 0, 0, tiled=True)
    rank = jnp.broadcast_to(visibility[:, None], (CELLS, LANES))
    (image,) = call(last_kernel, ((4, UP, CELLS * UP),))(slabs, rank)
    return advanced.reshape(27, CELLS, CELLS, LANES), jnp.swapaxes(image, 1, 2)


def solution(mesh):
    return jax.shard_map(
        body,
        mesh=mesh,
        in_specs=(P(None, "gx", "gy", "gz"), P("gx", "gy", "gz"), P("gx", "gy", "gz"), P()),
        out_specs=(P(None, "gx", "gy", "gz"), P(None, "gx", ("gy", "gz"))),
        check_vma=False,
    )
```

time: 68.6 us -> 63.3 us (0.923)
  waiting for transfers between devices: 16.7 us -> 13.4 us
  local copies, waits for them, and re-layouts: 2.75 us -> 1.24 us
  other arithmetic: 0 us -> 0.78 us
    ppermute x6, waiting for transfers between devices: 16.7 us -> 13.4 us  [both_ways(): return (lax.ppermute(hi, axis, forward), lax.ppermute(lo, axis, backward))]
    unnamed x8 -> x4, local copies, waits for them, and re-layouts: 2.68 us -> 1.17 us
    convert_element_type x0 -> x1, other arithmetic: none -> 0.78 us  [body(): jnp.stack([solid_mask, jet_mask]).astype(jnp.float32)]
  transfers between devices with their start and end apart: 6 -> 6, of which waited for: 5 -> 4; matrix products, arithmetic and copies ran while one was open for 0% -> 0% of each run, Pallas kernels for 1% -> 6%
where the time goes in v3:
time: 63.3 us; the launch traced here: 62.9 us
  starting transfers between devices  29.7 us (47%)
  waiting for transfers between devices  13.4 us (21%)
  blocking collectives  8.68 us (14%)
  Pallas kernels  8.41 us (13%)
  local copies, waits for them, and re-layouts  1.24 us (2%)
  other arithmetic  0.78 us (1%)
  between operations  0.74 us (1%)
    ppermute x6, starting transfers between devices, both_ways(): return (lax.ppermute(hi, axis, forward), lax.ppermute(lo, axis, backward))  29.7 us
    ppermute x6, waiting for transfers between devices, both_ways(): return (lax.ppermute(hi, axis, forward), lax.ppermute(lo, axis, backward))  13.4 us
    all_to_all x1, blocking collectives, body(): slabs = lax.all_to_all(slabs, 'gz', 0, 0, tiled=True)  8.68 us
    pallas_call x1, Pallas kernels, body(): call(steps_kernel, ((27, cells, LANES), (3, height, LANES), tile_shape),...  3.13 us
    pallas_call x1, Pallas kernels, body(): call(render_kernel, ((27, cells, LANES), (CELLS, LANES)), (edge, edge, ed...  2.36 us
  transfers between devices with their start and end apart: 6, of which 4 were waited for; matrix products, arithmetic and copies ran while one was open for 0% of the time, Pallas kernels for 6%

profile of v3, /device:TPU:24, one launch (start us, length us, event | category | flops | bytes accessed | tf_op | source)
XLA Modules:
  0.0 62.9 jit_solution(1162873468820864812)
XLA Ops:
  0.6 0.8 %add_convert_fusion.mask_ref = f32[2,64,128]{2,1,0:T(8,128)S(1)} fusion(s32[1,64,128]{2,1,0:T(8,128)} %bitcast.12, s32[1,64,128]{2,1,0:T(8,128)} %bitcast.13), kind=kLoop, calls=%fused_computation | loop fusion | flops 32768 | bytes 131072 | tf_op jit(solution)/shard_map/convert_element_type | solution.py:487
  1.4 0.0 copy-start
  1.4 1.2 %copy-done = f32[27,8,8,128]{3,2,1,0:T(8,128)S(1)} copy-done((f32[27,8,8,128]{3,2,1,0:T(8,128)S(1)}, f32[27,8,8,128]{3,2,1,0:T(8,128)}, u32[]{:S(2)}) %copy-start) | copy-done | bytes 884760
  2.6 0.4 shard_map.59
  3.0 4.7 %collective-permute-start = (f32[58,8,128]{2,1,0:T(8,128)S(1)}, f32[58,8,128]{2,1,0:T(8,128)S(1)}, u32[]{:S(2)}, u32[]{:S(2)}) collective-permute-start(f32[58,8,128]{2,1,0:T(8,128)S(1)} %get-tuple-element.19), channel_id=1, source_target_pairs={{0,128},{128,256},{256,384},{384,512},{512,640},{640,768},{768,896... | collective-permute-start | bytes 712712 | tf_op jit(solution)/shard_map/ppermute | solution.py:481
  7.7 1.9 %collective-permute-start.1 = (f32[58,8,128]{2,1,0:T(8,128)S(1)}, f32[58,8,128]{2,1,0:T(8,128)S(1)}, u32[]{:S(2)}, u32[]{:S(2)}) collective-permute-start(f32[58,8,128]{2,1,0:T(8,128)S(1)} %get-tuple-element.20), channel_id=1, source_target_pairs={{128,0},{256,128},{384,256},{512,384},{640,512},{768,640},{896,768... | collective-permute-start | bytes 712712 | tf_op jit(solution)/shard_map/ppermute | solution.py:481
  9.6 3.1 %collective-permute-done.xlo_ref = f32[58,8,128]{2,1,0:T(8,128)S(1)} collective-permute-done((f32[58,8,128]{2,1,0:T(8,128)S(1)}, f32[58,8,128]{2,1,0:T(8,128)S(1)}, u32[]{:S(2)}, u32[]{:S(2)}) %collective-permute-start) | collective-permute-done | bytes 237600 | tf_op jit(solution)/shard_map/ppermute | solution.py:481
  12.7 5.3 %collective-permute-done.1.xhi_ref = f32[58,8,128]{2,1,0:T(8,128)S(1)} collective-permute-done((f32[58,8,128]{2,1,0:T(8,128)S(1)}, f32[58,8,128]{2,1,0:T(8,128)S(1)}, u32[]{:S(2)}, u32[]{:S(2)}) %collective-permute-start.1) | collective-permute-done | bytes 237600 | tf_op jit(solution)/shard_map/ppermute | solution.py:481
  18.0 0.2 shard_map.60
  18.2 4.3 %collective-permute-start.2 = (f32[640,128]{1,0:T(8,128)S(1)}, f32[640,128]{1,0:T(8,128)S(1)}, u32[]{:S(2)}, u32[]{:S(2)}) collective-permute-start(f32[640,128]{1,0:T(8,128)S(1)} %get-tuple-element.21), channel_id=1, source_target_pairs={{0,8},{8,16},{16,24},{24,32},{32,40},{40,48},{48,56},{56,64},{64,7... | collective-permute-start | bytes 983048 | tf_op jit(solution)/shard_map/ppermute | solution.py:481
  22.5 15.9 %collective-permute-start.3 = (f32[640,128]{1,0:T(8,128)S(1)}, f32[640,128]{1,0:T(8,128)S(1)}, u32[]{:S(2)}, u32[]{:S(2)}) collective-permute-start(f32[640,128]{1,0:T(8,128)S(1)} %get-tuple-element.22), channel_id=1, source_target_pairs={{8,0},{16,8},{24,16},{32,24},{40,32},{48,40},{56,48},{64,56},{72,6... | collective-permute-start | bytes 983048 | tf_op jit(solution)/shard_map/ppermute | solution.py:481
  38.4 0.8 %shard_map.61 = (f32[29,8,128]{2,1,0:T(8,128)S(1)}, f32[29,8,128]{2,1,0:T(8,128)S(1)}) custom-call(f32[29,64,128]{2,1,0:T(8,128)S(1)} %get-tuple-element.18.p_ref, f32[58,8,128]{2,1,0:T(8,128)S(1)} %collective-permute-done.xlo_ref, f32[58,8,128]{2,1,0:T(8,128)S(1)} %collective-permute-done.1.xhi_ref), custom_call_target="tpu_custom_call" | custom-call | tf_op jit(solution)/shard_map/pallas_call | solution.py:495
  39.2 3.8 %collective-permute-done.2.ylo_ref = f32[640,128]{1,0:T(8,128)S(1)} collective-permute-done((f32[640,128]{1,0:T(8,128)S(1)}, f32[640,128]{1,0:T(8,128)S(1)}, u32[]{:S(2)}, u32[]{:S(2)}) %collective-permute-start.2) | collective-permute-done | bytes 327712 | tf_op jit(solution)/shard_map/ppermute | solution.py:481
  43.0 1.2 %collective-permute-done.3.yhi_ref = f32[640,128]{1,0:T(8,128)S(1)} collective-permute-done((f32[640,128]{1,0:T(8,128)S(1)}, f32[640,128]{1,0:T(8,128)S(1)}, u32[]{:S(2)}, u32[]{:S(2)}) %collective-permute-start.3) | collective-permute-done | bytes 327712 | tf_op jit(solution)/shard_map/ppermute | solution.py:481
  44.2 0.7 %shard_map.62 = (f32[29,120,128]{2,1,0:T(8,128)S(1)}, f32[29,8,128]{2,1,0:T(8,128)S(1)}, f32[15,16,128]{2,1,0:T(8,128)S(1)}, f32[15,16,128]{2,1,0:T(8,128)S(1)}) custom-call(f32[640,128]{1,0:T(8,128)S(1)} %collective-permute-done.2.ylo_ref, f32[640,128]{1,0:T(8,128)S(1)} %collective-permute-done.3.yhi_ref, f32[29,8,128]{2,1,0:T(8,128)S(1)} %get-tuple-element.23.main_ref.lmain_ref), custom_call_target="tpu_custom_call" | custom-call | tf_op jit(solution)/shard_map/pallas_call | solution.py:497
  44.9 0.0 collective-permute-start.4
  44.9 2.9 %collective-permute-start.5 = (f32[15,16,128]{2,1,0:T(8,128)S(1)}, f32[15,16,128]{2,1,0:T(8,128)S(1)}, u32[]{:S(2)}, u32[]{:S(2)}) collective-permute-start(f32[15,16,128]{2,1,0:T(8,128)S(1)} %get-tuple-element.31), channel_id=1, source_target_pairs={{1,0},{2,1},{3,2},{4,3},{5,4},{6,5},{7,6},{0,7},{9,8},{10,9},{11,1... | collective-permute-start | bytes 368648 | tf_op jit(solution)/shard_map/ppermute | solution.py:481
  47.9 3.1 %shard_map.63 = (f32[27,64,128]{2,1,0:T(8,128)S(1)}, f32[3,232,128]{2,1,0:T(8,128)S(1)}, f32[29,8,128]{2,1,0:T(8,128)S(1)}) custom-call(f32[29,64,128]{2,1,0:T(8,128)S(1)} %get-tuple-element.18.p_ref, f32[58,8,128]{2,1,0:T(8,128)S(1)} %collective-permute-done.xlo_ref, f32[58,8,128]{2,1,0:T(8,128)S(1)} %collective-permute-done.1.xhi_ref, ...), custom_call_target="tpu_custom_call" | custom-call | tf_op jit(solution)/shard_map/pallas_call | solution.py:502
  51.0 0.0 copy-start.1
  51.0 0.0 collective-permute-done.4.zlo_ref
  51.0 0.0 collective-permute-done.5.zhi_ref
  51.0 2.4 %shard_map.64 = (f32[27,64,128]{2,1,0:T(8,128)}, f32[8,128]{1,0:T(8,128)S(1)}) custom-call(f32[29,64,128]{2,1,0:T(8,128)S(1)} %get-tuple-element.18.p_ref, f32[27,64,128]{2,1,0:T(8,128)S(1)} %get-tuple-element.25.adv_ref, f32[3,232,128]{2,1,0:T(8,128)S(1)} %get-tuple-element.26.flow_ref, f32[29,8,128]{2,1,0:T(8,128)S(1)} %get-tuple-element.23.main_ref.lmain_ref, ...), custom_call_target="tpu_custom_call" | custom-call | tf_op jit(solution)/shard_map/pallas_call | solution.py:509
  53.4 8.7 %all_to_all.11 = f32[8,1,128]{2,1,0:T(1,128)S(1)} all-to-all(f32[8,1,128]{2,1,0:T(1,128)S(1)} %bitcast.11), channel_id=1, replica_groups=mesh['gx'=8,'gy'=16,'gz'=8] {'gz'}, dimensions={0} | all-to-all | bytes 8192 | tf_op jit(solution)/shard_map/all_to_all | solution.py:523
  62.1 0.0 copy-done.1
  62.1 0.1 broadcast_in_dim.2.rank_ref
  62.2 0.8 %shard_map.65 = f32[4,4,32]{2,1,0:T(4,128)} custom-call(f32[8,128]{1,0:T(8,128)S(1)} %bitcast.10, s32[8,128]{1,0:T(8,128)S(1)} %broadcast_in_dim.2.rank_ref), custom_call_target="tpu_custom_call" | custom-call | tf_op jit(solution)/shard_map/pallas_call | solution.py:525
Async XLA Ops:
  1.4 1.2 %copy-start = (f32[27,8,8,128]{3,2,1,0:T(8,128)S(1)}, f32[27,8,8,128]{3,2,1,0:T(8,128)}, u32[]{:S(2)}) copy-start(f32[27,8,8,128]{3,2,1,0:T(8,128)} %param.4) | copy-start | bytes 2654212
  3.0 9.7 %collective-permute-start = (f32[58,8,128]{2,1,0:T(8,128)S(1)}, f32[58,8,128]{2,1,0:T(8,128)S(1)}, u32[]{:S(2)}, u32[]{:S(2)}) collective-permute-start(f32[58,8,128]{2,1,0:T(8,128)S(1)} %get-tuple-element.19), channel_id=1, source_target_pairs={{0,128},{128,256},{256,384},{384,512},{512,640},{640,768},{768,896... | collective-permute-start | bytes 712712 | tf_op jit(solution)/shard_map/ppermute | solution.py:481
  7.7 10.3 %collective-permute-start.1 = (f32[58,8,128]{2,1,0:T(8,128)S(1)}, f32[58,8,128]{2,1,0:T(8,128)S(1)}, u32[]{:S(2)}, u32[]{:S(2)}) collective-permute-start(f32[58,8,128]{2,1,0:T(8,128)S(1)} %get-tuple-element.20), channel_id=1, source_target_pairs={{128,0},{256,128},{384,256},{512,384},{640,512},{768,640},{896,768... | collective-permute-start | bytes 712712 | tf_op jit(solution)/shard_map/ppermute | solution.py:481
  18.2 24.7 %collective-permute-start.2 = (f32[640,128]{1,0:T(8,128)S(1)}, f32[640,128]{1,0:T(8,128)S(1)}, u32[]{:S(2)}, u32[]{:S(2)}) collective-permute-start(f32[640,128]{1,0:T(8,128)S(1)} %get-tuple-element.21), channel_id=1, source_target_pairs={{0,8},{8,16},{16,24},{24,32},{32,40},{40,48},{48,56},{56,64},{64,7... | collective-permute-start | bytes 983048 | tf_op jit(solution)/shard_map/ppermute | solution.py:481
  22.5 21.6 %collective-permute-start.3 = (f32[640,128]{1,0:T(8,128)S(1)}, f32[640,128]{1,0:T(8,128)S(1)}, u32[]{:S(2)}, u32[]{:S(2)}) collective-permute-start(f32[640,128]{1,0:T(8,128)S(1)} %get-tuple-element.22), channel_id=1, source_target_pairs={{8,0},{16,8},{24,16},{32,24},{40,32},{48,40},{56,48},{64,56},{72,6... | collective-permute-start | bytes 983048 | tf_op jit(solution)/shard_map/ppermute | solution.py:481
  44.9 6.1 %collective-permute-start.4 = (f32[15,16,128]{2,1,0:T(8,128)S(1)}, f32[15,16,128]{2,1,0:T(8,128)S(1)}, u32[]{:S(2)}, u32[]{:S(2)}) collective-permute-start(f32[15,16,128]{2,1,0:T(8,128)S(1)} %get-tuple-element.30), channel_id=1, source_target_pairs={{0,1},{1,2},{2,3},{3,4},{4,5},{5,6},{6,7},{7,0},{8,9},{9,10},{10,1... | collective-permute-start | bytes 368648 | tf_op jit(solution)/shard_map/ppermute | solution.py:481
  44.9 6.1 %collective-permute-start.5 = (f32[15,16,128]{2,1,0:T(8,128)S(1)}, f32[15,16,128]{2,1,0:T(8,128)S(1)}, u32[]{:S(2)}, u32[]{:S(2)}) collective-permute-start(f32[15,16,128]{2,1,0:T(8,128)S(1)} %get-tuple-element.31), channel_id=1, source_target_pairs={{1,0},{2,1},{3,2},{4,3},{5,4},{6,5},{7,6},{0,7},{9,8},{10,9},{11,1... | collective-permute-start | bytes 368648 | tf_op jit(solution)/shard_map/ppermute | solution.py:481
  51.0 11.1 %copy-start.1 = (s32[8]{0:T(128)S(1)}, s32[8]{0:T(128)}, u32[]{:S(2)}) copy-start(s32[8]{0:T(128)} %param.7) | copy-start | bytes 100

commit v4 on v3

--- a/solution.py
+++ b/solution.py
@@ -56,7 +56,7 @@
 
 X_COUNT = len(axis_list(0, 1))
 Y_OWN = len(axis_list(1, 1)) * CELLS
-Y_COUNT = Y_OWN + -(-len(corner_list(1)) // 8) * 8
+Y_CORNER = -(-len(corner_list(1)) // 8) * 8
 
 
 def moments(f):
@@ -121,7 +121,7 @@
     return pltpu.roll(value, shift, axis)
 
 
-def first_kernel(f_ref, mask_ref, p_ref, lo_ref, hi_ref):
+def first_kernel(f_ref, mask_ref, p_ref, lo_ref, hi_ref, ylo_ref, yhi_ref):
     for k, key in enumerate(MASKS):
         p_ref[key] = mask_ref[k]
     for x in range(CELLS):
@@ -134,6 +134,10 @@
         lo_ref[k] = p_ref[key, pl.ds((dist - 1) * CELLS, CELLS), :]
     for k, (key, dist) in enumerate(axis_list(0, 1)):
         hi_ref[k] = p_ref[key, pl.ds((CELLS - dist) * CELLS, CELLS), :]
+    for inward, out_ref in ((-1, ylo_ref), (1, yhi_ref)):
+        for k, (key, dist) in enumerate(axis_list(1, inward)):
+            row = dist - 1 if inward < 0 else CELLS - dist
+            out_ref[pl.ds(k * CELLS, CELLS), :] = p_ref[key, pl.ds(row, CELLS, stride=CELLS), :]
 
 
 LOW_AT = {entry: k for k, entry in enumerate(axis_list(0, 1))}
@@ -148,14 +152,11 @@
     return p_ref.at[key, pl.ds(x * CELLS, CELLS), :]
 
 
-def second_kernel(p_ref, xlo_ref, xhi_ref, lo_ref, hi_ref):
+def second_kernel(xlo_ref, xhi_ref, lo_ref, hi_ref):
     for inward, out_ref in ((-1, lo_ref), (1, hi_ref)):
-        for k, (key, dist) in enumerate(axis_list(1, inward)):
-            row = dist - 1 if inward < 0 else CELLS - dist
-            out_ref[pl.ds(k * CELLS, CELLS), :] = p_ref[key, pl.ds(row, CELLS, stride=CELLS), :]
         for k, (key, dist, x) in enumerate(corner_list(inward)):
             row = dist - 1 if inward < 0 else CELLS - dist
-            out_ref[pl.ds(Y_OWN + k, 1), :] = plane_ref(key, x, p_ref, xlo_ref, xhi_ref)[pl.ds(row, 1), :]
+            out_ref[pl.ds(k, 1), :] = plane_ref(key, x, None, xlo_ref, xhi_ref)[pl.ds(row, 1), :]
 
 
 def pack(tiles):
@@ -197,15 +198,15 @@
     return [jnp.where(upper, turn(value, GROUP, 1), value) for value in pack(tiles)]
 
 
-def third_kernel(ylo_ref, yhi_ref, main_ref, h_ref, z_ref, lo_ref, hi_ref):
-    for inward, in_ref in ((1, ylo_ref), (-1, yhi_ref)):
+def third_kernel(ylo_ref, yhi_ref, clo_ref, chi_ref, main_ref, h_ref, z_ref, lo_ref, hi_ref):
+    for inward, in_ref, corner_ref in ((1, ylo_ref, clo_ref), (-1, yhi_ref, chi_ref)):
         for k, (key, dist) in enumerate(axis_list(1, inward)):
             start = CELLS * REACH + CELLS - dist if inward > 0 else CELLS * (REACH + 1) + dist - 1
             h_ref[key, pl.ds(start, CELLS, stride=CELLS), :] = in_ref[pl.ds(k * CELLS, CELLS), :]
         for k, (key, dist, x) in enumerate(corner_list(inward)):
             plane = x + REACH
             row = CELLS * plane + CELLS - dist if inward > 0 else CELLS * (plane + 1) + dist - 1
-            h_ref[key, pl.ds(row, 1), :] = in_ref[pl.ds(Y_OWN + k, 1), :]
+            h_ref[key, pl.ds(row, 1), :] = corner_ref[pl.ds(k, 1), :]
     halo = pack_halo(h_ref, 3)
     early = lanes_of(CELLS) % GROUP < REACH
     for key in range(29):
@@ -486,17 +487,19 @@
     f = populations.reshape(27, cells, LANES)
     masks = jnp.stack([solid_mask, jet_mask]).astype(jnp.float32).reshape(2, cells, LANES)
     x_shape = (X_COUNT, CELLS, LANES)
-    post, lo, hi = call(first_kernel, ((29, cells, LANES), x_shape, x_shape))(f, masks)
+    y_shape = (Y_OWN, LANES)
+    post, lo, hi, down, up = call(first_kernel, ((29, cells, LANES), x_shape, x_shape, y_shape, y_shape))(f, masks)
     xlo, xhi = both_ways(lo, hi, "gx")
-    y_shape = (Y_COUNT, LANES)
-    lo, hi = call(second_kernel, (y_shape, y_shape))(post, xlo, xhi)
-    ylo, yhi = both_ways(lo, hi, "gy")
+    ylo, yhi = both_ways(down, up, "gy")
+    corner_shape = (Y_CORNER, LANES)
+    lo, hi = call(second_kernel, (corner_shape, corner_shape))(xlo, xhi)
+    clo, chi = both_ways(lo, hi, "gy")
     tile_shape = (29, CELLS, LANES)
     low, high = call(faces_kernel, (tile_shape, tile_shape))(post, xlo, xhi)
     half_shape = (HALF, 2 * CELLS, LANES)
     halo, low_halo, lo, hi = call(
         third_kernel, ((29, (SPAN + 1) * CELLS, LANES), tile_shape, half_shape, half_shape)
-    )(ylo, yhi, low)
+    )(ylo, yhi, clo, chi, low)
     zlo, zhi = both_ways(lo, hi, "gz")
     height = SPAN * ROWS + CELLS
     moved, flow, high_halo = call(

time: 63.3 us -> 59.9 us (0.946)
  the two profiles are of different devices: /device:TPU:24 before, /device:TPU:1 now
where the time goes in v4:
time: 59.9 us; the launch traced here: 59.5 us
  starting transfers between devices  37.7 us (63%)
  blocking collectives  8.71 us (15%)
  Pallas kernels  8.42 us (14%)
  waiting for transfers between devices  1.84 us (3%)
  local copies, waits for them, and re-layouts  1.24 us (2%)
  other arithmetic  0.78 us (1%)
  between operations  0.78 us (1%)
    ppermute x8, starting transfers between devices, both_ways(): return (lax.ppermute(hi, axis, forward), lax.ppermute(lo, axis, backward))  37.7 us
    all_to_all x1, blocking collectives, body(): slabs = lax.all_to_all(slabs, 'gz', 0, 0, tiled=True)  8.71 us
    pallas_call x1, Pallas kernels, body(): call(steps_kernel, ((27, cells, LANES), (3, height, LANES), tile_shape),...  3.13 us
    pallas_call x1, Pallas kernels, body(): call(render_kernel, ((27, cells, LANES), (CELLS, LANES)), (edge, edge, ed...  2.36 us
    ppermute x8, waiting for transfers between devices, both_ways(): return (lax.ppermute(hi, axis, forward), lax.ppermute(lo, axis, backward))  1.84 us
  transfers between devices with their start and end apart: 8, of which 2 were waited for; matrix products, arithmetic and copies ran while one was open for 0% of the time, Pallas kernels for 7%

profile of v4, /device:TPU:1, one launch (start us, length us, event | category | flops | bytes accessed | tf_op | source)
XLA Modules:
  0.0 59.5 jit_solution(4295022904032083190)
XLA Ops:
  0.6 0.8 %add_convert_fusion.mask_ref = f32[2,64,128]{2,1,0:T(8,128)S(1)} fusion(s32[1,64,128]{2,1,0:T(8,128)} %bitcast.12, s32[1,64,128]{2,1,0:T(8,128)} %bitcast.13), kind=kLoop, calls=%fused_computation | loop fusion | flops 32768 | bytes 131072 | tf_op jit(solution)/shard_map/convert_element_type | solution.py:488
  1.4 0.0 copy-start
  1.4 1.2 %copy-done = f32[27,8,8,128]{3,2,1,0:T(8,128)S(1)} copy-done((f32[27,8,8,128]{3,2,1,0:T(8,128)S(1)}, f32[27,8,8,128]{3,2,1,0:T(8,128)}, u32[]{:S(2)}) %copy-start) | copy-done | bytes 884760
  2.6 0.5 shard_map.59
  3.0 4.0 %collective-permute-start = (f32[58,8,128]{2,1,0:T(8,128)S(1)}, f32[58,8,128]{2,1,0:T(8,128)S(1)}, u32[]{:S(2)}, u32[]{:S(2)}) collective-permute-start(f32[58,8,128]{2,1,0:T(8,128)S(1)} %get-tuple-element.21), channel_id=1, source_target_pairs={{0,128},{128,256},{256,384},{384,512},{512,640},{640,768},{768,896... | collective-permute-start | bytes 712712 | tf_op jit(solution)/shard_map/ppermute | solution.py:482
  7.1 3.8 %collective-permute-start.1 = (f32[58,8,128]{2,1,0:T(8,128)S(1)}, f32[58,8,128]{2,1,0:T(8,128)S(1)}, u32[]{:S(2)}, u32[]{:S(2)}) collective-permute-start(f32[58,8,128]{2,1,0:T(8,128)S(1)} %get-tuple-element.22), channel_id=1, source_target_pairs={{128,0},{256,128},{384,256},{512,384},{640,512},{768,640},{896,768... | collective-permute-start | bytes 712712 | tf_op jit(solution)/shard_map/ppermute | solution.py:482
  10.9 4.0 %collective-permute-start.2 = (f32[464,128]{1,0:T(8,128)S(1)}, f32[464,128]{1,0:T(8,128)S(1)}, u32[]{:S(2)}, u32[]{:S(2)}) collective-permute-start(f32[464,128]{1,0:T(8,128)S(1)} %get-tuple-element.23), channel_id=1, source_target_pairs={{0,8},{8,16},{16,24},{24,32},{32,40},{40,48},{48,56},{56,64},{64,7... | collective-permute-start | bytes 712712 | tf_op jit(solution)/shard_map/ppermute | solution.py:482
  14.9 15.9 %collective-permute-start.3 = (f32[464,128]{1,0:T(8,128)S(1)}, f32[464,128]{1,0:T(8,128)S(1)}, u32[]{:S(2)}, u32[]{:S(2)}) collective-permute-start(f32[464,128]{1,0:T(8,128)S(1)} %get-tuple-element.24), channel_id=1, source_target_pairs={{8,0},{16,8},{24,16},{32,24},{40,32},{48,40},{56,48},{64,56},{72,6... | collective-permute-start | bytes 712712 | tf_op jit(solution)/shard_map/ppermute | solution.py:482
  30.8 0.0 collective-permute-done.xlo_ref
  30.8 0.0 collective-permute-done.1.xhi_ref
  30.8 0.1 shard_map.60
  30.9 1.9 %collective-permute-start.4 = (f32[176,128]{1,0:T(8,128)S(1)}, f32[176,128]{1,0:T(8,128)S(1)}, u32[]{:S(2)}, u32[]{:S(2)}) collective-permute-start(f32[176,128]{1,0:T(8,128)S(1)} %get-tuple-element.25), channel_id=1, source_target_pairs={{0,8},{8,16},{16,24},{24,32},{32,40},{40,48},{48,56},{56,64},{64,7... | collective-permute-start | bytes 270344 | tf_op jit(solution)/shard_map/ppermute | solution.py:482
  32.9 4.6 %collective-permute-start.5 = (f32[176,128]{1,0:T(8,128)S(1)}, f32[176,128]{1,0:T(8,128)S(1)}, u32[]{:S(2)}, u32[]{:S(2)}) collective-permute-start(f32[176,128]{1,0:T(8,128)S(1)} %get-tuple-element.26), channel_id=1, source_target_pairs={{8,0},{16,8},{24,16},{32,24},{40,32},{48,40},{56,48},{64,56},{72,6... | collective-permute-start | bytes 270344 | tf_op jit(solution)/shard_map/ppermute | solution.py:482
  37.5 0.8 %shard_map.61 = (f32[29,8,128]{2,1,0:T(8,128)S(1)}, f32[29,8,128]{2,1,0:T(8,128)S(1)}) custom-call(f32[29,64,128]{2,1,0:T(8,128)S(1)} %get-tuple-element.20.p_ref, f32[58,8,128]{2,1,0:T(8,128)S(1)} %collective-permute-done.xlo_ref, f32[58,8,128]{2,1,0:T(8,128)S(1)} %collective-permute-done.1.xhi_ref), custom_call_target="tpu_custom_call" | custom-call | tf_op jit(solution)/shard_map/pallas_call | solution.py:498
  38.3 0.0 collective-permute-done.2.ylo_ref
  38.3 0.0 collective-permute-done.3.yhi_ref
  38.3 0.0 collective-permute-done.4.clo_ref
  38.3 0.7 %collective-permute-done.5.chi_ref = f32[176,128]{1,0:T(8,128)S(1)} collective-permute-done((f32[176,128]{1,0:T(8,128)S(1)}, f32[176,128]{1,0:T(8,128)S(1)}, u32[]{:S(2)}, u32[]{:S(2)}) %collective-permute-start.5) | collective-permute-done | bytes 90144 | tf_op jit(solution)/shard_map/ppermute | solution.py:482
  39.0 0.8 %shard_map.62 = (f32[29,120,128]{2,1,0:T(8,128)S(1)}, f32[29,8,128]{2,1,0:T(8,128)S(1)}, f32[15,16,128]{2,1,0:T(8,128)S(1)}, f32[15,16,128]{2,1,0:T(8,128)S(1)}) custom-call(f32[464,128]{1,0:T(8,128)S(1)} %collective-permute-done.2.ylo_ref, f32[464,128]{1,0:T(8,128)S(1)} %collective-permute-done.3.yhi_ref, f32[176,128]{1,0:T(8,128)S(1)} %collective-permute-done.4.clo_ref, ...), custom_call_target="tpu_custom_call" | custom-call | tf_op jit(solution)/shard_map/pallas_call | solution.py:500
  39.8 3.5 %collective-permute-start.6 = (f32[15,16,128]{2,1,0:T(8,128)S(1)}, f32[15,16,128]{2,1,0:T(8,128)S(1)}, u32[]{:S(2)}, u32[]{:S(2)}) collective-permute-start(f32[15,16,128]{2,1,0:T(8,128)S(1)} %get-tuple-element.34), channel_id=1, source_target_pairs={{0,1},{1,2},{2,3},{3,4},{4,5},{5,6},{6,7},{7,0},{8,9},{9,10},{10,1... | collective-permute-start | bytes 368648 | tf_op jit(solution)/shard_map/ppermute | solution.py:482
  43.2 0.0 collective-permute-start.7
  43.2 3.1 %shard_map.63 = (f32[27,64,128]{2,1,0:T(8,128)S(1)}, f32[3,232,128]{2,1,0:T(8,128)S(1)}, f32[29,8,128]{2,1,0:T(8,128)S(1)}) custom-call(f32[29,64,128]{2,1,0:T(8,128)S(1)} %get-tuple-element.20.p_ref, f32[58,8,128]{2,1,0:T(8,128)S(1)} %collective-permute-done.xlo_ref, f32[58,8,128]{2,1,0:T(8,128)S(1)} %collective-permute-done.1.xhi_ref, ...), custom_call_target="tpu_custom_call" | custom-call | tf_op jit(solution)/shard_map/pallas_call | solution.py:505
  46.4 0.0 copy-start.1
  46.4 0.0 collective-permute-done.6.zlo_ref
  46.4 1.1 %collective-permute-done.7.zhi_ref = f32[15,16,128]{2,1,0:T(8,128)S(1)} collective-permute-done((f32[15,16,128]{2,1,0:T(8,128)S(1)}, f32[15,16,128]{2,1,0:T(8,128)S(1)}, u32[]{:S(2)}, u32[]{:S(2)}) %collective-permute-start.7) | collective-permute-done | bytes 122912 | tf_op jit(solution)/shard_map/ppermute | solution.py:482
  47.5 2.4 %shard_map.64 = (f32[27,64,128]{2,1,0:T(8,128)}, f32[8,128]{1,0:T(8,128)S(1)}) custom-call(f32[29,64,128]{2,1,0:T(8,128)S(1)} %get-tuple-element.20.p_ref, f32[27,64,128]{2,1,0:T(8,128)S(1)} %get-tuple-element.29.adv_ref, f32[3,232,128]{2,1,0:T(8,128)S(1)} %get-tuple-element.30.flow_ref, f32[29,8,128]{2,1,0:T(8,128)S(1)} %get-tuple-element.27.main_ref.lmain_ref, ...), custom_call_target="tpu_custom_call" | custom-call | tf_op jit(solution)/shard_map/pallas_call | solution.py:512
  49.9 8.7 %all_to_all.11 = f32[8,1,128]{2,1,0:T(1,128)S(1)} all-to-all(f32[8,1,128]{2,1,0:T(1,128)S(1)} %bitcast.11), channel_id=1, replica_groups=mesh['gx'=8,'gy'=16,'gz'=8] {'gz'}, dimensions={0} | all-to-all | bytes 8192 | tf_op jit(solution)/shard_map/all_to_all | solution.py:526
  58.6 0.0 copy-done.1
  58.6 0.1 broadcast_in_dim.2.rank_ref
  58.7 0.8 %shard_map.65 = f32[4,4,32]{2,1,0:T(4,128)} custom-call(f32[8,128]{1,0:T(8,128)S(1)} %bitcast.10, s32[8,128]{1,0:T(8,128)S(1)} %broadcast_in_dim.2.rank_ref), custom_call_target="tpu_custom_call" | custom-call | tf_op jit(solution)/shard_map/pallas_call | solution.py:528
Async XLA Ops:
  1.4 1.2 %copy-start = (f32[27,8,8,128]{3,2,1,0:T(8,128)S(1)}, f32[27,8,8,128]{3,2,1,0:T(8,128)}, u32[]{:S(2)}) copy-start(f32[27,8,8,128]{3,2,1,0:T(8,128)} %param.4) | copy-start | bytes 2654212
  3.0 27.7 %collective-permute-start = (f32[58,8,128]{2,1,0:T(8,128)S(1)}, f32[58,8,128]{2,1,0:T(8,128)S(1)}, u32[]{:S(2)}, u32[]{:S(2)}) collective-permute-start(f32[58,8,128]{2,1,0:T(8,128)S(1)} %get-tuple-element.21), channel_id=1, source_target_pairs={{0,128},{128,256},{256,384},{384,512},{512,640},{640,768},{768,896... | collective-permute-start | bytes 712712 | tf_op jit(solution)/shard_map/ppermute | solution.py:482
  7.1 23.7 %collective-permute-start.1 = (f32[58,8,128]{2,1,0:T(8,128)S(1)}, f32[58,8,128]{2,1,0:T(8,128)S(1)}, u32[]{:S(2)}, u32[]{:S(2)}) collective-permute-start(f32[58,8,128]{2,1,0:T(8,128)S(1)} %get-tuple-element.22), channel_id=1, source_target_pairs={{128,0},{256,128},{384,256},{512,384},{640,512},{768,640},{896,768... | collective-permute-start | bytes 712712 | tf_op jit(solution)/shard_map/ppermute | solution.py:482
  10.9 27.4 %collective-permute-start.2 = (f32[464,128]{1,0:T(8,128)S(1)}, f32[464,128]{1,0:T(8,128)S(1)}, u32[]{:S(2)}, u32[]{:S(2)}) collective-permute-start(f32[464,128]{1,0:T(8,128)S(1)} %get-tuple-element.23), channel_id=1, source_target_pairs={{0,8},{8,16},{16,24},{24,32},{32,40},{40,48},{48,56},{56,64},{64,7... | collective-permute-start | bytes 712712 | tf_op jit(solution)/shard_map/ppermute | solution.py:482
  14.9 23.4 %collective-permute-start.3 = (f32[464,128]{1,0:T(8,128)S(1)}, f32[464,128]{1,0:T(8,128)S(1)}, u32[]{:S(2)}, u32[]{:S(2)}) collective-permute-start(f32[464,128]{1,0:T(8,128)S(1)} %get-tuple-element.24), channel_id=1, source_target_pairs={{8,0},{16,8},{24,16},{32,24},{40,32},{48,40},{56,48},{64,56},{72,6... | collective-permute-start | bytes 712712 | tf_op jit(solution)/shard_map/ppermute | solution.py:482
  30.9 7.4 %collective-permute-start.4 = (f32[176,128]{1,0:T(8,128)S(1)}, f32[176,128]{1,0:T(8,128)S(1)}, u32[]{:S(2)}, u32[]{:S(2)}) collective-permute-start(f32[176,128]{1,0:T(8,128)S(1)} %get-tuple-element.25), channel_id=1, source_target_pairs={{0,8},{8,16},{16,24},{24,32},{32,40},{40,48},{48,56},{56,64},{64,7... | collective-permute-start | bytes 270344 | tf_op jit(solution)/shard_map/ppermute | solution.py:482
  32.9 6.1 %collective-permute-start.5 = (f32[176,128]{1,0:T(8,128)S(1)}, f32[176,128]{1,0:T(8,128)S(1)}, u32[]{:S(2)}, u32[]{:S(2)}) collective-permute-start(f32[176,128]{1,0:T(8,128)S(1)} %get-tuple-element.26), channel_id=1, source_target_pairs={{8,0},{16,8},{24,16},{32,24},{40,32},{48,40},{56,48},{64,56},{72,6... | collective-permute-start | bytes 270344 | tf_op jit(solution)/shard_map/ppermute | solution.py:482
  39.8 6.6 %collective-permute-start.6 = (f32[15,16,128]{2,1,0:T(8,128)S(1)}, f32[15,16,128]{2,1,0:T(8,128)S(1)}, u32[]{:S(2)}, u32[]{:S(2)}) collective-permute-start(f32[15,16,128]{2,1,0:T(8,128)S(1)} %get-tuple-element.34), channel_id=1, source_target_pairs={{0,1},{1,2},{2,3},{3,4},{4,5},{5,6},{6,7},{7,0},{8,9},{9,10},{10,1... | collective-permute-start | bytes 368648 | tf_op jit(solution)/shard_map/ppermute | solution.py:482
  43.2 4.3 %collective-permute-start.7 = (f32[15,16,128]{2,1,0:T(8,128)S(1)}, f32[15,16,128]{2,1,0:T(8,128)S(1)}, u32[]{:S(2)}, u32[]{:S(2)}) collective-permute-start(f32[15,16,128]{2,1,0:T(8,128)S(1)} %get-tuple-element.35), channel_id=1, source_target_pairs={{1,0},{2,1},{3,2},{4,3},{5,4},{6,5},{7,6},{0,7},{9,8},{10,9},{11,1... | collective-permute-start | bytes 368648 | tf_op jit(solution)/shard_map/ppermute | solution.py:482
  46.4 12.2 %copy-start.1 = (s32[8]{0:T(128)S(1)}, s32[8]{0:T(128)}, u32[]{:S(2)}) copy-start(s32[8]{0:T(128)} %param.7) | copy-start | bytes 100

commit v5 on v3

--- a/solution.py
+++ b/solution.py
@@ -36,27 +36,26 @@
     return out
 
 
-def held(key, x):
-    dist, inward = (-x, 1) if x < 0 else (x - CELLS + 1, -1)
+def held(key, cell, axis=0):
+    dist, inward = (-cell, 1) if cell < 0 else (cell - CELLS + 1, -1)
     if dist <= 0:
         return True
-    return (key, dist) in axis_list(0, inward)
+    return (key, dist) in axis_list(axis, inward)
 
 
 def corner_list(inward):
     out = []
-    for key, dist in axis_list(1, inward):
+    for key, dist in axis_list(0, inward):
         first, second = (0, 0) if key in MASKS else DIRS[key][:2]
-        for x in (-3, -2, -1, 8, 9, 10):
-            far = -(x + first) if x < 0 else x + first - CELLS + 1
-            if held(key, x) and not (far >= 2 and dist - inward * second >= 2):
-                out.append((key, dist, x))
+        for y in (-3, -2, -1, 8, 9, 10):
+            far = -(y + second) if y < 0 else y + second - CELLS + 1
+            if held(key, y, 1) and not (far >= 2 and dist - inward * first >= 2):
+                out.append((key, dist, y))
     return out
 
 
 X_COUNT = len(axis_list(0, 1))
-Y_OWN = len(axis_list(1, 1)) * CELLS
-Y_COUNT = Y_OWN + -(-len(corner_list(1)) // 8) * 8
+CORNER = -(-len(corner_list(1)) // 8) * 8
 
 
 def moments(f):
@@ -121,7 +120,11 @@
     return pltpu.roll(value, shift, axis)
 
 
-def first_kernel(f_ref, mask_ref, p_ref, lo_ref, hi_ref):
+def is_even(axis):
+    return lax.axis_index(axis) % 2 == 0
+
+
+def first_kernel(f_ref, mask_ref, p_ref, xa_ref, xb_ref, ya_ref, yb_ref):
     for k, key in enumerate(MASKS):
         p_ref[key] = mask_ref[k]
     for x in range(CELLS):
@@ -130,32 +133,45 @@
         post = collide(f, mask_ref[0, rows, :] > 0.5, mask_ref[1, rows, :] > 0.5)
         for i in range(27):
             p_ref[i, rows, :] = post[i]
-    for k, (key, dist) in enumerate(axis_list(0, -1)):
-        lo_ref[k] = p_ref[key, pl.ds((dist - 1) * CELLS, CELLS), :]
-    for k, (key, dist) in enumerate(axis_list(0, 1)):
-        hi_ref[k] = p_ref[key, pl.ds((CELLS - dist) * CELLS, CELLS), :]
-
-
-LOW_AT = {entry: k for k, entry in enumerate(axis_list(0, 1))}
-HIGH_AT = {entry: k for k, entry in enumerate(axis_list(0, -1))}
-
-
-def plane_ref(key, x, p_ref, xlo_ref, xhi_ref):
+    even = is_even("gx")
+    for k, (low, high) in enumerate(zip(axis_list(0, -1), axis_list(0, 1))):
+        lo = p_ref[low[0], pl.ds((low[1] - 1) * CELLS, CELLS), :]
+        hi = p_ref[high[0], pl.ds((CELLS - high[1]) * CELLS, CELLS), :]
+        xa_ref[k] = jnp.where(even, hi, lo)
+        xb_ref[k] = jnp.where(even, lo, hi)
+    even = is_even("gy")
+    for k, (low, high) in enumerate(zip(axis_list(1, -1), axis_list(1, 1))):
+        lo = p_ref[low[0], pl.ds(low[1] - 1, CELLS, stride=CELLS), :]
+        hi = p_ref[high[0], pl.ds(CELLS - high[1], CELLS, stride=CELLS), :]
+        ya_ref[k] = jnp.where(even, hi, lo)
+        yb_ref[k] = jnp.where(even, lo, hi)
+
+
+ENTRY = {(axis, inward): {e: k for k, e in enumerate(axis_list(axis, inward))} for axis in (0, 1) for inward in (1, -1)}
+
+
+def from_pair(axis, inward, dist, key, a_ref, b_ref, even, rows=slice(None)):
+    k = ENTRY[(axis, inward)][(key, dist)]
+    if inward > 0:
+        return jnp.where(even, b_ref[k, rows, :], a_ref[k, rows, :])
+    return jnp.where(even, a_ref[k, rows, :], b_ref[k, rows, :])
+
+
+def plane_value(key, x, p_ref, xa_ref, xb_ref, even):
     if x < 0:
-        return xlo_ref.at[LOW_AT[(key, -x)]]
+        return from_pair(0, 1, -x, key, xa_ref, xb_ref, even)
     if x >= CELLS:
-        return xhi_ref.at[HIGH_AT[(key, x - CELLS + 1)]]
-    return p_ref.at[key, pl.ds(x * CELLS, CELLS), :]
-
-
-def second_kernel(p_ref, xlo_ref, xhi_ref, lo_ref, hi_ref):
+        return from_pair(0, -1, x - CELLS + 1, key, xa_ref, xb_ref, even)
+    return p_ref[key, pl.ds(x * CELLS, CELLS), :]
+
+
+def second_kernel(ya_ref, yb_ref, lo_ref, hi_ref):
+    even = is_even("gy")
     for inward, out_ref in ((-1, lo_ref), (1, hi_ref)):
-        for k, (key, dist) in enumerate(axis_list(1, inward)):
-            row = dist - 1 if inward < 0 else CELLS - dist
-            out_ref[pl.ds(k * CELLS, CELLS), :] = p_ref[key, pl.ds(row, CELLS, stride=CELLS), :]
-        for k, (key, dist, x) in enumerate(corner_list(inward)):
-            row = dist - 1 if inward < 0 else CELLS - dist
-            out_ref[pl.ds(Y_OWN + k, 1), :] = plane_ref(key, x, p_ref, xlo_ref, xhi_ref)[pl.ds(row, 1), :]
+        for k, (key, dist, y) in enumerate(corner_list(inward)):
+            row = pl.ds(dist - 1 if inward < 0 else CELLS - dist, 1)
+            side, far = (1, -y) if y < 0 else (-1, y - CELLS + 1)
+            out_ref[pl.ds(k, 1), :] = from_pair(1, side, far, key, ya_ref, yb_ref, even, row)
 
 
 def pack(tiles):
@@ -170,10 +186,12 @@
     return acc
 
 
-def faces_kernel(p_ref, xlo_ref, xhi_ref, low_ref, high_ref):
+def faces_kernel(p_ref, xa_ref, xb_ref, low_ref, high_ref):
+    even = is_even("gx")
+
     def load(key, plane):
         if held(key, plane - REACH):
-            return plane_ref(key, plane - REACH, p_ref, xlo_ref, xhi_ref)[...]
+            return plane_value(key, plane - REACH, p_ref, xa_ref, xb_ref, even)
 
     for out_ref, start in ((low_ref, 3), (high_ref, 5)):
         tiles = [
@@ -197,15 +215,17 @@
     return [jnp.where(upper, turn(value, GROUP, 1), value) for value in pack(tiles)]
 
 
-def third_kernel(ylo_ref, yhi_ref, main_ref, h_ref, z_ref, lo_ref, hi_ref):
-    for inward, in_ref in ((1, ylo_ref), (-1, yhi_ref)):
-        for k, (key, dist) in enumerate(axis_list(1, inward)):
+def third_kernel(ya_ref, yb_ref, clo_ref, chi_ref, main_ref, h_ref, z_ref, lo_ref, hi_ref):
+    even = is_even("gy")
+    for inward in (1, -1):
+        for key, dist in axis_list(1, inward):
             start = CELLS * REACH + CELLS - dist if inward > 0 else CELLS * (REACH + 1) + dist - 1
-            h_ref[key, pl.ds(start, CELLS, stride=CELLS), :] = in_ref[pl.ds(k * CELLS, CELLS), :]
-        for k, (key, dist, x) in enumerate(corner_list(inward)):
-            plane = x + REACH
-            row = CELLS * plane + CELLS - dist if inward > 0 else CELLS * (plane + 1) + dist - 1
-            h_ref[key, pl.ds(row, 1), :] = in_ref[pl.ds(Y_OWN + k, 1), :]
+            h_ref[key, pl.ds(start, CELLS, stride=CELLS), :] = from_pair(1, inward, dist, key, ya_ref, yb_ref, even)
+    for inward, corner_ref in ((1, clo_ref), (-1, chi_ref)):
+        for k, (key, dist, y) in enumerate(corner_list(inward)):
+            plane = REACH - dist if inward > 0 else REACH + CELLS - 1 + dist
+            row = CELLS * plane + CELLS + y if y < 0 else CELLS * (plane + 1) + y - CELLS
+            h_ref[key, pl.ds(row, 1), :] = corner_ref[pl.ds(k, 1), :]
     halo = pack_halo(h_ref, 3)
     early = lanes_of(CELLS) % GROUP < REACH
     for key in range(29):
@@ -235,11 +255,12 @@
     return first * scale, second * scale, third * scale
 
 
-def steps_kernel(p_ref, xlo_ref, xhi_ref, h_ref, adv_ref, flow_ref, high_ref, e_ref, g_ref):
+def steps_kernel(p_ref, xa_ref, xb_ref, h_ref, adv_ref, flow_ref, high_ref, e_ref, g_ref):
+    even = is_even("gx")
     for plane in range(SPAN):
         for key in range(29):
             if held(key, plane - REACH):
-                e_ref[key, plane_rows(plane, 0), :] = plane_ref(key, plane - REACH, p_ref, xlo_ref, xhi_ref)[...]
+                e_ref[key, plane_rows(plane, 0), :] = plane_value(key, plane - REACH, p_ref, xa_ref, xb_ref, even)
     for tile in range(SPAN + 1):
         for key in range(29):
             e_ref[key, pl.ds(tile * ROWS, CELLS), :] = h_ref[key, pl.ds(tile * CELLS, CELLS), :]
@@ -481,29 +502,42 @@
     return lax.ppermute(hi, axis, forward), lax.ppermute(lo, axis, backward)
 
 
+def in_pairs(first, second, axis):
+    count = lax.axis_size(axis)
+    out = []
+    for start, value in ((0, first), (1, second)):
+        pairs = []
+        for i in range(start, count + start, 2):
+            left, right = i % count, (i + 1) % count
+            pairs += [(left, right), (right, left)]
+        out.append(lax.ppermute(value, axis, pairs))
+    return out
+
+
 def body(populations, solid_mask, jet_mask, visibility):
     cells = CELLS * CELLS
     f = populations.reshape(27, cells, LANES)
     masks = jnp.stack([solid_mask, jet_mask]).astype(jnp.float32).reshape(2, cells, LANES)
-    x_shape = (X_COUNT, CELLS, LANES)
-    post, lo, hi = call(first_kernel, ((29, cells, LANES), x_shape, x_shape))(f, masks)
-    xlo, xhi = both_ways(lo, hi, "gx")
-    y_shape = (Y_COUNT, LANES)
-    lo, hi = call(second_kernel, (y_shape, y_shape))(post, xlo, xhi)
-    ylo, yhi = both_ways(lo, hi, "gy")
+    send_shape = (X_COUNT, CELLS, LANES)
+    post, xa, xb, ya, yb = call(first_kernel, ((29, cells, LANES),) + (send_shape,) * 4)(f, masks)
+    ya, yb = in_pairs(ya, yb, "gy")
+    xa, xb = in_pairs(xa, xb, "gx")
+    corner_shape = (CORNER, LANES)
+    lo, hi = call(second_kernel, (corner_shape, corner_shape))(ya, yb)
+    clo, chi = both_ways(lo, hi, "gx")
     tile_shape = (29, CELLS, LANES)
-    low, high = call(faces_kernel, (tile_shape, tile_shape))(post, xlo, xhi)
+    low, high = call(faces_kernel, (tile_shape, tile_shape))(post, xa, xb)
     half_shape = (HALF, 2 * CELLS, LANES)
     halo, low_halo, lo, hi = call(
         third_kernel, ((29, (SPAN + 1) * CELLS, LANES), tile_shape, half_shape, half_shape)
-    )(ylo, yhi, low)
+    )(ya, yb, clo, chi, low)
     zlo, zhi = both_ways(lo, hi, "gz")
     height = SPAN * ROWS + CELLS
     moved, flow, high_halo = call(
         steps_kernel,
         ((27, cells, LANES), (3, height, LANES), tile_shape),
         (pltpu.VMEM((29, height, LANES), jnp.float32), pltpu.VMEM((27, height, LANES), jnp.float32)),
-    )(post, xlo, xhi, halo)
+    )(post, xa, xb, halo)
     edge = pltpu.VMEM((29, 3 * CELLS, LANES), jnp.float32)
     edge_post = pltpu.VMEM((27, 3 * CELLS, LANES), jnp.float32)
     advanced, slabs = call(

time: 63.3 us -> 61.8 us (0.976)
  the two profiles are of different devices: /device:TPU:24 before, /device:TPU:1 now
where the time goes in v5:
time: 61.8 us; the launch traced here: 61.3 us
  starting transfers between devices  39.6 us (64%)
  blocking collectives  8.71 us (14%)
  Pallas kernels  8.5 us (14%)
  waiting for transfers between devices  1.76 us (3%)
  local copies, waits for them, and re-layouts  1.24 us (2%)
  other arithmetic  0.78 us (1%)
  between operations  0.78 us (1%)
    ppermute x4, starting transfers between devices, in_pairs(): out.append(lax.ppermute(value, axis, pairs))  29 us
    ppermute x4, starting transfers between devices, both_ways(): return (lax.ppermute(hi, axis, forward), lax.ppermute(lo, axis, backward))  10.5 us
    all_to_all x1, blocking collectives, body(): slabs = lax.all_to_all(slabs, 'gz', 0, 0, tiled=True)  8.71 us
    pallas_call x1, Pallas kernels, body(): call(steps_kernel, ((27, cells, LANES), (3, height, LANES), tile_shape),...  3.16 us
    pallas_call x1, Pallas kernels, body(): call(render_kernel, ((27, cells, LANES), (CELLS, LANES)), (edge, edge, ed...  2.35 us
    ppermute x4, waiting for transfers between devices, both_ways(): return (lax.ppermute(hi, axis, forward), lax.ppermute(lo, axis, backward))  1.75 us
  transfers between devices with their start and end apart: 8, of which 2 were waited for; matrix products, arithmetic and copies ran while one was open for 0% of the time, Pallas kernels for 7%

profile of v5, /device:TPU:1, one launch (start us, length us, event | category | flops | bytes accessed | tf_op | source)
XLA Modules:
  0.0 61.3 jit_solution(14125465930997322124)
XLA Ops:
  0.6 0.8 %add_convert_fusion.mask_ref = f32[2,64,128]{2,1,0:T(8,128)S(1)} fusion(s32[1,64,128]{2,1,0:T(8,128)} %bitcast.12, s32[1,64,128]{2,1,0:T(8,128)} %bitcast.13), kind=kLoop, calls=%fused_computation | loop fusion | flops 32768 | bytes 131072 | tf_op jit(solution)/shard_map/convert_element_type | solution.py:520
  1.4 0.0 copy-start
  1.4 1.2 %copy-done = f32[27,8,8,128]{3,2,1,0:T(8,128)S(1)} copy-done((f32[27,8,8,128]{3,2,1,0:T(8,128)S(1)}, f32[27,8,8,128]{3,2,1,0:T(8,128)}, u32[]{:S(2)}) %copy-start) | copy-done | bytes 884760
  2.6 0.5 shard_map.59
  3.0 4.8 %collective-permute-start.2 = (f32[58,8,128]{2,1,0:T(8,128)S(1)}, f32[58,8,128]{2,1,0:T(8,128)S(1)}, u32[]{:S(2)}, u32[]{:S(2)}) collective-permute-start(f32[58,8,128]{2,1,0:T(8,128)S(1)} %get-tuple-element.23), channel_id=1, source_target_pairs={{0,8},{8,0},{16,24},{24,16},{32,40},{40,32},{48,56},{56,48},{64,72... | collective-permute-start | bytes 712712 | tf_op jit(solution)/shard_map/ppermute | solution.py:513
  7.9 16.1 %collective-permute-start.3 = (f32[58,8,128]{2,1,0:T(8,128)S(1)}, f32[58,8,128]{2,1,0:T(8,128)S(1)}, u32[]{:S(2)}, u32[]{:S(2)}) collective-permute-start(f32[58,8,128]{2,1,0:T(8,128)S(1)} %get-tuple-element.24), channel_id=1, source_target_pairs={{8,16},{16,8},{24,32},{32,24},{40,48},{48,40},{56,64},{64,56},{72,... | collective-permute-start | bytes 712712 | tf_op jit(solution)/shard_map/ppermute | solution.py:513
  24.0 3.2 %collective-permute-start = (f32[58,8,128]{2,1,0:T(8,128)S(1)}, f32[58,8,128]{2,1,0:T(8,128)S(1)}, u32[]{:S(2)}, u32[]{:S(2)}) collective-permute-start(f32[58,8,128]{2,1,0:T(8,128)S(1)} %get-tuple-element.21), channel_id=1, source_target_pairs={{0,128},{128,0},{256,384},{384,256},{512,640},{640,512},{768,896},... | collective-permute-start | bytes 712712 | tf_op jit(solution)/shard_map/ppermute | solution.py:513
  27.2 4.9 %collective-permute-start.1 = (f32[58,8,128]{2,1,0:T(8,128)S(1)}, f32[58,8,128]{2,1,0:T(8,128)S(1)}, u32[]{:S(2)}, u32[]{:S(2)}) collective-permute-start(f32[58,8,128]{2,1,0:T(8,128)S(1)} %get-tuple-element.22), channel_id=1, source_target_pairs={{128,256},{256,128},{384,512},{512,384},{640,768},{768,640},{896,0... | collective-permute-start | bytes 712712 | tf_op jit(solution)/shard_map/ppermute | solution.py:513
  32.1 0.0 collective-permute-done.2.ya_ref
  32.1 0.0 collective-permute-done.3.yb_ref
  32.1 0.2 shard_map.60
  32.3 1.9 %collective-permute-start.4 = (f32[176,128]{1,0:T(8,128)S(1)}, f32[176,128]{1,0:T(8,128)S(1)}, u32[]{:S(2)}, u32[]{:S(2)}) collective-permute-start(f32[176,128]{1,0:T(8,128)S(1)} %get-tuple-element.25), channel_id=1, source_target_pairs={{0,128},{128,256},{256,384},{384,512},{512,640},{640,768},{768,896... | collective-permute-start | bytes 270344 | tf_op jit(solution)/shard_map/ppermute | solution.py:502
  34.2 4.6 %collective-permute-start.5 = (f32[176,128]{1,0:T(8,128)S(1)}, f32[176,128]{1,0:T(8,128)S(1)}, u32[]{:S(2)}, u32[]{:S(2)}) collective-permute-start(f32[176,128]{1,0:T(8,128)S(1)} %get-tuple-element.26), channel_id=1, source_target_pairs={{128,0},{256,128},{384,256},{512,384},{640,512},{768,640},{896,768... | collective-permute-start | bytes 270344 | tf_op jit(solution)/shard_map/ppermute | solution.py:502
  38.8 0.0 collective-permute-done.xa_ref
  38.8 0.0 collective-permute-done.1.xb_ref
  38.8 0.9 %shard_map.61 = (f32[29,8,128]{2,1,0:T(8,128)S(1)}, f32[29,8,128]{2,1,0:T(8,128)S(1)}) custom-call(f32[29,64,128]{2,1,0:T(8,128)S(1)} %get-tuple-element.20.p_ref, f32[58,8,128]{2,1,0:T(8,128)S(1)} %collective-permute-done.xa_ref, f32[58,8,128]{2,1,0:T(8,128)S(1)} %collective-permute-done.1.xb_ref), custom_call_target="tpu_custom_call" | custom-call | tf_op jit(solution)/shard_map/pallas_call | solution.py:529
  39.7 0.0 collective-permute-done.4.clo_ref
  39.7 0.6 %collective-permute-done.5.chi_ref = f32[176,128]{1,0:T(8,128)S(1)} collective-permute-done((f32[176,128]{1,0:T(8,128)S(1)}, f32[176,128]{1,0:T(8,128)S(1)}, u32[]{:S(2)}, u32[]{:S(2)}) %collective-permute-start.5) | collective-permute-done | bytes 90144 | tf_op jit(solution)/shard_map/ppermute | solution.py:502
  40.3 0.7 %shard_map.62 = (f32[29,120,128]{2,1,0:T(8,128)S(1)}, f32[29,8,128]{2,1,0:T(8,128)S(1)}, f32[15,16,128]{2,1,0:T(8,128)S(1)}, f32[15,16,128]{2,1,0:T(8,128)S(1)}) custom-call(f32[58,8,128]{2,1,0:T(8,128)S(1)} %collective-permute-done.2.ya_ref, f32[58,8,128]{2,1,0:T(8,128)S(1)} %collective-permute-done.3.yb_ref, ...), custom_call_target="tpu_custom_call" | custom-call | tf_op jit(solution)/shard_map/pallas_call | solution.py:531
  41.1 4.0 %collective-permute-start.6 = (f32[15,16,128]{2,1,0:T(8,128)S(1)}, f32[15,16,128]{2,1,0:T(8,128)S(1)}, u32[]{:S(2)}, u32[]{:S(2)}) collective-permute-start(f32[15,16,128]{2,1,0:T(8,128)S(1)} %get-tuple-element.34), channel_id=1, source_target_pairs={{0,1},{1,2},{2,3},{3,4},{4,5},{5,6},{6,7},{7,0},{8,9},{9,10},{10,1... | collective-permute-start | bytes 368648 | tf_op jit(solution)/shard_map/ppermute | solution.py:502
  45.1 0.0 collective-permute-start.7
  45.1 3.2 %shard_map.63 = (f32[27,64,128]{2,1,0:T(8,128)S(1)}, f32[3,232,128]{2,1,0:T(8,128)S(1)}, f32[29,8,128]{2,1,0:T(8,128)S(1)}) custom-call(f32[29,64,128]{2,1,0:T(8,128)S(1)} %get-tuple-element.20.p_ref, f32[58,8,128]{2,1,0:T(8,128)S(1)} %collective-permute-done.xa_ref, f32[58,8,128]{2,1,0:T(8,128)S(1)} %collective-permute-done.1.xb_ref, ...), custom_call_target="tpu_custom_call" | custom-call | tf_op jit(solution)/shard_map/pallas_call | solution.py:536
  48.3 0.0 copy-start.1
  48.3 0.0 collective-permute-done.6.zlo_ref
  48.3 1.1 %collective-permute-done.7.zhi_ref = f32[15,16,128]{2,1,0:T(8,128)S(1)} collective-permute-done((f32[15,16,128]{2,1,0:T(8,128)S(1)}, f32[15,16,128]{2,1,0:T(8,128)S(1)}, u32[]{:S(2)}, u32[]{:S(2)}) %collective-permute-start.7) | collective-permute-done | bytes 122912 | tf_op jit(solution)/shard_map/ppermute | solution.py:502
  49.4 2.4 %shard_map.64 = (f32[27,64,128]{2,1,0:T(8,128)}, f32[8,128]{1,0:T(8,128)S(1)}) custom-call(f32[29,64,128]{2,1,0:T(8,128)S(1)} %get-tuple-element.20.p_ref, f32[27,64,128]{2,1,0:T(8,128)S(1)} %get-tuple-element.29.adv_ref, f32[3,232,128]{2,1,0:T(8,128)S(1)} %get-tuple-element.30.flow_ref, f32[29,8,128]{2,1,0:T(8,128)S(1)} %get-tuple-element.27.main_ref.lmain_ref, ...), custom_call_target="tpu_custom_call" | custom-call | tf_op jit(solution)/shard_map/pallas_call | solution.py:543
  51.8 8.7 %all_to_all.11 = f32[8,1,128]{2,1,0:T(1,128)S(1)} all-to-all(f32[8,1,128]{2,1,0:T(1,128)S(1)} %bitcast.11), channel_id=1, replica_groups=mesh['gx'=8,'gy'=16,'gz'=8] {'gz'}, dimensions={0} | all-to-all | bytes 8192 | tf_op jit(solution)/shard_map/all_to_all | solution.py:557
  60.5 0.0 copy-done.1
  60.5 0.1 broadcast_in_dim.2.rank_ref
  60.6 0.8 %shard_map.65 = f32[4,4,32]{2,1,0:T(4,128)} custom-call(f32[8,128]{1,0:T(8,128)S(1)} %bitcast.10, s32[8,128]{1,0:T(8,128)S(1)} %broadcast_in_dim.2.rank_ref), custom_call_target="tpu_custom_call" | custom-call | tf_op jit(solution)/shard_map/pallas_call | solution.py:559
Async XLA Ops:
  1.4 1.2 %copy-start = (f32[27,8,8,128]{3,2,1,0:T(8,128)S(1)}, f32[27,8,8,128]{3,2,1,0:T(8,128)}, u32[]{:S(2)}) copy-start(f32[27,8,8,128]{3,2,1,0:T(8,128)} %param.4) | copy-start | bytes 2654212
  3.0 29.1 %collective-permute-start.2 = (f32[58,8,128]{2,1,0:T(8,128)S(1)}, f32[58,8,128]{2,1,0:T(8,128)S(1)}, u32[]{:S(2)}, u32[]{:S(2)}) collective-permute-start(f32[58,8,128]{2,1,0:T(8,128)S(1)} %get-tuple-element.23), channel_id=1, source_target_pairs={{0,8},{8,0},{16,24},{24,16},{32,40},{40,32},{48,56},{56,48},{64,72... | collective-permute-start | bytes 712712 | tf_op jit(solution)/shard_map/ppermute | solution.py:513
  7.9 24.2 %collective-permute-start.3 = (f32[58,8,128]{2,1,0:T(8,128)S(1)}, f32[58,8,128]{2,1,0:T(8,128)S(1)}, u32[]{:S(2)}, u32[]{:S(2)}) collective-permute-start(f32[58,8,128]{2,1,0:T(8,128)S(1)} %get-tuple-element.24), channel_id=1, source_target_pairs={{8,16},{16,8},{24,32},{32,24},{40,48},{48,40},{56,64},{64,56},{72,... | collective-permute-start | bytes 712712 | tf_op jit(solution)/shard_map/ppermute | solution.py:513
  24.0 14.8 %collective-permute-start = (f32[58,8,128]{2,1,0:T(8,128)S(1)}, f32[58,8,128]{2,1,0:T(8,128)S(1)}, u32[]{:S(2)}, u32[]{:S(2)}) collective-permute-start(f32[58,8,128]{2,1,0:T(8,128)S(1)} %get-tuple-element.21), channel_id=1, source_target_pairs={{0,128},{128,0},{256,384},{384,256},{512,640},{640,512},{768,896},... | collective-permute-start | bytes 712712 | tf_op jit(solution)/shard_map/ppermute | solution.py:513
  27.2 11.6 %collective-permute-start.1 = (f32[58,8,128]{2,1,0:T(8,128)S(1)}, f32[58,8,128]{2,1,0:T(8,128)S(1)}, u32[]{:S(2)}, u32[]{:S(2)}) collective-permute-start(f32[58,8,128]{2,1,0:T(8,128)S(1)} %get-tuple-element.22), channel_id=1, source_target_pairs={{128,256},{256,128},{384,512},{512,384},{640,768},{768,640},{896,0... | collective-permute-start | bytes 712712 | tf_op jit(solution)/shard_map/ppermute | solution.py:513
  32.3 7.4 %collective-permute-start.4 = (f32[176,128]{1,0:T(8,128)S(1)}, f32[176,128]{1,0:T(8,128)S(1)}, u32[]{:S(2)}, u32[]{:S(2)}) collective-permute-start(f32[176,128]{1,0:T(8,128)S(1)} %get-tuple-element.25), channel_id=1, source_target_pairs={{0,128},{128,256},{256,384},{384,512},{512,640},{640,768},{768,896... | collective-permute-start | bytes 270344 | tf_op jit(solution)/shard_map/ppermute | solution.py:502
  34.2 6.1 %collective-permute-start.5 = (f32[176,128]{1,0:T(8,128)S(1)}, f32[176,128]{1,0:T(8,128)S(1)}, u32[]{:S(2)}, u32[]{:S(2)}) collective-permute-start(f32[176,128]{1,0:T(8,128)S(1)} %get-tuple-element.26), channel_id=1, source_target_pairs={{128,0},{256,128},{384,256},{512,384},{640,512},{768,640},{896,768... | collective-permute-start | bytes 270344 | tf_op jit(solution)/shard_map/ppermute | solution.py:502
  41.1 7.2 %collective-permute-start.6 = (f32[15,16,128]{2,1,0:T(8,128)S(1)}, f32[15,16,128]{2,1,0:T(8,128)S(1)}, u32[]{:S(2)}, u32[]{:S(2)}) collective-permute-start(f32[15,16,128]{2,1,0:T(8,128)S(1)} %get-tuple-element.34), channel_id=1, source_target_pairs={{0,1},{1,2},{2,3},{3,4},{4,5},{5,6},{6,7},{7,0},{8,9},{9,10},{10,1... | collective-permute-start | bytes 368648 | tf_op jit(solution)/shard_map/ppermute | solution.py:502
  45.1 4.3 %collective-permute-start.7 = (f32[15,16,128]{2,1,0:T(8,128)S(1)}, f32[15,16,128]{2,1,0:T(8,128)S(1)}, u32[]{:S(2)}, u32[]{:S(2)}) collective-permute-start(f32[15,16,128]{2,1,0:T(8,128)S(1)} %get-tuple-element.35), channel_id=1, source_target_pairs={{1,0},{2,1},{3,2},{4,3},{5,4},{6,5},{7,6},{0,7},{9,8},{10,9},{11,1... | collective-permute-start | bytes 368648 | tf_op jit(solution)/shard_map/ppermute | solution.py:502
  48.3 12.2 %copy-start.1 = (s32[8]{0:T(128)S(1)}, s32[8]{0:T(128)}, u32[]{:S(2)}) copy-start(s32[8]{0:T(128)} %param.7) | copy-start | bytes 100

commit v6 on v5

--- a/solution.py
+++ b/solution.py
@@ -124,13 +124,26 @@
     return lax.axis_index(axis) % 2 == 0
 
 
-def first_kernel(f_ref, mask_ref, p_ref, xa_ref, xb_ref, ya_ref, yb_ref):
-    for k, key in enumerate(MASKS):
-        p_ref[key] = mask_ref[k]
+def first_kernel(f_hbm, solid_hbm, jet_hbm, p_ref, xa_ref, xb_ref, ya_ref, yb_ref, f_ref, solid_ref, jet_ref, sems):
+    masks = [
+        pltpu.make_async_copy(solid_hbm, solid_ref, sems.at[CELLS]),
+        pltpu.make_async_copy(jet_hbm, jet_ref, sems.at[CELLS + 1]),
+    ]
+    copies = []
     for x in range(CELLS):
         rows = pl.ds(x * CELLS, CELLS)
+        copies.append(pltpu.make_async_copy(f_hbm.at[:, rows, :], f_ref.at[:, rows, :], sems.at[x]))
+    for copy in masks + copies:
+        copy.start()
+    for copy in masks:
+        copy.wait()
+    p_ref[SOLID] = solid_ref[...].astype(jnp.float32)
+    p_ref[JET] = jet_ref[...].astype(jnp.float32)
+    for x in range(CELLS):
+        copies[x].wait()
+        rows = pl.ds(x * CELLS, CELLS)
         f = [f_ref[i, rows, :] for i in range(27)]
-        post = collide(f, mask_ref[0, rows, :] > 0.5, mask_ref[1, rows, :] > 0.5)
+        post = collide(f, solid_ref[rows, :] == 1, jet_ref[rows, :] == 1)
         for i in range(27):
             p_ref[i, rows, :] = post[i]
     even = is_even("gx")
@@ -480,9 +493,11 @@
         out_ref[ch] = jnp.broadcast_to(turn(row, -ch * CELLS * UP, 1)[:, : CELLS * UP], (UP, CELLS * UP))
 
 
-def call(kernel, outs, scratch=(), first_out_hbm=False):
+def call(kernel, outs, scratch=(), first_out_hbm=False, in_hbm=False):
     shapes = tuple(jax.ShapeDtypeStruct(shape, jnp.float32) for shape in outs)
     extra = {}
+    if in_hbm:
+        extra["in_specs"] = [pl.BlockSpec(memory_space=pltpu.HBM)] * 3
     if first_out_hbm:
         spaces = [pltpu.HBM] + [pltpu.VMEM] * (len(outs) - 1)
         extra["out_specs"] = tuple(pl.BlockSpec(memory_space=space) for space in spaces)
@@ -517,11 +532,24 @@
 def body(populations, solid_mask, jet_mask, visibility):
     cells = CELLS * CELLS
     f = populations.reshape(27, cells, LANES)
-    masks = jnp.stack([solid_mask, jet_mask]).astype(jnp.float32).reshape(2, cells, LANES)
+    solid = solid_mask.reshape(cells, LANES)
+    jet = jet_mask.reshape(cells, LANES)
+    f, solid, jet = [pltpu.with_memory_space_constraint(value, pltpu.HBM) for value in (f, solid, jet)]
     send_shape = (X_COUNT, CELLS, LANES)
-    post, xa, xb, ya, yb = call(first_kernel, ((29, cells, LANES),) + (send_shape,) * 4)(f, masks)
+    post, xa, xb, ya, yb = call(
+        first_kernel,
+        ((29, cells, LANES),) + (send_shape,) * 4,
+        (
+            pltpu.VMEM((27, cells, LANES), jnp.float32),
+            pltpu.VMEM((cells, LANES), jnp.int32),
+            pltpu.VMEM((cells, LANES), jnp.int32),
+            pltpu.SemaphoreType.DMA((CELLS + 2,)),
+        ),
+        in_hbm=True,
+    )(f, solid, jet)
+    xa, xb = in_pairs(xa, xb, "gx")
     ya, yb = in_pairs(ya, yb, "gy")
-    xa, xb = in_pairs(xa, xb, "gx")
+    xa, xb, ya, yb = lax.optimization_barrier((xa, xb, ya, yb))
     corner_shape = (CORNER, LANES)
     lo, hi = call(second_kernel, (corner_shape, corner_shape))(ya, yb)
     clo, chi = both_ways(lo, hi, "gx")

time: 61.8 us -> 65.8 us (1.065)
  waiting for transfers between devices: 1.76 us -> 6.3 us
  local copies, waits for them, and re-layouts: 1.24 us -> 0.08 us
  Pallas kernels: 8.5 us -> 9.65 us
  other arithmetic: 0.78 us -> 0 us
    ppermute x4, waiting for transfers between devices: 0.01 us -> 4.53 us  [in_pairs(): out.append(lax.ppermute(value, axis, pairs))]
    unnamed x4 -> x2, local copies, waits for them, and re-layouts: 1.17 us -> 0.01 us
    pallas_call x1, Pallas kernels: 0.45 us -> 1.61 us  [body(): call(first_kernel, ((29, cells, LANES),) + (send_shape,) * 4, (pltpu.VMEM...]
    convert_element_type x1 -> x0, other arithmetic: 0.78 us -> none  [body(): jnp.stack([solid_mask, jet_mask]).astype(jnp.float32)]
  transfers between devices with their start and end apart: 8 -> 8, of which waited for: 2 -> 3; matrix products, arithmetic and copies ran while one was open for 0% -> 0% of each run, Pallas kernels for 7% -> 6%
where the time goes in v6:
time: 65.8 us; the launch traced here: 65.4 us
  starting transfers between devices  39.9 us (61%)
  Pallas kernels  9.65 us (15%)
  blocking collectives  8.71 us (13%)
  waiting for transfers between devices  6.3 us (10%)
  between operations  0.77 us (1%)
    ppermute x4, starting transfers between devices, in_pairs(): out.append(lax.ppermute(value, axis, pairs))  29 us
    ppermute x4, starting transfers between devices, both_ways(): return (lax.ppermute(hi, axis, forward), lax.ppermute(lo, axis, backward))  10.9 us
    all_to_all x1, blocking collectives, body(): slabs = lax.all_to_all(slabs, 'gz', 0, 0, tiled=True)  8.71 us
    ppermute x4, waiting for transfers between devices, in_pairs(): out.append(lax.ppermute(value, axis, pairs))  4.53 us
    pallas_call x1, Pallas kernels, body(): call(steps_kernel, ((27, cells, LANES), (3, height, LANES), tile_shape),...  3.16 us
    pallas_call x1, Pallas kernels, body(): call(render_kernel, ((27, cells, LANES), (CELLS, LANES)), (edge, edge, ed...  2.35 us
    ppermute x4, waiting for transfers between devices, both_ways(): return (lax.ppermute(hi, axis, forward), lax.ppermute(lo, axis, backward))  1.77 us
    pallas_call x1, Pallas kernels, body(): call(first_kernel, ((29, cells, LANES),) + (send_shape,) * 4, (pltpu.VMEM...  1.61 us
  transfers between devices with their start and end apart: 8, of which 3 were waited for; matrix products, arithmetic and copies ran while one was open for 0% of the time, Pallas kernels for 6%

profile of v6, /device:TPU:1, one launch (start us, length us, event | category | flops | bytes accessed | tf_op | source)
XLA Modules:
  0.0 65.4 jit_solution(15447883884555478949)
XLA Ops:
  0.6 1.6 %shard_map.59 = (f32[29,64,128]{2,1,0:T(8,128)S(1)}, f32[58,8,128]{2,1,0:T(8,128)S(1)}, f32[58,8,128]{2,1,0:T(8,128)S(1)}, f32[58,8,128]{2,1,0:T(8,128)S(1)}, f32[58,8,128]{2,1,0:T(8,128)S(1)}) custom-call(f32[27,64,128]{2,1,0:T(8,128)} %bitcast.11, s32[64,128]{1,0:T(8,128)} %bitcast.12, s32[64,128]{1,0:T(8,128)} %bitcast.13), custom_call_target="tpu_custom_call" | custom-call | tf_op jit(solution)/shard_map/pallas_call | solution.py:539
  2.2 4.0 %collective-permute-start = (f32[58,8,128]{2,1,0:T(8,128)S(1)}, f32[58,8,128]{2,1,0:T(8,128)S(1)}, u32[]{:S(2)}, u32[]{:S(2)}) collective-permute-start(f32[58,8,128]{2,1,0:T(8,128)S(1)} %get-tuple-element.25), channel_id=1, source_target_pairs={{0,128},{128,0},{256,384},{384,256},{512,640},{640,512},{768,896},... | collective-permute-start | bytes 712712 | tf_op jit(solution)/shard_map/ppermute | solution.py:528
  6.3 4.9 %collective-permute-start.1 = (f32[58,8,128]{2,1,0:T(8,128)S(1)}, f32[58,8,128]{2,1,0:T(8,128)S(1)}, u32[]{:S(2)}, u32[]{:S(2)}) collective-permute-start(f32[58,8,128]{2,1,0:T(8,128)S(1)} %get-tuple-element.26), channel_id=1, source_target_pairs={{128,256},{256,128},{384,512},{512,384},{640,768},{768,640},{896,0... | collective-permute-start | bytes 712712 | tf_op jit(solution)/shard_map/ppermute | solution.py:528
  11.2 4.0 %collective-permute-start.2 = (f32[58,8,128]{2,1,0:T(8,128)S(1)}, f32[58,8,128]{2,1,0:T(8,128)S(1)}, u32[]{:S(2)}, u32[]{:S(2)}) collective-permute-start(f32[58,8,128]{2,1,0:T(8,128)S(1)} %get-tuple-element.27), channel_id=1, source_target_pairs={{0,8},{8,0},{16,24},{24,16},{32,40},{40,32},{48,56},{56,48},{64,72... | collective-permute-start | bytes 712712 | tf_op jit(solution)/shard_map/ppermute | solution.py:528
  15.2 16.1 %collective-permute-start.3 = (f32[58,8,128]{2,1,0:T(8,128)S(1)}, f32[58,8,128]{2,1,0:T(8,128)S(1)}, u32[]{:S(2)}, u32[]{:S(2)}) collective-permute-start(f32[58,8,128]{2,1,0:T(8,128)S(1)} %get-tuple-element.28), channel_id=1, source_target_pairs={{8,16},{16,8},{24,32},{32,24},{40,48},{48,40},{56,64},{64,56},{72,... | collective-permute-start | bytes 712712 | tf_op jit(solution)/shard_map/ppermute | solution.py:528
  31.3 0.0 collective-permute-done.xa_ref
  31.3 0.0 collective-permute-done.1.xb_ref
  31.3 0.0 collective-permute-done.2.ya_ref
  31.3 4.5 %collective-permute-done.3.yb_ref = f32[58,8,128]{2,1,0:T(8,128)S(1)} collective-permute-done((f32[58,8,128]{2,1,0:T(8,128)S(1)}, f32[58,8,128]{2,1,0:T(8,128)S(1)}, u32[]{:S(2)}, u32[]{:S(2)}) %collective-permute-start.3) | collective-permute-done | bytes 237600 | tf_op jit(solution)/shard_map/ppermute | solution.py:528
  35.9 0.1 shard_map.60
  36.0 1.9 %collective-permute-start.4 = (f32[176,128]{1,0:T(8,128)S(1)}, f32[176,128]{1,0:T(8,128)S(1)}, u32[]{:S(2)}, u32[]{:S(2)}) collective-permute-start(f32[176,128]{1,0:T(8,128)S(1)} %get-tuple-element.33), channel_id=1, source_target_pairs={{0,128},{128,256},{256,384},{384,512},{512,640},{640,768},{768,896... | collective-permute-start | bytes 270344 | tf_op jit(solution)/shard_map/ppermute | solution.py:517
  37.9 4.6 %collective-permute-start.5 = (f32[176,128]{1,0:T(8,128)S(1)}, f32[176,128]{1,0:T(8,128)S(1)}, u32[]{:S(2)}, u32[]{:S(2)}) collective-permute-start(f32[176,128]{1,0:T(8,128)S(1)} %get-tuple-element.34), channel_id=1, source_target_pairs={{128,0},{256,128},{384,256},{512,384},{640,512},{768,640},{896,768... | collective-permute-start | bytes 270344 | tf_op jit(solution)/shard_map/ppermute | solution.py:517
  42.5 0.9 %shard_map.61 = (f32[29,8,128]{2,1,0:T(8,128)S(1)}, f32[29,8,128]{2,1,0:T(8,128)S(1)}) custom-call(f32[29,64,128]{2,1,0:T(8,128)S(1)} %get-tuple-element.24.p_ref, f32[58,8,128]{2,1,0:T(8,128)S(1)} %collective-permute-done.xa_ref, f32[58,8,128]{2,1,0:T(8,128)S(1)} %collective-permute-done.1.xb_ref), custom_call_target="tpu_custom_call" | custom-call | tf_op jit(solution)/shard_map/pallas_call | solution.py:557
  43.4 0.0 collective-permute-done.4.clo_ref
  43.4 0.7 collective-permute-done.5.chi_ref
  44.1 0.7 %shard_map.62 = (f32[29,120,128]{2,1,0:T(8,128)S(1)}, f32[29,8,128]{2,1,0:T(8,128)S(1)}, f32[15,16,128]{2,1,0:T(8,128)S(1)}, f32[15,16,128]{2,1,0:T(8,128)S(1)}) custom-call(f32[58,8,128]{2,1,0:T(8,128)S(1)} %collective-permute-done.2.ya_ref, f32[58,8,128]{2,1,0:T(8,128)S(1)} %collective-permute-done.3.yb_ref, ...), custom_call_target="tpu_custom_call" | custom-call | tf_op jit(solution)/shard_map/pallas_call | solution.py:559
  44.8 4.4 %collective-permute-start.6 = (f32[15,16,128]{2,1,0:T(8,128)S(1)}, f32[15,16,128]{2,1,0:T(8,128)S(1)}, u32[]{:S(2)}, u32[]{:S(2)}) collective-permute-start(f32[15,16,128]{2,1,0:T(8,128)S(1)} %get-tuple-element.42), channel_id=1, source_target_pairs={{0,1},{1,2},{2,3},{3,4},{4,5},{5,6},{6,7},{7,0},{8,9},{9,10},{10,1... | collective-permute-start | bytes 368648 | tf_op jit(solution)/shard_map/ppermute | solution.py:517
  49.2 0.0 collective-permute-start.7
  49.2 3.2 %shard_map.63 = (f32[27,64,128]{2,1,0:T(8,128)S(1)}, f32[3,232,128]{2,1,0:T(8,128)S(1)}, f32[29,8,128]{2,1,0:T(8,128)S(1)}) custom-call(f32[29,64,128]{2,1,0:T(8,128)S(1)} %get-tuple-element.24.p_ref, f32[58,8,128]{2,1,0:T(8,128)S(1)} %collective-permute-done.xa_ref, f32[58,8,128]{2,1,0:T(8,128)S(1)} %collective-permute-done.1.xb_ref, ...), custom_call_target="tpu_custom_call" | custom-call | tf_op jit(solution)/shard_map/pallas_call | solution.py:564
  52.4 0.0 copy-start
  52.4 0.0 collective-permute-done.6.zlo_ref
  52.4 1.1 %collective-permute-done.7.zhi_ref = f32[15,16,128]{2,1,0:T(8,128)S(1)} collective-permute-done((f32[15,16,128]{2,1,0:T(8,128)S(1)}, f32[15,16,128]{2,1,0:T(8,128)S(1)}, u32[]{:S(2)}, u32[]{:S(2)}) %collective-permute-start.7) | collective-permute-done | bytes 122912 | tf_op jit(solution)/shard_map/ppermute | solution.py:517
  53.5 2.4 %shard_map.64 = (f32[27,64,128]{2,1,0:T(8,128)}, f32[8,128]{1,0:T(8,128)S(1)}) custom-call(f32[29,64,128]{2,1,0:T(8,128)S(1)} %get-tuple-element.24.p_ref, f32[27,64,128]{2,1,0:T(8,128)S(1)} %get-tuple-element.37.adv_ref, f32[3,232,128]{2,1,0:T(8,128)S(1)} %get-tuple-element.38.flow_ref, f32[29,8,128]{2,1,0:T(8,128)S(1)} %get-tuple-element.35.main_ref.lmain_ref, ...), custom_call_target="tpu_custom_call" | custom-call | tf_op jit(solution)/shard_map/pallas_call | solution.py:571
  55.9 8.7 %all_to_all.11 = f32[8,1,128]{2,1,0:T(1,128)S(1)} all-to-all(f32[8,1,128]{2,1,0:T(1,128)S(1)} %bitcast.10), channel_id=1, replica_groups=mesh['gx'=8,'gy'=16,'gz'=8] {'gz'}, dimensions={0} | all-to-all | bytes 8192 | tf_op jit(solution)/shard_map/all_to_all | solution.py:585
  64.6 0.0 copy-done
  64.6 0.1 broadcast_in_dim.2.rank_ref
  64.7 0.8 %shard_map.65 = f32[4,4,32]{2,1,0:T(4,128)} custom-call(f32[8,128]{1,0:T(8,128)S(1)} %bitcast.9, s32[8,128]{1,0:T(8,128)S(1)} %broadcast_in_dim.2.rank_ref), custom_call_target="tpu_custom_call" | custom-call | tf_op jit(solution)/shard_map/pallas_call | solution.py:587
Async XLA Ops:
  2.2 29.1 %collective-permute-start = (f32[58,8,128]{2,1,0:T(8,128)S(1)}, f32[58,8,128]{2,1,0:T(8,128)S(1)}, u32[]{:S(2)}, u32[]{:S(2)}) collective-permute-start(f32[58,8,128]{2,1,0:T(8,128)S(1)} %get-tuple-element.25), channel_id=1, source_target_pairs={{0,128},{128,0},{256,384},{384,256},{512,640},{640,512},{768,896},... | collective-permute-start | bytes 712712 | tf_op jit(solution)/shard_map/ppermute | solution.py:528
  6.3 25.0 %collective-permute-start.1 = (f32[58,8,128]{2,1,0:T(8,128)S(1)}, f32[58,8,128]{2,1,0:T(8,128)S(1)}, u32[]{:S(2)}, u32[]{:S(2)}) collective-permute-start(f32[58,8,128]{2,1,0:T(8,128)S(1)} %get-tuple-element.26), channel_id=1, source_target_pairs={{128,256},{256,128},{384,512},{512,384},{640,768},{768,640},{896,0... | collective-permute-start | bytes 712712 | tf_op jit(solution)/shard_map/ppermute | solution.py:528
  11.2 20.2 %collective-permute-start.2 = (f32[58,8,128]{2,1,0:T(8,128)S(1)}, f32[58,8,128]{2,1,0:T(8,128)S(1)}, u32[]{:S(2)}, u32[]{:S(2)}) collective-permute-start(f32[58,8,128]{2,1,0:T(8,128)S(1)} %get-tuple-element.27), channel_id=1, source_target_pairs={{0,8},{8,0},{16,24},{24,16},{32,40},{40,32},{48,56},{56,48},{64,72... | collective-permute-start | bytes 712712 | tf_op jit(solution)/shard_map/ppermute | solution.py:528
  15.2 20.7 %collective-permute-start.3 = (f32[58,8,128]{2,1,0:T(8,128)S(1)}, f32[58,8,128]{2,1,0:T(8,128)S(1)}, u32[]{:S(2)}, u32[]{:S(2)}) collective-permute-start(f32[58,8,128]{2,1,0:T(8,128)S(1)} %get-tuple-element.28), channel_id=1, source_target_pairs={{8,16},{16,8},{24,32},{32,24},{40,48},{48,40},{56,64},{64,56},{72,... | collective-permute-start | bytes 712712 | tf_op jit(solution)/shard_map/ppermute | solution.py:528
  36.0 7.4 %collective-permute-start.4 = (f32[176,128]{1,0:T(8,128)S(1)}, f32[176,128]{1,0:T(8,128)S(1)}, u32[]{:S(2)}, u32[]{:S(2)}) collective-permute-start(f32[176,128]{1,0:T(8,128)S(1)} %get-tuple-element.33), channel_id=1, source_target_pairs={{0,128},{128,256},{256,384},{384,512},{512,640},{640,768},{768,896... | collective-permute-start | bytes 270344 | tf_op jit(solution)/shard_map/ppermute | solution.py:517
  37.9 6.1 %collective-permute-start.5 = (f32[176,128]{1,0:T(8,128)S(1)}, f32[176,128]{1,0:T(8,128)S(1)}, u32[]{:S(2)}, u32[]{:S(2)}) collective-permute-start(f32[176,128]{1,0:T(8,128)S(1)} %get-tuple-element.34), channel_id=1, source_target_pairs={{128,0},{256,128},{384,256},{512,384},{640,512},{768,640},{896,768... | collective-permute-start | bytes 270344 | tf_op jit(solution)/shard_map/ppermute | solution.py:517
  44.8 7.6 %collective-permute-start.6 = (f32[15,16,128]{2,1,0:T(8,128)S(1)}, f32[15,16,128]{2,1,0:T(8,128)S(1)}, u32[]{:S(2)}, u32[]{:S(2)}) collective-permute-start(f32[15,16,128]{2,1,0:T(8,128)S(1)} %get-tuple-element.42), channel_id=1, source_target_pairs={{0,1},{1,2},{2,3},{3,4},{4,5},{5,6},{6,7},{7,0},{8,9},{9,10},{10,1... | collective-permute-start | bytes 368648 | tf_op jit(solution)/shard_map/ppermute | solution.py:517
  49.2 4.3 %collective-permute-start.7 = (f32[15,16,128]{2,1,0:T(8,128)S(1)}, f32[15,16,128]{2,1,0:T(8,128)S(1)}, u32[]{:S(2)}, u32[]{:S(2)}) collective-permute-start(f32[15,16,128]{2,1,0:T(8,128)S(1)} %get-tuple-element.43), channel_id=1, source_target_pairs={{1,0},{2,1},{3,2},{4,3},{5,4},{6,5},{7,6},{0,7},{9,8},{10,9},{11,1... | collective-permute-start | bytes 368648 | tf_op jit(solution)/shard_map/ppermute | solution.py:517
  52.4 12.2 %copy-start = (s32[8]{0:T(128)S(1)}, s32[8]{0:T(128)}, u32[]{:S(2)}) copy-start(s32[8]{0:T(128)} %param.7) | copy-start | bytes 100

commit v7 on v4

--- a/solution.py
+++ b/solution.py
@@ -121,13 +121,28 @@
     return pltpu.roll(value, shift, axis)
 
 
-def first_kernel(f_ref, mask_ref, p_ref, lo_ref, hi_ref, ylo_ref, yhi_ref):
-    for k, key in enumerate(MASKS):
-        p_ref[key] = mask_ref[k]
+def first_kernel(
+    f_hbm, solid_hbm, jet_hbm, p_ref, lo_ref, hi_ref, ylo_ref, yhi_ref, f_ref, solid_ref, jet_ref, sems
+):
+    masks = [
+        pltpu.make_async_copy(solid_hbm, solid_ref, sems.at[CELLS]),
+        pltpu.make_async_copy(jet_hbm, jet_ref, sems.at[CELLS + 1]),
+    ]
+    copies = []
     for x in range(CELLS):
         rows = pl.ds(x * CELLS, CELLS)
+        copies.append(pltpu.make_async_copy(f_hbm.at[:, rows, :], f_ref.at[:, rows, :], sems.at[x]))
+    for copy in masks + copies:
+        copy.start()
+    for copy in masks:
+        copy.wait()
+    p_ref[SOLID] = solid_ref[...].astype(jnp.float32)
+    p_ref[JET] = jet_ref[...].astype(jnp.float32)
+    for x in range(CELLS):
+        copies[x].wait()
+        rows = pl.ds(x * CELLS, CELLS)
         f = [f_ref[i, rows, :] for i in range(27)]
-        post = collide(f, mask_ref[0, rows, :] > 0.5, mask_ref[1, rows, :] > 0.5)
+        post = collide(f, solid_ref[rows, :] == 1, jet_ref[rows, :] == 1)
         for i in range(27):
             p_ref[i, rows, :] = post[i]
     for k, (key, dist) in enumerate(axis_list(0, -1)):
@@ -460,9 +475,11 @@
         out_ref[ch] = jnp.broadcast_to(turn(row, -ch * CELLS * UP, 1)[:, : CELLS * UP], (UP, CELLS * UP))
 
 
-def call(kernel, outs, scratch=(), first_out_hbm=False):
+def call(kernel, outs, scratch=(), first_out_hbm=False, in_hbm=False):
     shapes = tuple(jax.ShapeDtypeStruct(shape, jnp.float32) for shape in outs)
     extra = {}
+    if in_hbm:
+        extra["in_specs"] = [pl.BlockSpec(memory_space=pltpu.HBM)] * 3
     if first_out_hbm:
         spaces = [pltpu.HBM] + [pltpu.VMEM] * (len(outs) - 1)
         extra["out_specs"] = tuple(pl.BlockSpec(memory_space=space) for space in spaces)
@@ -485,10 +502,22 @@
 def body(populations, solid_mask, jet_mask, visibility):
     cells = CELLS * CELLS
     f = populations.reshape(27, cells, LANES)
-    masks = jnp.stack([solid_mask, jet_mask]).astype(jnp.float32).reshape(2, cells, LANES)
+    solid = solid_mask.reshape(cells, LANES)
+    jet = jet_mask.reshape(cells, LANES)
+    f, solid, jet = [pltpu.with_memory_space_constraint(value, pltpu.HBM) for value in (f, solid, jet)]
     x_shape = (X_COUNT, CELLS, LANES)
     y_shape = (Y_OWN, LANES)
-    post, lo, hi, down, up = call(first_kernel, ((29, cells, LANES), x_shape, x_shape, y_shape, y_shape))(f, masks)
+    post, lo, hi, down, up = call(
+        first_kernel,
+        ((29, cells, LANES), x_shape, x_shape, y_shape, y_shape),
+        (
+            pltpu.VMEM((27, cells, LANES), jnp.float32),
+            pltpu.VMEM((cells, LANES), jnp.int32),
+            pltpu.VMEM((cells, LANES), jnp.int32),
+            pltpu.SemaphoreType.DMA((CELLS + 2,)),
+        ),
+        in_hbm=True,
+    )(f, solid, jet)
     xlo, xhi = both_ways(lo, hi, "gx")
     ylo, yhi = both_ways(down, up, "gy")
     corner_shape = (Y_CORNER, LANES)

time: 59.9 us -> 59 us (0.985)
  local copies, waits for them, and re-layouts: 1.24 us -> 0.08 us
  Pallas kernels: 8.42 us -> 9.56 us
  other arithmetic: 0.78 us -> 0 us
    unnamed x4 -> x2, local copies, waits for them, and re-layouts: 1.17 us -> 0.01 us
    pallas_call x1, Pallas kernels: 0.46 us -> 1.61 us  [body(): call(first_kernel, ((29, cells, LANES), x_shape, x_shape, y_shape, y_shap...]
    convert_element_type x1 -> x0, other arithmetic: 0.78 us -> none  [body(): jnp.stack([solid_mask, jet_mask]).astype(jnp.float32)]
where the time goes in v7:
time: 59 us; the launch traced here: 58.7 us
  starting transfers between devices  37.7 us (64%)
  Pallas kernels  9.56 us (16%)
  blocking collectives  8.71 us (15%)
  waiting for transfers between devices  1.84 us (3%)
  between operations  0.78 us (1%)
    ppermute x8, starting transfers between devices, both_ways(): return (lax.ppermute(hi, axis, forward), lax.ppermute(lo, axis, backward))  37.7 us
    all_to_all x1, blocking collectives, body(): slabs = lax.all_to_all(slabs, 'gz', 0, 0, tiled=True)  8.71 us
    pallas_call x1, Pallas kernels, body(): call(steps_kernel, ((27, cells, LANES), (3, height, LANES), tile_shape),...  3.13 us
    pallas_call x1, Pallas kernels, body(): call(render_kernel, ((27, cells, LANES), (CELLS, LANES)), (edge, edge, ed...  2.36 us
    ppermute x8, waiting for transfers between devices, both_ways(): return (lax.ppermute(hi, axis, forward), lax.ppermute(lo, axis, backward))  1.84 us
    pallas_call x1, Pallas kernels, body(): call(first_kernel, ((29, cells, LANES), x_shape, x_shape, y_shape, y_shap...  1.61 us
  transfers between devices with their start and end apart: 8, of which 2 were waited for; matrix products, arithmetic and copies ran while one was open for 0% of the time, Pallas kernels for 7%

profile of v7, /device:TPU:1, one launch (start us, length us, event | category | flops | bytes accessed | tf_op | source)
XLA Modules:
  0.0 58.7 jit_solution(1668513241110872653)
XLA Ops:
  0.6 1.6 %shard_map.59 = (f32[29,64,128]{2,1,0:T(8,128)S(1)}, f32[58,8,128]{2,1,0:T(8,128)S(1)}, f32[58,8,128]{2,1,0:T(8,128)S(1)}, f32[464,128]{1,0:T(8,128)S(1)}, f32[464,128]{1,0:T(8,128)S(1)}) custom-call(f32[27,64,128]{2,1,0:T(8,128)} %bitcast.11, s32[64,128]{1,0:T(8,128)} %bitcast.12, s32[64,128]{1,0:T(8,128)} %bitcast.13), custom_call_target="tpu_custom_call" | custom-call | tf_op jit(solution)/shard_map/pallas_call | solution.py:510
  2.2 4.0 %collective-permute-start = (f32[58,8,128]{2,1,0:T(8,128)S(1)}, f32[58,8,128]{2,1,0:T(8,128)S(1)}, u32[]{:S(2)}, u32[]{:S(2)}) collective-permute-start(f32[58,8,128]{2,1,0:T(8,128)S(1)} %get-tuple-element.21), channel_id=1, source_target_pairs={{0,128},{128,256},{256,384},{384,512},{512,640},{640,768},{768,896... | collective-permute-start | bytes 712712 | tf_op jit(solution)/shard_map/ppermute | solution.py:499
  6.3 3.8 %collective-permute-start.1 = (f32[58,8,128]{2,1,0:T(8,128)S(1)}, f32[58,8,128]{2,1,0:T(8,128)S(1)}, u32[]{:S(2)}, u32[]{:S(2)}) collective-permute-start(f32[58,8,128]{2,1,0:T(8,128)S(1)} %get-tuple-element.22), channel_id=1, source_target_pairs={{128,0},{256,128},{384,256},{512,384},{640,512},{768,640},{896,768... | collective-permute-start | bytes 712712 | tf_op jit(solution)/shard_map/ppermute | solution.py:499
  10.1 4.0 %collective-permute-start.2 = (f32[464,128]{1,0:T(8,128)S(1)}, f32[464,128]{1,0:T(8,128)S(1)}, u32[]{:S(2)}, u32[]{:S(2)}) collective-permute-start(f32[464,128]{1,0:T(8,128)S(1)} %get-tuple-element.23), channel_id=1, source_target_pairs={{0,8},{8,16},{16,24},{24,32},{32,40},{40,48},{48,56},{56,64},{64,7... | collective-permute-start | bytes 712712 | tf_op jit(solution)/shard_map/ppermute | solution.py:499
  14.1 15.9 %collective-permute-start.3 = (f32[464,128]{1,0:T(8,128)S(1)}, f32[464,128]{1,0:T(8,128)S(1)}, u32[]{:S(2)}, u32[]{:S(2)}) collective-permute-start(f32[464,128]{1,0:T(8,128)S(1)} %get-tuple-element.24), channel_id=1, source_target_pairs={{8,0},{16,8},{24,16},{32,24},{40,32},{48,40},{56,48},{64,56},{72,6... | collective-permute-start | bytes 712712 | tf_op jit(solution)/shard_map/ppermute | solution.py:499
  30.0 0.0 collective-permute-done.xlo_ref
  30.0 0.0 collective-permute-done.1.xhi_ref
  30.0 0.1 shard_map.60
  30.1 1.9 %collective-permute-start.4 = (f32[176,128]{1,0:T(8,128)S(1)}, f32[176,128]{1,0:T(8,128)S(1)}, u32[]{:S(2)}, u32[]{:S(2)}) collective-permute-start(f32[176,128]{1,0:T(8,128)S(1)} %get-tuple-element.25), channel_id=1, source_target_pairs={{0,8},{8,16},{16,24},{24,32},{32,40},{40,48},{48,56},{56,64},{64,7... | collective-permute-start | bytes 270344 | tf_op jit(solution)/shard_map/ppermute | solution.py:499
  32.1 4.6 %collective-permute-start.5 = (f32[176,128]{1,0:T(8,128)S(1)}, f32[176,128]{1,0:T(8,128)S(1)}, u32[]{:S(2)}, u32[]{:S(2)}) collective-permute-start(f32[176,128]{1,0:T(8,128)S(1)} %get-tuple-element.26), channel_id=1, source_target_pairs={{8,0},{16,8},{24,16},{32,24},{40,32},{48,40},{56,48},{64,56},{72,6... | collective-permute-start | bytes 270344 | tf_op jit(solution)/shard_map/ppermute | solution.py:499
  36.7 0.8 %shard_map.61 = (f32[29,8,128]{2,1,0:T(8,128)S(1)}, f32[29,8,128]{2,1,0:T(8,128)S(1)}) custom-call(f32[29,64,128]{2,1,0:T(8,128)S(1)} %get-tuple-element.20.p_ref, f32[58,8,128]{2,1,0:T(8,128)S(1)} %collective-permute-done.xlo_ref, f32[58,8,128]{2,1,0:T(8,128)S(1)} %collective-permute-done.1.xhi_ref), custom_call_target="tpu_custom_call" | custom-call | tf_op jit(solution)/shard_map/pallas_call | solution.py:527
  37.5 0.0 collective-permute-done.2.ylo_ref
  37.5 0.0 collective-permute-done.3.yhi_ref
  37.5 0.0 collective-permute-done.4.clo_ref
  37.5 0.7 %collective-permute-done.5.chi_ref = f32[176,128]{1,0:T(8,128)S(1)} collective-permute-done((f32[176,128]{1,0:T(8,128)S(1)}, f32[176,128]{1,0:T(8,128)S(1)}, u32[]{:S(2)}, u32[]{:S(2)}) %collective-permute-start.5) | collective-permute-done | bytes 90144 | tf_op jit(solution)/shard_map/ppermute | solution.py:499
  38.2 0.8 %shard_map.62 = (f32[29,120,128]{2,1,0:T(8,128)S(1)}, f32[29,8,128]{2,1,0:T(8,128)S(1)}, f32[15,16,128]{2,1,0:T(8,128)S(1)}, f32[15,16,128]{2,1,0:T(8,128)S(1)}) custom-call(f32[464,128]{1,0:T(8,128)S(1)} %collective-permute-done.2.ylo_ref, f32[464,128]{1,0:T(8,128)S(1)} %collective-permute-done.3.yhi_ref, f32[176,128]{1,0:T(8,128)S(1)} %collective-permute-done.4.clo_ref, ...), custom_call_target="tpu_custom_call" | custom-call | tf_op jit(solution)/shard_map/pallas_call | solution.py:529
  39.0 3.5 %collective-permute-start.6 = (f32[15,16,128]{2,1,0:T(8,128)S(1)}, f32[15,16,128]{2,1,0:T(8,128)S(1)}, u32[]{:S(2)}, u32[]{:S(2)}) collective-permute-start(f32[15,16,128]{2,1,0:T(8,128)S(1)} %get-tuple-element.34), channel_id=1, source_target_pairs={{0,1},{1,2},{2,3},{3,4},{4,5},{5,6},{6,7},{7,0},{8,9},{9,10},{10,1... | collective-permute-start | bytes 368648 | tf_op jit(solution)/shard_map/ppermute | solution.py:499
  42.4 0.0 collective-permute-start.7
  42.4 3.1 %shard_map.63 = (f32[27,64,128]{2,1,0:T(8,128)S(1)}, f32[3,232,128]{2,1,0:T(8,128)S(1)}, f32[29,8,128]{2,1,0:T(8,128)S(1)}) custom-call(f32[29,64,128]{2,1,0:T(8,128)S(1)} %get-tuple-element.20.p_ref, f32[58,8,128]{2,1,0:T(8,128)S(1)} %collective-permute-done.xlo_ref, f32[58,8,128]{2,1,0:T(8,128)S(1)} %collective-permute-done.1.xhi_ref, ...), custom_call_target="tpu_custom_call" | custom-call | tf_op jit(solution)/shard_map/pallas_call | solution.py:534
  45.6 0.0 copy-start
  45.6 0.0 collective-permute-done.6.zlo_ref
  45.6 1.1 %collective-permute-done.7.zhi_ref = f32[15,16,128]{2,1,0:T(8,128)S(1)} collective-permute-done((f32[15,16,128]{2,1,0:T(8,128)S(1)}, f32[15,16,128]{2,1,0:T(8,128)S(1)}, u32[]{:S(2)}, u32[]{:S(2)}) %collective-permute-start.7) | collective-permute-done | bytes 122912 | tf_op jit(solution)/shard_map/ppermute | solution.py:499
  46.7 2.4 %shard_map.64 = (f32[27,64,128]{2,1,0:T(8,128)}, f32[8,128]{1,0:T(8,128)S(1)}) custom-call(f32[29,64,128]{2,1,0:T(8,128)S(1)} %get-tuple-element.20.p_ref, f32[27,64,128]{2,1,0:T(8,128)S(1)} %get-tuple-element.29.adv_ref, f32[3,232,128]{2,1,0:T(8,128)S(1)} %get-tuple-element.30.flow_ref, f32[29,8,128]{2,1,0:T(8,128)S(1)} %get-tuple-element.27.main_ref.lmain_ref, ...), custom_call_target="tpu_custom_call" | custom-call | tf_op jit(solution)/shard_map/pallas_call | solution.py:541
  49.1 8.7 %all_to_all.11 = f32[8,1,128]{2,1,0:T(1,128)S(1)} all-to-all(f32[8,1,128]{2,1,0:T(1,128)S(1)} %bitcast.10), channel_id=1, replica_groups=mesh['gx'=8,'gy'=16,'gz'=8] {'gz'}, dimensions={0} | all-to-all | bytes 8192 | tf_op jit(solution)/shard_map/all_to_all | solution.py:555
  57.8 0.0 copy-done
  57.8 0.1 broadcast_in_dim.2.rank_ref
  57.9 0.8 %shard_map.65 = f32[4,4,32]{2,1,0:T(4,128)} custom-call(f32[8,128]{1,0:T(8,128)S(1)} %bitcast.9, s32[8,128]{1,0:T(8,128)S(1)} %broadcast_in_dim.2.rank_ref), custom_call_target="tpu_custom_call" | custom-call | tf_op jit(solution)/shard_map/pallas_call | solution.py:557
Async XLA Ops:
  2.2 27.7 %collective-permute-start = (f32[58,8,128]{2,1,0:T(8,128)S(1)}, f32[58,8,128]{2,1,0:T(8,128)S(1)}, u32[]{:S(2)}, u32[]{:S(2)}) collective-permute-start(f32[58,8,128]{2,1,0:T(8,128)S(1)} %get-tuple-element.21), channel_id=1, source_target_pairs={{0,128},{128,256},{256,384},{384,512},{512,640},{640,768},{768,896... | collective-permute-start | bytes 712712 | tf_op jit(solution)/shard_map/ppermute | solution.py:499
  6.3 23.7 %collective-permute-start.1 = (f32[58,8,128]{2,1,0:T(8,128)S(1)}, f32[58,8,128]{2,1,0:T(8,128)S(1)}, u32[]{:S(2)}, u32[]{:S(2)}) collective-permute-start(f32[58,8,128]{2,1,0:T(8,128)S(1)} %get-tuple-element.22), channel_id=1, source_target_pairs={{128,0},{256,128},{384,256},{512,384},{640,512},{768,640},{896,768... | collective-permute-start | bytes 712712 | tf_op jit(solution)/shard_map/ppermute | solution.py:499
  10.1 27.4 %collective-permute-start.2 = (f32[464,128]{1,0:T(8,128)S(1)}, f32[464,128]{1,0:T(8,128)S(1)}, u32[]{:S(2)}, u32[]{:S(2)}) collective-permute-start(f32[464,128]{1,0:T(8,128)S(1)} %get-tuple-element.23), channel_id=1, source_target_pairs={{0,8},{8,16},{16,24},{24,32},{32,40},{40,48},{48,56},{56,64},{64,7... | collective-permute-start | bytes 712712 | tf_op jit(solution)/shard_map/ppermute | solution.py:499
  14.1 23.4 %collective-permute-start.3 = (f32[464,128]{1,0:T(8,128)S(1)}, f32[464,128]{1,0:T(8,128)S(1)}, u32[]{:S(2)}, u32[]{:S(2)}) collective-permute-start(f32[464,128]{1,0:T(8,128)S(1)} %get-tuple-element.24), channel_id=1, source_target_pairs={{8,0},{16,8},{24,16},{32,24},{40,32},{48,40},{56,48},{64,56},{72,6... | collective-permute-start | bytes 712712 | tf_op jit(solution)/shard_map/ppermute | solution.py:499
  30.1 7.4 %collective-permute-start.4 = (f32[176,128]{1,0:T(8,128)S(1)}, f32[176,128]{1,0:T(8,128)S(1)}, u32[]{:S(2)}, u32[]{:S(2)}) collective-permute-start(f32[176,128]{1,0:T(8,128)S(1)} %get-tuple-element.25), channel_id=1, source_target_pairs={{0,8},{8,16},{16,24},{24,32},{32,40},{40,48},{48,56},{56,64},{64,7... | collective-permute-start | bytes 270344 | tf_op jit(solution)/shard_map/ppermute | solution.py:499
  32.1 6.1 %collective-permute-start.5 = (f32[176,128]{1,0:T(8,128)S(1)}, f32[176,128]{1,0:T(8,128)S(1)}, u32[]{:S(2)}, u32[]{:S(2)}) collective-permute-start(f32[176,128]{1,0:T(8,128)S(1)} %get-tuple-element.26), channel_id=1, source_target_pairs={{8,0},{16,8},{24,16},{32,24},{40,32},{48,40},{56,48},{64,56},{72,6... | collective-permute-start | bytes 270344 | tf_op jit(solution)/shard_map/ppermute | solution.py:499
  39.0 6.6 %collective-permute-start.6 = (f32[15,16,128]{2,1,0:T(8,128)S(1)}, f32[15,16,128]{2,1,0:T(8,128)S(1)}, u32[]{:S(2)}, u32[]{:S(2)}) collective-permute-start(f32[15,16,128]{2,1,0:T(8,128)S(1)} %get-tuple-element.34), channel_id=1, source_target_pairs={{0,1},{1,2},{2,3},{3,4},{4,5},{5,6},{6,7},{7,0},{8,9},{9,10},{10,1... | collective-permute-start | bytes 368648 | tf_op jit(solution)/shard_map/ppermute | solution.py:499
  42.4 4.3 %collective-permute-start.7 = (f32[15,16,128]{2,1,0:T(8,128)S(1)}, f32[15,16,128]{2,1,0:T(8,128)S(1)}, u32[]{:S(2)}, u32[]{:S(2)}) collective-permute-start(f32[15,16,128]{2,1,0:T(8,128)S(1)} %get-tuple-element.35), channel_id=1, source_target_pairs={{1,0},{2,1},{3,2},{4,3},{5,4},{6,5},{7,6},{0,7},{9,8},{10,9},{11,1... | collective-permute-start | bytes 368648 | tf_op jit(solution)/shard_map/ppermute | solution.py:499
  45.6 12.2 %copy-start = (s32[8]{0:T(128)S(1)}, s32[8]{0:T(128)}, u32[]{:S(2)}) copy-start(s32[8]{0:T(128)} %param.7) | copy-start | bytes 100

commit v8 on v7

--- a/solution.py
+++ b/solution.py
@@ -167,11 +167,22 @@
     return p_ref.at[key, pl.ds(x * CELLS, CELLS), :]
 
 
-def second_kernel(xlo_ref, xhi_ref, lo_ref, hi_ref):
-    for inward, out_ref in ((-1, lo_ref), (1, hi_ref)):
-        for k, (key, dist, x) in enumerate(corner_list(inward)):
+def is_even(axis):
+    return lax.axis_index(axis) % 2 == 0
+
+
+def second_kernel(xlo_ref, xhi_ref, a_ref, b_ref):
+    even = is_even("gy")
+    rows = []
+    for inward in (-1, 1):
+        out = []
+        for key, dist, x in corner_list(inward):
             row = dist - 1 if inward < 0 else CELLS - dist
-            out_ref[pl.ds(k, 1), :] = plane_ref(key, x, None, xlo_ref, xhi_ref)[pl.ds(row, 1), :]
+            out.append(plane_ref(key, x, None, xlo_ref, xhi_ref)[pl.ds(row, 1), :])
+        rows.append(out)
+    for k, (lo, hi) in enumerate(zip(*rows)):
+        a_ref[pl.ds(k, 1), :] = jnp.where(even, hi, lo)
+        b_ref[pl.ds(k, 1), :] = jnp.where(even, lo, hi)
 
 
 def pack(tiles):
@@ -213,15 +224,17 @@
     return [jnp.where(upper, turn(value, GROUP, 1), value) for value in pack(tiles)]
 
 
-def third_kernel(ylo_ref, yhi_ref, clo_ref, chi_ref, main_ref, h_ref, z_ref, lo_ref, hi_ref):
-    for inward, in_ref, corner_ref in ((1, ylo_ref, clo_ref), (-1, yhi_ref, chi_ref)):
+def third_kernel(ylo_ref, yhi_ref, ca_ref, cb_ref, main_ref, h_ref, z_ref, lo_ref, hi_ref):
+    even = is_even("gy")
+    for inward, in_ref in ((1, ylo_ref), (-1, yhi_ref)):
         for k, (key, dist) in enumerate(axis_list(1, inward)):
             start = CELLS * REACH + CELLS - dist if inward > 0 else CELLS * (REACH + 1) + dist - 1
             h_ref[key, pl.ds(start, CELLS, stride=CELLS), :] = in_ref[pl.ds(k * CELLS, CELLS), :]
         for k, (key, dist, x) in enumerate(corner_list(inward)):
             plane = x + REACH
             row = CELLS * plane + CELLS - dist if inward > 0 else CELLS * (plane + 1) + dist - 1
-            h_ref[key, pl.ds(row, 1), :] = corner_ref[pl.ds(k, 1), :]
+            one, two = (cb_ref, ca_ref) if inward > 0 else (ca_ref, cb_ref)
+            h_ref[key, pl.ds(row, 1), :] = jnp.where(even, one[pl.ds(k, 1), :], two[pl.ds(k, 1), :])
     halo = pack_halo(h_ref, 3)
     early = lanes_of(CELLS) % GROUP < REACH
     for key in range(29):
@@ -499,6 +512,18 @@
     return lax.ppermute(hi, axis, forward), lax.ppermute(lo, axis, backward)
 
 
+def in_pairs(first, second, axis):
+    count = lax.axis_size(axis)
+    out = []
+    for start, value in ((0, first), (1, second)):
+        pairs = []
+        for i in range(start, count + start, 2):
+            left, right = i % count, (i + 1) % count
+            pairs += [(left, right), (right, left)]
+        out.append(lax.ppermute(value, axis, pairs))
+    return out
+
+
 def body(populations, solid_mask, jet_mask, visibility):
     cells = CELLS * CELLS
     f = populations.reshape(27, cells, LANES)
@@ -521,14 +546,14 @@
     xlo, xhi = both_ways(lo, hi, "gx")
     ylo, yhi = both_ways(down, up, "gy")
     corner_shape = (Y_CORNER, LANES)
-    lo, hi = call(second_kernel, (corner_shape, corner_shape))(xlo, xhi)
-    clo, chi = both_ways(lo, hi, "gy")
+    first, second = call(second_kernel, (corner_shape, corner_shape))(xlo, xhi)
+    first, second = in_pairs(first, second, "gy")
     tile_shape = (29, CELLS, LANES)
     low, high = call(faces_kernel, (tile_shape, tile_shape))(post, xlo, xhi)
     half_shape = (HALF, 2 * CELLS, LANES)
     halo, low_halo, lo, hi = call(
         third_kernel, ((29, (SPAN + 1) * CELLS, LANES), tile_shape, half_shape, half_shape)
-    )(ylo, yhi, clo, chi, low)
+    )(ylo, yhi, first, second, low)
     zlo, zhi = both_ways(lo, hi, "gz")
     height = SPAN * ROWS + CELLS
     moved, flow, high_halo = call(

time: 59 us -> 59.8 us (1.014)
  waiting for transfers between devices: 1.84 us -> 3.15 us
  starting transfers between devices: 37.7 us -> 36.7 us
    ppermute x8 -> x6, starting transfers between devices: 37.7 us -> 31.2 us  [both_ways(): return (lax.ppermute(hi, axis, forward), lax.ppermute(lo, axis, backward))]
    ppermute x0 -> x2, starting transfers between devices: none -> 5.54 us  [in_pairs(): out.append(lax.ppermute(value, axis, pairs))]
    ppermute x0 -> x2, waiting for transfers between devices: none -> 2 us  [in_pairs(): out.append(lax.ppermute(value, axis, pairs))]
    ppermute x8 -> x6, waiting for transfers between devices: 1.84 us -> 1.15 us  [both_ways(): return (lax.ppermute(hi, axis, forward), lax.ppermute(lo, axis, backward))]
where the time goes in v8:
time: 59.8 us; the launch traced here: 59.1 us
  starting transfers between devices  36.7 us (61%)
  Pallas kernels  9.6 us (16%)
  blocking collectives  8.71 us (15%)
  waiting for transfers between devices  3.15 us (5%)
  between operations  0.78 us (1%)
    ppermute x6, starting transfers between devices, both_ways(): return (lax.ppermute(hi, axis, forward), lax.ppermute(lo, axis, backward))  31.2 us
    all_to_all x1, blocking collectives, body(): slabs = lax.all_to_all(slabs, 'gz', 0, 0, tiled=True)  8.71 us
    ppermute x2, starting transfers between devices, in_pairs(): out.append(lax.ppermute(value, axis, pairs))  5.54 us
    pallas_call x1, Pallas kernels, body(): call(steps_kernel, ((27, cells, LANES), (3, height, LANES), tile_shape),...  3.13 us
    pallas_call x1, Pallas kernels, body(): call(render_kernel, ((27, cells, LANES), (CELLS, LANES)), (edge, edge, ed...  2.36 us
    ppermute x2, waiting for transfers between devices, in_pairs(): out.append(lax.ppermute(value, axis, pairs))  2 us
    pallas_call x1, Pallas kernels, body(): call(first_kernel, ((29, cells, LANES), x_shape, x_shape, y_shape, y_shap...  1.61 us
  transfers between devices with their start and end apart: 8, of which 2 were waited for; matrix products, arithmetic and copies ran while one was open for 0% of the time, Pallas kernels for 7%

profile of v8, /device:TPU:1, one launch (start us, length us, event | category | flops | bytes accessed | tf_op | source)
XLA Modules:
  0.0 59.1 jit_solution(12540507032914676374)
XLA Ops:
  0.6 1.6 %shard_map.59 = (f32[29,64,128]{2,1,0:T(8,128)S(1)}, f32[58,8,128]{2,1,0:T(8,128)S(1)}, f32[58,8,128]{2,1,0:T(8,128)S(1)}, f32[464,128]{1,0:T(8,128)S(1)}, f32[464,128]{1,0:T(8,128)S(1)}) custom-call(f32[27,64,128]{2,1,0:T(8,128)} %bitcast.11, s32[64,128]{1,0:T(8,128)} %bitcast.12, s32[64,128]{1,0:T(8,128)} %bitcast.13), custom_call_target="tpu_custom_call" | custom-call | tf_op jit(solution)/shard_map/pallas_call | solution.py:535
  2.2 4.0 %collective-permute-start = (f32[58,8,128]{2,1,0:T(8,128)S(1)}, f32[58,8,128]{2,1,0:T(8,128)S(1)}, u32[]{:S(2)}, u32[]{:S(2)}) collective-permute-start(f32[58,8,128]{2,1,0:T(8,128)S(1)} %get-tuple-element.21), channel_id=1, source_target_pairs={{0,128},{128,256},{256,384},{384,512},{512,640},{640,768},{768,896... | collective-permute-start | bytes 712712 | tf_op jit(solution)/shard_map/ppermute | solution.py:512
  6.3 3.8 %collective-permute-start.1 = (f32[58,8,128]{2,1,0:T(8,128)S(1)}, f32[58,8,128]{2,1,0:T(8,128)S(1)}, u32[]{:S(2)}, u32[]{:S(2)}) collective-permute-start(f32[58,8,128]{2,1,0:T(8,128)S(1)} %get-tuple-element.22), channel_id=1, source_target_pairs={{128,0},{256,128},{384,256},{512,384},{640,512},{768,640},{896,768... | collective-permute-start | bytes 712712 | tf_op jit(solution)/shard_map/ppermute | solution.py:512
  10.1 4.0 %collective-permute-start.2 = (f32[464,128]{1,0:T(8,128)S(1)}, f32[464,128]{1,0:T(8,128)S(1)}, u32[]{:S(2)}, u32[]{:S(2)}) collective-permute-start(f32[464,128]{1,0:T(8,128)S(1)} %get-tuple-element.23), channel_id=1, source_target_pairs={{0,8},{8,16},{16,24},{24,32},{32,40},{40,48},{48,56},{56,64},{64,7... | collective-permute-start | bytes 712712 | tf_op jit(solution)/shard_map/ppermute | solution.py:512
  14.1 15.9 %collective-permute-start.3 = (f32[464,128]{1,0:T(8,128)S(1)}, f32[464,128]{1,0:T(8,128)S(1)}, u32[]{:S(2)}, u32[]{:S(2)}) collective-permute-start(f32[464,128]{1,0:T(8,128)S(1)} %get-tuple-element.24), channel_id=1, source_target_pairs={{8,0},{16,8},{24,16},{32,24},{40,32},{48,40},{56,48},{64,56},{72,6... | collective-permute-start | bytes 712712 | tf_op jit(solution)/shard_map/ppermute | solution.py:512
  30.0 0.0 collective-permute-done.xlo_ref
  30.0 0.0 collective-permute-done.1.xhi_ref
  30.0 0.1 shard_map.60
  30.2 1.9 %collective-permute-start.4 = (f32[176,128]{1,0:T(8,128)S(1)}, f32[176,128]{1,0:T(8,128)S(1)}, u32[]{:S(2)}, u32[]{:S(2)}) collective-permute-start(f32[176,128]{1,0:T(8,128)S(1)} %get-tuple-element.25), channel_id=1, source_target_pairs={{0,8},{8,0},{16,24},{24,16},{32,40},{40,32},{48,56},{56,48},{64,72... | collective-permute-start | bytes 270344 | tf_op jit(solution)/shard_map/ppermute | solution.py:523
  32.1 3.6 %collective-permute-start.5 = (f32[176,128]{1,0:T(8,128)S(1)}, f32[176,128]{1,0:T(8,128)S(1)}, u32[]{:S(2)}, u32[]{:S(2)}) collective-permute-start(f32[176,128]{1,0:T(8,128)S(1)} %get-tuple-element.26), channel_id=1, source_target_pairs={{8,16},{16,8},{24,32},{32,24},{40,48},{48,40},{56,64},{64,56},{72,... | collective-permute-start | bytes 270344 | tf_op jit(solution)/shard_map/ppermute | solution.py:523
  35.7 0.8 %shard_map.61 = (f32[29,8,128]{2,1,0:T(8,128)S(1)}, f32[29,8,128]{2,1,0:T(8,128)S(1)}) custom-call(f32[29,64,128]{2,1,0:T(8,128)S(1)} %get-tuple-element.20.p_ref, f32[58,8,128]{2,1,0:T(8,128)S(1)} %collective-permute-done.xlo_ref, f32[58,8,128]{2,1,0:T(8,128)S(1)} %collective-permute-done.1.xhi_ref), custom_call_target="tpu_custom_call" | custom-call | tf_op jit(solution)/shard_map/pallas_call | solution.py:552
  36.5 0.0 collective-permute-done.2.ylo_ref
  36.5 0.0 collective-permute-done.3.yhi_ref
  36.6 0.0 collective-permute-done.4.ca_ref
  36.6 2.0 %collective-permute-done.5.cb_ref = f32[176,128]{1,0:T(8,128)S(1)} collective-permute-done((f32[176,128]{1,0:T(8,128)S(1)}, f32[176,128]{1,0:T(8,128)S(1)}, u32[]{:S(2)}, u32[]{:S(2)}) %collective-permute-start.5) | collective-permute-done | bytes 90144 | tf_op jit(solution)/shard_map/ppermute | solution.py:523
  38.6 0.8 %shard_map.62 = (f32[29,120,128]{2,1,0:T(8,128)S(1)}, f32[29,8,128]{2,1,0:T(8,128)S(1)}, f32[15,16,128]{2,1,0:T(8,128)S(1)}, f32[15,16,128]{2,1,0:T(8,128)S(1)}) custom-call(f32[464,128]{1,0:T(8,128)S(1)} %collective-permute-done.2.ylo_ref, f32[464,128]{1,0:T(8,128)S(1)} %collective-permute-done.3.yhi_ref, f32[176,128]{1,0:T(8,128)S(1)} %collective-permute-done.4.ca_ref, ...), custom_call_target="tpu_custom_call" | custom-call | tf_op jit(solution)/shard_map/pallas_call | solution.py:554
  39.4 3.5 %collective-permute-start.6 = (f32[15,16,128]{2,1,0:T(8,128)S(1)}, f32[15,16,128]{2,1,0:T(8,128)S(1)}, u32[]{:S(2)}, u32[]{:S(2)}) collective-permute-start(f32[15,16,128]{2,1,0:T(8,128)S(1)} %get-tuple-element.34), channel_id=1, source_target_pairs={{0,1},{1,2},{2,3},{3,4},{4,5},{5,6},{6,7},{7,0},{8,9},{9,10},{10,1... | collective-permute-start | bytes 368648 | tf_op jit(solution)/shard_map/ppermute | solution.py:512
  42.9 0.0 collective-permute-start.7
  42.9 3.1 %shard_map.63 = (f32[27,64,128]{2,1,0:T(8,128)S(1)}, f32[3,232,128]{2,1,0:T(8,128)S(1)}, f32[29,8,128]{2,1,0:T(8,128)S(1)}) custom-call(f32[29,64,128]{2,1,0:T(8,128)S(1)} %get-tuple-element.20.p_ref, f32[58,8,128]{2,1,0:T(8,128)S(1)} %collective-permute-done.xlo_ref, f32[58,8,128]{2,1,0:T(8,128)S(1)} %collective-permute-done.1.xhi_ref, ...), custom_call_target="tpu_custom_call" | custom-call | tf_op jit(solution)/shard_map/pallas_call | solution.py:559
  46.0 0.0 copy-start
  46.0 0.0 collective-permute-done.6.zlo_ref
  46.0 1.1 %collective-permute-done.7.zhi_ref = f32[15,16,128]{2,1,0:T(8,128)S(1)} collective-permute-done((f32[15,16,128]{2,1,0:T(8,128)S(1)}, f32[15,16,128]{2,1,0:T(8,128)S(1)}, u32[]{:S(2)}, u32[]{:S(2)}) %collective-permute-start.7) | collective-permute-done | bytes 122912 | tf_op jit(solution)/shard_map/ppermute | solution.py:512
  47.2 2.4 %shard_map.64 = (f32[27,64,128]{2,1,0:T(8,128)}, f32[8,128]{1,0:T(8,128)S(1)}) custom-call(f32[29,64,128]{2,1,0:T(8,128)S(1)} %get-tuple-element.20.p_ref, f32[27,64,128]{2,1,0:T(8,128)S(1)} %get-tuple-element.29.adv_ref, f32[3,232,128]{2,1,0:T(8,128)S(1)} %get-tuple-element.30.flow_ref, f32[29,8,128]{2,1,0:T(8,128)S(1)} %get-tuple-element.27.main_ref.lmain_ref, ...), custom_call_target="tpu_custom_call" | custom-call | tf_op jit(solution)/shard_map/pallas_call | solution.py:566
  49.5 8.7 %all_to_all.11 = f32[8,1,128]{2,1,0:T(1,128)S(1)} all-to-all(f32[8,1,128]{2,1,0:T(1,128)S(1)} %bitcast.10), channel_id=1, replica_groups=mesh['gx'=8,'gy'=16,'gz'=8] {'gz'}, dimensions={0} | all-to-all | bytes 8192 | tf_op jit(solution)/shard_map/all_to_all | solution.py:580
  58.2 0.0 copy-done
  58.2 0.1 broadcast_in_dim.2.rank_ref
  58.3 0.8 %shard_map.65 = f32[4,4,32]{2,1,0:T(4,128)} custom-call(f32[8,128]{1,0:T(8,128)S(1)} %bitcast.9, s32[8,128]{1,0:T(8,128)S(1)} %broadcast_in_dim.2.rank_ref), custom_call_target="tpu_custom_call" | custom-call | tf_op jit(solution)/shard_map/pallas_call | solution.py:582
Async XLA Ops:
  2.2 27.7 %collective-permute-start = (f32[58,8,128]{2,1,0:T(8,128)S(1)}, f32[58,8,128]{2,1,0:T(8,128)S(1)}, u32[]{:S(2)}, u32[]{:S(2)}) collective-permute-start(f32[58,8,128]{2,1,0:T(8,128)S(1)} %get-tuple-element.21), channel_id=1, source_target_pairs={{0,128},{128,256},{256,384},{384,512},{512,640},{640,768},{768,896... | collective-permute-start | bytes 712712 | tf_op jit(solution)/shard_map/ppermute | solution.py:512
  6.3 23.7 %collective-permute-start.1 = (f32[58,8,128]{2,1,0:T(8,128)S(1)}, f32[58,8,128]{2,1,0:T(8,128)S(1)}, u32[]{:S(2)}, u32[]{:S(2)}) collective-permute-start(f32[58,8,128]{2,1,0:T(8,128)S(1)} %get-tuple-element.22), channel_id=1, source_target_pairs={{128,0},{256,128},{384,256},{512,384},{640,512},{768,640},{896,768... | collective-permute-start | bytes 712712 | tf_op jit(solution)/shard_map/ppermute | solution.py:512
  10.1 26.4 %collective-permute-start.2 = (f32[464,128]{1,0:T(8,128)S(1)}, f32[464,128]{1,0:T(8,128)S(1)}, u32[]{:S(2)}, u32[]{:S(2)}) collective-permute-start(f32[464,128]{1,0:T(8,128)S(1)} %get-tuple-element.23), channel_id=1, source_target_pairs={{0,8},{8,16},{16,24},{24,32},{32,40},{40,48},{48,56},{56,64},{64,7... | collective-permute-start | bytes 712712 | tf_op jit(solution)/shard_map/ppermute | solution.py:512
  14.1 22.4 %collective-permute-start.3 = (f32[464,128]{1,0:T(8,128)S(1)}, f32[464,128]{1,0:T(8,128)S(1)}, u32[]{:S(2)}, u32[]{:S(2)}) collective-permute-start(f32[464,128]{1,0:T(8,128)S(1)} %get-tuple-element.24), channel_id=1, source_target_pairs={{8,0},{16,8},{24,16},{32,24},{40,32},{48,40},{56,48},{64,56},{72,6... | collective-permute-start | bytes 712712 | tf_op jit(solution)/shard_map/ppermute | solution.py:512
  30.2 6.4 %collective-permute-start.4 = (f32[176,128]{1,0:T(8,128)S(1)}, f32[176,128]{1,0:T(8,128)S(1)}, u32[]{:S(2)}, u32[]{:S(2)}) collective-permute-start(f32[176,128]{1,0:T(8,128)S(1)} %get-tuple-element.25), channel_id=1, source_target_pairs={{0,8},{8,0},{16,24},{24,16},{32,40},{40,32},{48,56},{56,48},{64,72... | collective-permute-start | bytes 270344 | tf_op jit(solution)/shard_map/ppermute | solution.py:523
  32.1 6.5 %collective-permute-start.5 = (f32[176,128]{1,0:T(8,128)S(1)}, f32[176,128]{1,0:T(8,128)S(1)}, u32[]{:S(2)}, u32[]{:S(2)}) collective-permute-start(f32[176,128]{1,0:T(8,128)S(1)} %get-tuple-element.26), channel_id=1, source_target_pairs={{8,16},{16,8},{24,32},{32,24},{40,48},{48,40},{56,64},{64,56},{72,... | collective-permute-start | bytes 270344 | tf_op jit(solution)/shard_map/ppermute | solution.py:523
  39.4 6.6 %collective-permute-start.6 = (f32[15,16,128]{2,1,0:T(8,128)S(1)}, f32[15,16,128]{2,1,0:T(8,128)S(1)}, u32[]{:S(2)}, u32[]{:S(2)}) collective-permute-start(f32[15,16,128]{2,1,0:T(8,128)S(1)} %get-tuple-element.34), channel_id=1, source_target_pairs={{0,1},{1,2},{2,3},{3,4},{4,5},{5,6},{6,7},{7,0},{8,9},{9,10},{10,1... | collective-permute-start | bytes 368648 | tf_op jit(solution)/shard_map/ppermute | solution.py:512
  42.9 4.3 %collective-permute-start.7 = (f32[15,16,128]{2,1,0:T(8,128)S(1)}, f32[15,16,128]{2,1,0:T(8,128)S(1)}, u32[]{:S(2)}, u32[]{:S(2)}) collective-permute-start(f32[15,16,128]{2,1,0:T(8,128)S(1)} %get-tuple-element.35), channel_id=1, source_target_pairs={{1,0},{2,1},{3,2},{4,3},{5,4},{6,5},{7,6},{0,7},{9,8},{10,9},{11,1... | collective-permute-start | bytes 368648 | tf_op jit(solution)/shard_map/ppermute | solution.py:512
  46.0 12.2 %copy-start = (s32[8]{0:T(128)S(1)}, s32[8]{0:T(128)}, u32[]{:S(2)}) copy-start(s32[8]{0:T(128)} %param.7) | copy-start | bytes 100

commit v9 on v6

--- a/solution.py
+++ b/solution.py
@@ -36,26 +36,26 @@
     return out
 
 
-def held(key, cell, axis=0):
-    dist, inward = (-cell, 1) if cell < 0 else (cell - CELLS + 1, -1)
+def held(key, x):
+    dist, inward = (-x, 1) if x < 0 else (x - CELLS + 1, -1)
     if dist <= 0:
         return True
-    return (key, dist) in axis_list(axis, inward)
+    return (key, dist) in axis_list(0, inward)
 
 
 def corner_list(inward):
     out = []
-    for key, dist in axis_list(0, inward):
+    for key, dist in axis_list(1, inward):
         first, second = (0, 0) if key in MASKS else DIRS[key][:2]
-        for y in (-3, -2, -1, 8, 9, 10):
-            far = -(y + second) if y < 0 else y + second - CELLS + 1
-            if held(key, y, 1) and not (far >= 2 and dist - inward * first >= 2):
-                out.append((key, dist, y))
+        for x in (-3, -2, -1, 8, 9, 10):
+            far = -(x + first) if x < 0 else x + first - CELLS + 1
+            if held(key, x) and not (far >= 2 and dist - inward * second >= 2):
+                out.append((key, dist, x))
     return out
 
 
 X_COUNT = len(axis_list(0, 1))
-CORNER = -(-len(corner_list(1)) // 8) * 8
+Y_CORNER = -(-len(corner_list(1)) // 8) * 8
 
 
 def moments(f):
@@ -178,13 +178,13 @@
     return p_ref[key, pl.ds(x * CELLS, CELLS), :]
 
 
-def second_kernel(ya_ref, yb_ref, lo_ref, hi_ref):
-    even = is_even("gy")
+def second_kernel(xa_ref, xb_ref, lo_ref, hi_ref):
+    even = is_even("gx")
     for inward, out_ref in ((-1, lo_ref), (1, hi_ref)):
-        for k, (key, dist, y) in enumerate(corner_list(inward)):
+        for k, (key, dist, x) in enumerate(corner_list(inward)):
             row = pl.ds(dist - 1 if inward < 0 else CELLS - dist, 1)
-            side, far = (1, -y) if y < 0 else (-1, y - CELLS + 1)
-            out_ref[pl.ds(k, 1), :] = from_pair(1, side, far, key, ya_ref, yb_ref, even, row)
+            side, far = (1, -x) if x < 0 else (-1, x - CELLS + 1)
+            out_ref[pl.ds(k, 1), :] = from_pair(0, side, far, key, xa_ref, xb_ref, even, row)
 
 
 def pack(tiles):
@@ -230,14 +230,13 @@
 
 def third_kernel(ya_ref, yb_ref, clo_ref, chi_ref, main_ref, h_ref, z_ref, lo_ref, hi_ref):
     even = is_even("gy")
-    for inward in (1, -1):
-        for key, dist in axis_list(1, inward):
+    for inward, corner_ref in ((1, clo_ref), (-1, chi_ref)):
+        for k, (key, dist) in enumerate(axis_list(1, inward)):
             start = CELLS * REACH + CELLS - dist if inward > 0 else CELLS * (REACH + 1) + dist - 1
             h_ref[key, pl.ds(start, CELLS, stride=CELLS), :] = from_pair(1, inward, dist, key, ya_ref, yb_ref, even)
-    for inward, corner_ref in ((1, clo_ref), (-1, chi_ref)):
-        for k, (key, dist, y) in enumerate(corner_list(inward)):
-            plane = REACH - dist if inward > 0 else REACH + CELLS - 1 + dist
-            row = CELLS * plane + CELLS + y if y < 0 else CELLS * (plane + 1) + y - CELLS
+        for k, (key, dist, x) in enumerate(corner_list(inward)):
+            plane = x + REACH
+            row = CELLS * plane + CELLS - dist if inward > 0 else CELLS * (plane + 1) + dist - 1
             h_ref[key, pl.ds(row, 1), :] = corner_ref[pl.ds(k, 1), :]
     halo = pack_halo(h_ref, 3)
     early = lanes_of(CELLS) % GROUP < REACH
@@ -549,10 +548,9 @@
     )(f, solid, jet)
     xa, xb = in_pairs(xa, xb, "gx")
     ya, yb = in_pairs(ya, yb, "gy")
-    xa, xb, ya, yb = lax.optimization_barrier((xa, xb, ya, yb))
-    corner_shape = (CORNER, LANES)
-    lo, hi = call(second_kernel, (corner_shape, corner_shape))(ya, yb)
-    clo, chi = both_ways(lo, hi, "gx")
+    corner_shape = (Y_CORNER, LANES)
+    lo, hi = call(second_kernel, (corner_shape, corner_shape))(xa, xb)
+    clo, chi = both_ways(lo, hi, "gy")
     tile_shape = (29, CELLS, LANES)
     low, high = call(faces_kernel, (tile_shape, tile_shape))(post, xa, xb)
     half_shape = (HALF, 2 * CELLS, LANES)

time: 65.8 us -> 60.9 us (0.926)
  waiting for transfers between devices: 6.3 us -> 1.78 us
    ppermute x4, waiting for transfers between devices: 4.53 us -> 0.01 us  [in_pairs(): out.append(lax.ppermute(value, axis, pairs))]
  transfers between devices with their start and end apart: 8 -> 8, of which waited for: 3 -> 2; matrix products, arithmetic and copies ran while one was open for 0% -> 0% of each run, Pallas kernels for 6% -> 7%
where the time goes in v9:
time: 60.9 us; the launch traced here: 60.6 us
  starting transfers between devices  39.6 us (65%)
  Pallas kernels  9.66 us (16%)
  blocking collectives  8.71 us (14%)
  waiting for transfers between devices  1.78 us (3%)
  between operations  0.78 us (1%)
    ppermute x4, starting transfers between devices, in_pairs(): out.append(lax.ppermute(value, axis, pairs))  29 us
    ppermute x4, starting transfers between devices, both_ways(): return (lax.ppermute(hi, axis, forward), lax.ppermute(lo, axis, backward))  10.5 us
    all_to_all x1, blocking collectives, body(): slabs = lax.all_to_all(slabs, 'gz', 0, 0, tiled=True)  8.71 us
    pallas_call x1, Pallas kernels, body(): call(steps_kernel, ((27, cells, LANES), (3, height, LANES), tile_shape),...  3.16 us
    pallas_call x1, Pallas kernels, body(): call(render_kernel, ((27, cells, LANES), (CELLS, LANES)), (edge, edge, ed...  2.36 us
    ppermute x4, waiting for transfers between devices, both_ways(): return (lax.ppermute(hi, axis, forward), lax.ppermute(lo, axis, backward))  1.77 us
    pallas_call x1, Pallas kernels, body(): call(first_kernel, ((29, cells, LANES),) + (send_shape,) * 4, (pltpu.VMEM...  1.61 us
  transfers between devices with their start and end apart: 8, of which 2 were waited for; matrix products, arithmetic and copies ran while one was open for 0% of the time, Pallas kernels for 7%

profile of v9, /device:TPU:1, one launch (start us, length us, event | category | flops | bytes accessed | tf_op | source)
XLA Modules:
  0.0 60.6 jit_solution(13035430606515918722)
XLA Ops:
  0.6 1.6 %shard_map.59 = (f32[29,64,128]{2,1,0:T(8,128)S(1)}, f32[58,8,128]{2,1,0:T(8,128)S(1)}, f32[58,8,128]{2,1,0:T(8,128)S(1)}, f32[58,8,128]{2,1,0:T(8,128)S(1)}, f32[58,8,128]{2,1,0:T(8,128)S(1)}) custom-call(f32[27,64,128]{2,1,0:T(8,128)} %bitcast.11, s32[64,128]{1,0:T(8,128)} %bitcast.12, s32[64,128]{1,0:T(8,128)} %bitcast.13), custom_call_target="tpu_custom_call" | custom-call | tf_op jit(solution)/shard_map/pallas_call | solution.py:538
  2.2 4.0 %collective-permute-start = (f32[58,8,128]{2,1,0:T(8,128)S(1)}, f32[58,8,128]{2,1,0:T(8,128)S(1)}, u32[]{:S(2)}, u32[]{:S(2)}) collective-permute-start(f32[58,8,128]{2,1,0:T(8,128)S(1)} %get-tuple-element.21), channel_id=1, source_target_pairs={{0,128},{128,0},{256,384},{384,256},{512,640},{640,512},{768,896},... | collective-permute-start | bytes 712712 | tf_op jit(solution)/shard_map/ppermute | solution.py:527
  6.3 4.9 %collective-permute-start.1 = (f32[58,8,128]{2,1,0:T(8,128)S(1)}, f32[58,8,128]{2,1,0:T(8,128)S(1)}, u32[]{:S(2)}, u32[]{:S(2)}) collective-permute-start(f32[58,8,128]{2,1,0:T(8,128)S(1)} %get-tuple-element.22), channel_id=1, source_target_pairs={{128,256},{256,128},{384,512},{512,384},{640,768},{768,640},{896,0... | collective-permute-start | bytes 712712 | tf_op jit(solution)/shard_map/ppermute | solution.py:527
  11.2 4.0 %collective-permute-start.2 = (f32[58,8,128]{2,1,0:T(8,128)S(1)}, f32[58,8,128]{2,1,0:T(8,128)S(1)}, u32[]{:S(2)}, u32[]{:S(2)}) collective-permute-start(f32[58,8,128]{2,1,0:T(8,128)S(1)} %get-tuple-element.23), channel_id=1, source_target_pairs={{0,8},{8,0},{16,24},{24,16},{32,40},{40,32},{48,56},{56,48},{64,72... | collective-permute-start | bytes 712712 | tf_op jit(solution)/shard_map/ppermute | solution.py:527
  15.2 16.1 %collective-permute-start.3 = (f32[58,8,128]{2,1,0:T(8,128)S(1)}, f32[58,8,128]{2,1,0:T(8,128)S(1)}, u32[]{:S(2)}, u32[]{:S(2)}) collective-permute-start(f32[58,8,128]{2,1,0:T(8,128)S(1)} %get-tuple-element.24), channel_id=1, source_target_pairs={{8,16},{16,8},{24,32},{32,24},{40,48},{48,40},{56,64},{64,56},{72,... | collective-permute-start | bytes 712712 | tf_op jit(solution)/shard_map/ppermute | solution.py:527
  31.3 0.0 collective-permute-done.xa_ref
  31.3 0.0 collective-permute-done.1.xb_ref
  31.3 0.2 shard_map.60
  31.5 1.9 %collective-permute-start.4 = (f32[176,128]{1,0:T(8,128)S(1)}, f32[176,128]{1,0:T(8,128)S(1)}, u32[]{:S(2)}, u32[]{:S(2)}) collective-permute-start(f32[176,128]{1,0:T(8,128)S(1)} %get-tuple-element.25), channel_id=1, source_target_pairs={{0,8},{8,16},{16,24},{24,32},{32,40},{40,48},{48,56},{56,64},{64,7... | collective-permute-start | bytes 270344 | tf_op jit(solution)/shard_map/ppermute | solution.py:516
  33.4 4.6 %collective-permute-start.5 = (f32[176,128]{1,0:T(8,128)S(1)}, f32[176,128]{1,0:T(8,128)S(1)}, u32[]{:S(2)}, u32[]{:S(2)}) collective-permute-start(f32[176,128]{1,0:T(8,128)S(1)} %get-tuple-element.26), channel_id=1, source_target_pairs={{8,0},{16,8},{24,16},{32,24},{40,32},{48,40},{56,48},{64,56},{72,6... | collective-permute-start | bytes 270344 | tf_op jit(solution)/shard_map/ppermute | solution.py:516
  38.0 0.8 %shard_map.61 = (f32[29,8,128]{2,1,0:T(8,128)S(1)}, f32[29,8,128]{2,1,0:T(8,128)S(1)}) custom-call(f32[29,64,128]{2,1,0:T(8,128)S(1)} %get-tuple-element.20.p_ref, f32[58,8,128]{2,1,0:T(8,128)S(1)} %collective-permute-done.xa_ref, f32[58,8,128]{2,1,0:T(8,128)S(1)} %collective-permute-done.1.xb_ref), custom_call_target="tpu_custom_call" | custom-call | tf_op jit(solution)/shard_map/pallas_call | solution.py:555
  38.8 0.0 collective-permute-done.2.ya_ref
  38.9 0.0 collective-permute-done.3.yb_ref
  38.9 0.0 collective-permute-done.4.clo_ref
  38.9 0.7 %collective-permute-done.5.chi_ref = f32[176,128]{1,0:T(8,128)S(1)} collective-permute-done((f32[176,128]{1,0:T(8,128)S(1)}, f32[176,128]{1,0:T(8,128)S(1)}, u32[]{:S(2)}, u32[]{:S(2)}) %collective-permute-start.5) | collective-permute-done | bytes 90144 | tf_op jit(solution)/shard_map/ppermute | solution.py:516
  39.5 0.8 %shard_map.62 = (f32[29,120,128]{2,1,0:T(8,128)S(1)}, f32[29,8,128]{2,1,0:T(8,128)S(1)}, f32[15,16,128]{2,1,0:T(8,128)S(1)}, f32[15,16,128]{2,1,0:T(8,128)S(1)}) custom-call(f32[58,8,128]{2,1,0:T(8,128)S(1)} %collective-permute-done.2.ya_ref, f32[58,8,128]{2,1,0:T(8,128)S(1)} %collective-permute-done.3.yb_ref, ...), custom_call_target="tpu_custom_call" | custom-call | tf_op jit(solution)/shard_map/pallas_call | solution.py:557
  40.3 4.0 %collective-permute-start.6 = (f32[15,16,128]{2,1,0:T(8,128)S(1)}, f32[15,16,128]{2,1,0:T(8,128)S(1)}, u32[]{:S(2)}, u32[]{:S(2)}) collective-permute-start(f32[15,16,128]{2,1,0:T(8,128)S(1)} %get-tuple-element.34), channel_id=1, source_target_pairs={{0,1},{1,2},{2,3},{3,4},{4,5},{5,6},{6,7},{7,0},{8,9},{9,10},{10,1... | collective-permute-start | bytes 368648 | tf_op jit(solution)/shard_map/ppermute | solution.py:516
  44.3 0.0 collective-permute-start.7
  44.3 3.2 %shard_map.63 = (f32[27,64,128]{2,1,0:T(8,128)S(1)}, f32[3,232,128]{2,1,0:T(8,128)S(1)}, f32[29,8,128]{2,1,0:T(8,128)S(1)}) custom-call(f32[29,64,128]{2,1,0:T(8,128)S(1)} %get-tuple-element.20.p_ref, f32[58,8,128]{2,1,0:T(8,128)S(1)} %collective-permute-done.xa_ref, f32[58,8,128]{2,1,0:T(8,128)S(1)} %collective-permute-done.1.xb_ref, ...), custom_call_target="tpu_custom_call" | custom-call | tf_op jit(solution)/shard_map/pallas_call | solution.py:562
  47.5 0.0 copy-start
  47.5 0.0 collective-permute-done.6.zlo_ref
  47.5 1.1 %collective-permute-done.7.zhi_ref = f32[15,16,128]{2,1,0:T(8,128)S(1)} collective-permute-done((f32[15,16,128]{2,1,0:T(8,128)S(1)}, f32[15,16,128]{2,1,0:T(8,128)S(1)}, u32[]{:S(2)}, u32[]{:S(2)}) %collective-permute-start.7) | collective-permute-done | bytes 122912 | tf_op jit(solution)/shard_map/ppermute | solution.py:516
  48.6 2.4 %shard_map.64 = (f32[27,64,128]{2,1,0:T(8,128)}, f32[8,128]{1,0:T(8,128)S(1)}) custom-call(f32[29,64,128]{2,1,0:T(8,128)S(1)} %get-tuple-element.20.p_ref, f32[27,64,128]{2,1,0:T(8,128)S(1)} %get-tuple-element.29.adv_ref, f32[3,232,128]{2,1,0:T(8,128)S(1)} %get-tuple-element.30.flow_ref, f32[29,8,128]{2,1,0:T(8,128)S(1)} %get-tuple-element.27.main_ref.lmain_ref, ...), custom_call_target="tpu_custom_call" | custom-call | tf_op jit(solution)/shard_map/pallas_call | solution.py:569
  51.0 8.7 %all_to_all.11 = f32[8,1,128]{2,1,0:T(1,128)S(1)} all-to-all(f32[8,1,128]{2,1,0:T(1,128)S(1)} %bitcast.10), channel_id=1, replica_groups=mesh['gx'=8,'gy'=16,'gz'=8] {'gz'}, dimensions={0} | all-to-all | bytes 8192 | tf_op jit(solution)/shard_map/all_to_all | solution.py:583
  59.7 0.0 copy-done
  59.7 0.1 broadcast_in_dim.2.rank_ref
  59.8 0.8 %shard_map.65 = f32[4,4,32]{2,1,0:T(4,128)} custom-call(f32[8,128]{1,0:T(8,128)S(1)} %bitcast.9, s32[8,128]{1,0:T(8,128)S(1)} %broadcast_in_dim.2.rank_ref), custom_call_target="tpu_custom_call" | custom-call | tf_op jit(solution)/shard_map/pallas_call | solution.py:585
Async XLA Ops:
  2.2 29.1 %collective-permute-start = (f32[58,8,128]{2,1,0:T(8,128)S(1)}, f32[58,8,128]{2,1,0:T(8,128)S(1)}, u32[]{:S(2)}, u32[]{:S(2)}) collective-permute-start(f32[58,8,128]{2,1,0:T(8,128)S(1)} %get-tuple-element.21), channel_id=1, source_target_pairs={{0,128},{128,0},{256,384},{384,256},{512,640},{640,512},{768,896},... | collective-permute-start | bytes 712712 | tf_op jit(solution)/shard_map/ppermute | solution.py:527
  6.3 25.0 %collective-permute-start.1 = (f32[58,8,128]{2,1,0:T(8,128)S(1)}, f32[58,8,128]{2,1,0:T(8,128)S(1)}, u32[]{:S(2)}, u32[]{:S(2)}) collective-permute-start(f32[58,8,128]{2,1,0:T(8,128)S(1)} %get-tuple-element.22), channel_id=1, source_target_pairs={{128,256},{256,128},{384,512},{512,384},{640,768},{768,640},{896,0... | collective-permute-start | bytes 712712 | tf_op jit(solution)/shard_map/ppermute | solution.py:527
  11.2 27.7 %collective-permute-start.2 = (f32[58,8,128]{2,1,0:T(8,128)S(1)}, f32[58,8,128]{2,1,0:T(8,128)S(1)}, u32[]{:S(2)}, u32[]{:S(2)}) collective-permute-start(f32[58,8,128]{2,1,0:T(8,128)S(1)} %get-tuple-element.23), channel_id=1, source_target_pairs={{0,8},{8,0},{16,24},{24,16},{32,40},{40,32},{48,56},{56,48},{64,72... | collective-permute-start | bytes 712712 | tf_op jit(solution)/shard_map/ppermute | solution.py:527
  15.2 23.7 %collective-permute-start.3 = (f32[58,8,128]{2,1,0:T(8,128)S(1)}, f32[58,8,128]{2,1,0:T(8,128)S(1)}, u32[]{:S(2)}, u32[]{:S(2)}) collective-permute-start(f32[58,8,128]{2,1,0:T(8,128)S(1)} %get-tuple-element.24), channel_id=1, source_target_pairs={{8,16},{16,8},{24,32},{32,24},{40,48},{48,40},{56,64},{64,56},{72,... | collective-permute-start | bytes 712712 | tf_op jit(solution)/shard_map/ppermute | solution.py:527
  31.5 7.4 %collective-permute-start.4 = (f32[176,128]{1,0:T(8,128)S(1)}, f32[176,128]{1,0:T(8,128)S(1)}, u32[]{:S(2)}, u32[]{:S(2)}) collective-permute-start(f32[176,128]{1,0:T(8,128)S(1)} %get-tuple-element.25), channel_id=1, source_target_pairs={{0,8},{8,16},{16,24},{24,32},{32,40},{40,48},{48,56},{56,64},{64,7... | collective-permute-start | bytes 270344 | tf_op jit(solution)/shard_map/ppermute | solution.py:516
  33.4 6.1 %collective-permute-start.5 = (f32[176,128]{1,0:T(8,128)S(1)}, f32[176,128]{1,0:T(8,128)S(1)}, u32[]{:S(2)}, u32[]{:S(2)}) collective-permute-start(f32[176,128]{1,0:T(8,128)S(1)} %get-tuple-element.26), channel_id=1, source_target_pairs={{8,0},{16,8},{24,16},{32,24},{40,32},{48,40},{56,48},{64,56},{72,6... | collective-permute-start | bytes 270344 | tf_op jit(solution)/shard_map/ppermute | solution.py:516
  40.3 7.2 %collective-permute-start.6 = (f32[15,16,128]{2,1,0:T(8,128)S(1)}, f32[15,16,128]{2,1,0:T(8,128)S(1)}, u32[]{:S(2)}, u32[]{:S(2)}) collective-permute-start(f32[15,16,128]{2,1,0:T(8,128)S(1)} %get-tuple-element.34), channel_id=1, source_target_pairs={{0,1},{1,2},{2,3},{3,4},{4,5},{5,6},{6,7},{7,0},{8,9},{9,10},{10,1... | collective-permute-start | bytes 368648 | tf_op jit(solution)/shard_map/ppermute | solution.py:516
  44.3 4.3 %collective-permute-start.7 = (f32[15,16,128]{2,1,0:T(8,128)S(1)}, f32[15,16,128]{2,1,0:T(8,128)S(1)}, u32[]{:S(2)}, u32[]{:S(2)}) collective-permute-start(f32[15,16,128]{2,1,0:T(8,128)S(1)} %get-tuple-element.35), channel_id=1, source_target_pairs={{1,0},{2,1},{3,2},{4,3},{5,4},{6,5},{7,6},{0,7},{9,8},{10,9},{11,1... | collective-permute-start | bytes 368648 | tf_op jit(solution)/shard_map/ppermute | solution.py:516
  47.5 12.2 %copy-start = (s32[8]{0:T(128)S(1)}, s32[8]{0:T(128)}, u32[]{:S(2)}) copy-start(s32[8]{0:T(128)} %param.7) | copy-start | bytes 100

commit v10 on v7

--- a/solution.py
+++ b/solution.py
@@ -121,8 +121,12 @@
     return pltpu.roll(value, shift, axis)
 
 
+def is_even(axis):
+    return lax.axis_index(axis) % 2 == 0
+
+
 def first_kernel(
-    f_hbm, solid_hbm, jet_hbm, p_ref, lo_ref, hi_ref, ylo_ref, yhi_ref, f_ref, solid_ref, jet_ref, sems
+    f_hbm, solid_hbm, jet_hbm, p_ref, lo_ref, hi_ref, ya_ref, yb_ref, f_ref, solid_ref, jet_ref, sems
 ):
     masks = [
         pltpu.make_async_copy(solid_hbm, solid_ref, sems.at[CELLS]),
@@ -149,10 +153,13 @@
         lo_ref[k] = p_ref[key, pl.ds((dist - 1) * CELLS, CELLS), :]
     for k, (key, dist) in enumerate(axis_list(0, 1)):
         hi_ref[k] = p_ref[key, pl.ds((CELLS - dist) * CELLS, CELLS), :]
-    for inward, out_ref in ((-1, ylo_ref), (1, yhi_ref)):
-        for k, (key, dist) in enumerate(axis_list(1, inward)):
-            row = dist - 1 if inward < 0 else CELLS - dist
-            out_ref[pl.ds(k * CELLS, CELLS), :] = p_ref[key, pl.ds(row, CELLS, stride=CELLS), :]
+    even = is_even("gy")
+    for k, (low, high) in enumerate(zip(axis_list(1, -1), axis_list(1, 1))):
+        rows = pl.ds(k * CELLS, CELLS)
+        lo = p_ref[low[0], pl.ds(low[1] - 1, CELLS, stride=CELLS), :]
+        hi = p_ref[high[0], pl.ds(CELLS - high[1], CELLS, stride=CELLS), :]
+        ya_ref[rows, :] = jnp.where(even, hi, lo)
+        yb_ref[rows, :] = jnp.where(even, lo, hi)
 
 
 LOW_AT = {entry: k for k, entry in enumerate(axis_list(0, 1))}
@@ -213,11 +220,14 @@
     return [jnp.where(upper, turn(value, GROUP, 1), value) for value in pack(tiles)]
 
 
-def third_kernel(ylo_ref, yhi_ref, clo_ref, chi_ref, main_ref, h_ref, z_ref, lo_ref, hi_ref):
-    for inward, in_ref, corner_ref in ((1, ylo_ref, clo_ref), (-1, yhi_ref, chi_ref)):
+def third_kernel(ya_ref, yb_ref, clo_ref, chi_ref, main_ref, h_ref, z_ref, lo_ref, hi_ref):
+    even = is_even("gy")
+    for inward, one_ref, two_ref, corner_ref in ((1, yb_ref, ya_ref, clo_ref), (-1, ya_ref, yb_ref, chi_ref)):
         for k, (key, dist) in enumerate(axis_list(1, inward)):
             start = CELLS * REACH + CELLS - dist if inward > 0 else CELLS * (REACH + 1) + dist - 1
-            h_ref[key, pl.ds(start, CELLS, stride=CELLS), :] = in_ref[pl.ds(k * CELLS, CELLS), :]
+            h_ref[key, pl.ds(start, CELLS, stride=CELLS), :] = jnp.where(
+                even, one_ref[pl.ds(k * CELLS, CELLS), :], two_ref[pl.ds(k * CELLS, CELLS), :]
+            )
         for k, (key, dist, x) in enumerate(corner_list(inward)):
             plane = x + REACH
             row = CELLS * plane + CELLS - dist if inward > 0 else CELLS * (plane + 1) + dist - 1
@@ -499,6 +509,18 @@
     return lax.ppermute(hi, axis, forward), lax.ppermute(lo, axis, backward)
 
 
+def in_pairs(first, second, axis):
+    count = lax.axis_size(axis)
+    out = []
+    for start, value in ((0, first), (1, second)):
+        pairs = []
+        for i in range(start, count + start, 2):
+            left, right = i % count, (i + 1) % count
+            pairs += [(left, right), (right, left)]
+        out.append(lax.ppermute(value, axis, pairs))
+    return out
+
+
 def body(populations, solid_mask, jet_mask, visibility):
     cells = CELLS * CELLS
     f = populations.reshape(27, cells, LANES)
@@ -507,7 +529,7 @@
     f, solid, jet = [pltpu.with_memory_space_constraint(value, pltpu.HBM) for value in (f, solid, jet)]
     x_shape = (X_COUNT, CELLS, LANES)
     y_shape = (Y_OWN, LANES)
-    post, lo, hi, down, up = call(
+    post, lo, hi, ya, yb = call(
         first_kernel,
         ((29, cells, LANES), x_shape, x_shape, y_shape, y_shape),
         (
@@ -519,7 +541,7 @@
         in_hbm=True,
     )(f, solid, jet)
     xlo, xhi = both_ways(lo, hi, "gx")
-    ylo, yhi = both_ways(down, up, "gy")
+    ya, yb = in_pairs(ya, yb, "gy")
     corner_shape = (Y_CORNER, LANES)
     lo, hi = call(second_kernel, (corner_shape, corner_shape))(xlo, xhi)
     clo, chi = both_ways(lo, hi, "gy")
@@ -528,7 +550,7 @@
     half_shape = (HALF, 2 * CELLS, LANES)
     halo, low_halo, lo, hi = call(
         third_kernel, ((29, (SPAN + 1) * CELLS, LANES), tile_shape, half_shape, half_shape)
-    )(ylo, yhi, clo, chi, low)
+    )(ya, yb, clo, chi, low)
     zlo, zhi = both_ways(lo, hi, "gz")
     height = SPAN * ROWS + CELLS
     moved, flow, high_halo = call(

time: 59 us -> 59.5 us (level)
    ppermute x0 -> x2, starting transfers between devices: none -> 20.1 us  [in_pairs(): out.append(lax.ppermute(value, axis, pairs))]
    ppermute x8 -> x6, starting transfers between devices: 37.7 us -> 18.1 us  [both_ways(): return (lax.ppermute(hi, axis, forward), lax.ppermute(lo, axis, backward))]
    ppermute x8 -> x6, waiting for transfers between devices: 1.84 us -> 1.84 us  [both_ways(): return (lax.ppermute(hi, axis, forward), lax.ppermute(lo, axis, backward))]
where the time goes in v10:
time: 59.5 us; the launch traced here: 59.2 us
  starting transfers between devices  38.2 us (64%)
  Pallas kernels  9.56 us (16%)
  blocking collectives  8.71 us (15%)
  waiting for transfers between devices  1.84 us (3%)
  between operations  0.78 us (1%)
    ppermute x2, starting transfers between devices, in_pairs(): out.append(lax.ppermute(value, axis, pairs))  20.1 us
    ppermute x6, starting transfers between devices, both_ways(): return (lax.ppermute(hi, axis, forward), lax.ppermute(lo, axis, backward))  18.1 us
    all_to_all x1, blocking collectives, body(): slabs = lax.all_to_all(slabs, 'gz', 0, 0, tiled=True)  8.71 us
    pallas_call x1, Pallas kernels, body(): call(steps_kernel, ((27, cells, LANES), (3, height, LANES), tile_shape),...  3.13 us
    pallas_call x1, Pallas kernels, body(): call(render_kernel, ((27, cells, LANES), (CELLS, LANES)), (edge, edge, ed...  2.36 us
    ppermute x6, waiting for transfers between devices, both_ways(): return (lax.ppermute(hi, axis, forward), lax.ppermute(lo, axis, backward))  1.84 us
    pallas_call x1, Pallas kernels, body(): call(first_kernel, ((29, cells, LANES), x_shape, x_shape, y_shape, y_shap...  1.6 us
  transfers between devices with their start and end apart: 8, of which 2 were waited for; matrix products, arithmetic and copies ran while one was open for 0% of the time, Pallas kernels for 7%

profile of v10, /device:TPU:1, one launch (start us, length us, event | category | flops | bytes accessed | tf_op | source)
XLA Modules:
  0.0 59.2 jit_solution(4713164567200085727)
XLA Ops:
  0.6 1.6 %shard_map.59 = (f32[29,64,128]{2,1,0:T(8,128)S(1)}, f32[58,8,128]{2,1,0:T(8,128)S(1)}, f32[58,8,128]{2,1,0:T(8,128)S(1)}, f32[464,128]{1,0:T(8,128)S(1)}, f32[464,128]{1,0:T(8,128)S(1)}) custom-call(f32[27,64,128]{2,1,0:T(8,128)} %bitcast.11, s32[64,128]{1,0:T(8,128)} %bitcast.12, s32[64,128]{1,0:T(8,128)} %bitcast.13), custom_call_target="tpu_custom_call" | custom-call | tf_op jit(solution)/shard_map/pallas_call | solution.py:532
  2.2 4.0 %collective-permute-start = (f32[58,8,128]{2,1,0:T(8,128)S(1)}, f32[58,8,128]{2,1,0:T(8,128)S(1)}, u32[]{:S(2)}, u32[]{:S(2)}) collective-permute-start(f32[58,8,128]{2,1,0:T(8,128)S(1)} %get-tuple-element.21), channel_id=1, source_target_pairs={{0,128},{128,256},{256,384},{384,512},{512,640},{640,768},{768,896... | collective-permute-start | bytes 712712 | tf_op jit(solution)/shard_map/ppermute | solution.py:509
  6.3 3.8 %collective-permute-start.1 = (f32[58,8,128]{2,1,0:T(8,128)S(1)}, f32[58,8,128]{2,1,0:T(8,128)S(1)}, u32[]{:S(2)}, u32[]{:S(2)}) collective-permute-start(f32[58,8,128]{2,1,0:T(8,128)S(1)} %get-tuple-element.22), channel_id=1, source_target_pairs={{128,0},{256,128},{384,256},{512,384},{640,512},{768,640},{896,768... | collective-permute-start | bytes 712712 | tf_op jit(solution)/shard_map/ppermute | solution.py:509
  10.1 4.0 %collective-permute-start.2 = (f32[464,128]{1,0:T(8,128)S(1)}, f32[464,128]{1,0:T(8,128)S(1)}, u32[]{:S(2)}, u32[]{:S(2)}) collective-permute-start(f32[464,128]{1,0:T(8,128)S(1)} %get-tuple-element.23), channel_id=1, source_target_pairs={{0,8},{8,0},{16,24},{24,16},{32,40},{40,32},{48,56},{56,48},{64,72... | collective-permute-start | bytes 712712 | tf_op jit(solution)/shard_map/ppermute | solution.py:520
  14.1 16.1 %collective-permute-start.3 = (f32[464,128]{1,0:T(8,128)S(1)}, f32[464,128]{1,0:T(8,128)S(1)}, u32[]{:S(2)}, u32[]{:S(2)}) collective-permute-start(f32[464,128]{1,0:T(8,128)S(1)} %get-tuple-element.24), channel_id=1, source_target_pairs={{8,16},{16,8},{24,32},{32,24},{40,48},{48,40},{56,64},{64,56},{72,... | collective-permute-start | bytes 712712 | tf_op jit(solution)/shard_map/ppermute | solution.py:520
  30.2 0.0 collective-permute-done.xlo_ref
  30.3 0.0 collective-permute-done.1.xhi_ref
  30.3 0.1 shard_map.60
  30.4 1.9 %collective-permute-start.4 = (f32[176,128]{1,0:T(8,128)S(1)}, f32[176,128]{1,0:T(8,128)S(1)}, u32[]{:S(2)}, u32[]{:S(2)}) collective-permute-start(f32[176,128]{1,0:T(8,128)S(1)} %get-tuple-element.25), channel_id=1, source_target_pairs={{0,8},{8,16},{16,24},{24,32},{32,40},{40,48},{48,56},{56,64},{64,7... | collective-permute-start | bytes 270344 | tf_op jit(solution)/shard_map/ppermute | solution.py:509
  32.3 4.6 %collective-permute-start.5 = (f32[176,128]{1,0:T(8,128)S(1)}, f32[176,128]{1,0:T(8,128)S(1)}, u32[]{:S(2)}, u32[]{:S(2)}) collective-permute-start(f32[176,128]{1,0:T(8,128)S(1)} %get-tuple-element.26), channel_id=1, source_target_pairs={{8,0},{16,8},{24,16},{32,24},{40,32},{48,40},{56,48},{64,56},{72,6... | collective-permute-start | bytes 270344 | tf_op jit(solution)/shard_map/ppermute | solution.py:509
  36.9 0.8 %shard_map.61 = (f32[29,8,128]{2,1,0:T(8,128)S(1)}, f32[29,8,128]{2,1,0:T(8,128)S(1)}) custom-call(f32[29,64,128]{2,1,0:T(8,128)S(1)} %get-tuple-element.20.p_ref, f32[58,8,128]{2,1,0:T(8,128)S(1)} %collective-permute-done.xlo_ref, f32[58,8,128]{2,1,0:T(8,128)S(1)} %collective-permute-done.1.xhi_ref), custom_call_target="tpu_custom_call" | custom-call | tf_op jit(solution)/shard_map/pallas_call | solution.py:549
  37.7 0.0 collective-permute-done.2.ya_ref
  37.7 0.0 collective-permute-done.3.yb_ref
  37.7 0.0 collective-permute-done.4.clo_ref
  37.8 0.7 %collective-permute-done.5.chi_ref = f32[176,128]{1,0:T(8,128)S(1)} collective-permute-done((f32[176,128]{1,0:T(8,128)S(1)}, f32[176,128]{1,0:T(8,128)S(1)}, u32[]{:S(2)}, u32[]{:S(2)}) %collective-permute-start.5) | collective-permute-done | bytes 90144 | tf_op jit(solution)/shard_map/ppermute | solution.py:509
  38.4 0.8 %shard_map.62 = (f32[29,120,128]{2,1,0:T(8,128)S(1)}, f32[29,8,128]{2,1,0:T(8,128)S(1)}, f32[15,16,128]{2,1,0:T(8,128)S(1)}, f32[15,16,128]{2,1,0:T(8,128)S(1)}) custom-call(f32[464,128]{1,0:T(8,128)S(1)} %collective-permute-done.2.ya_ref, f32[464,128]{1,0:T(8,128)S(1)} %collective-permute-done.3.yb_ref, f32[176,128]{1,0:T(8,128)S(1)} %collective-permute-done.4.clo_ref, ...), custom_call_target="tpu_custom_call" | custom-call | tf_op jit(solution)/shard_map/pallas_call | solution.py:551
  39.2 3.8 %collective-permute-start.6 = (f32[15,16,128]{2,1,0:T(8,128)S(1)}, f32[15,16,128]{2,1,0:T(8,128)S(1)}, u32[]{:S(2)}, u32[]{:S(2)}) collective-permute-start(f32[15,16,128]{2,1,0:T(8,128)S(1)} %get-tuple-element.34), channel_id=1, source_target_pairs={{0,1},{1,2},{2,3},{3,4},{4,5},{5,6},{6,7},{7,0},{8,9},{9,10},{10,1... | collective-permute-start | bytes 368648 | tf_op jit(solution)/shard_map/ppermute | solution.py:509
  43.0 0.0 collective-permute-start.7
  43.0 3.1 %shard_map.63 = (f32[27,64,128]{2,1,0:T(8,128)S(1)}, f32[3,232,128]{2,1,0:T(8,128)S(1)}, f32[29,8,128]{2,1,0:T(8,128)S(1)}) custom-call(f32[29,64,128]{2,1,0:T(8,128)S(1)} %get-tuple-element.20.p_ref, f32[58,8,128]{2,1,0:T(8,128)S(1)} %collective-permute-done.xlo_ref, f32[58,8,128]{2,1,0:T(8,128)S(1)} %collective-permute-done.1.xhi_ref, ...), custom_call_target="tpu_custom_call" | custom-call | tf_op jit(solution)/shard_map/pallas_call | solution.py:556
  46.1 0.0 copy-start
  46.1 0.0 collective-permute-done.6.zlo_ref
  46.1 1.1 %collective-permute-done.7.zhi_ref = f32[15,16,128]{2,1,0:T(8,128)S(1)} collective-permute-done((f32[15,16,128]{2,1,0:T(8,128)S(1)}, f32[15,16,128]{2,1,0:T(8,128)S(1)}, u32[]{:S(2)}, u32[]{:S(2)}) %collective-permute-start.7) | collective-permute-done | bytes 122912 | tf_op jit(solution)/shard_map/ppermute | solution.py:509
  47.3 2.4 %shard_map.64 = (f32[27,64,128]{2,1,0:T(8,128)}, f32[8,128]{1,0:T(8,128)S(1)}) custom-call(f32[29,64,128]{2,1,0:T(8,128)S(1)} %get-tuple-element.20.p_ref, f32[27,64,128]{2,1,0:T(8,128)S(1)} %get-tuple-element.29.adv_ref, f32[3,232,128]{2,1,0:T(8,128)S(1)} %get-tuple-element.30.flow_ref, f32[29,8,128]{2,1,0:T(8,128)S(1)} %get-tuple-element.27.main_ref.lmain_ref, ...), custom_call_target="tpu_custom_call" | custom-call | tf_op jit(solution)/shard_map/pallas_call | solution.py:563
  49.6 8.7 %all_to_all.11 = f32[8,1,128]{2,1,0:T(1,128)S(1)} all-to-all(f32[8,1,128]{2,1,0:T(1,128)S(1)} %bitcast.10), channel_id=1, replica_groups=mesh['gx'=8,'gy'=16,'gz'=8] {'gz'}, dimensions={0} | all-to-all | bytes 8192 | tf_op jit(solution)/shard_map/all_to_all | solution.py:577
  58.4 0.0 copy-done
  58.4 0.1 broadcast_in_dim.2.rank_ref
  58.4 0.8 %shard_map.65 = f32[4,4,32]{2,1,0:T(4,128)} custom-call(f32[8,128]{1,0:T(8,128)S(1)} %bitcast.9, s32[8,128]{1,0:T(8,128)S(1)} %broadcast_in_dim.2.rank_ref), custom_call_target="tpu_custom_call" | custom-call | tf_op jit(solution)/shard_map/pallas_call | solution.py:579
Async XLA Ops:
  2.2 28.0 %collective-permute-start = (f32[58,8,128]{2,1,0:T(8,128)S(1)}, f32[58,8,128]{2,1,0:T(8,128)S(1)}, u32[]{:S(2)}, u32[]{:S(2)}) collective-permute-start(f32[58,8,128]{2,1,0:T(8,128)S(1)} %get-tuple-element.21), channel_id=1, source_target_pairs={{0,128},{128,256},{256,384},{384,512},{512,640},{640,768},{768,896... | collective-permute-start | bytes 712712 | tf_op jit(solution)/shard_map/ppermute | solution.py:509
  6.3 24.0 %collective-permute-start.1 = (f32[58,8,128]{2,1,0:T(8,128)S(1)}, f32[58,8,128]{2,1,0:T(8,128)S(1)}, u32[]{:S(2)}, u32[]{:S(2)}) collective-permute-start(f32[58,8,128]{2,1,0:T(8,128)S(1)} %get-tuple-element.22), channel_id=1, source_target_pairs={{128,0},{256,128},{384,256},{512,384},{640,512},{768,640},{896,768... | collective-permute-start | bytes 712712 | tf_op jit(solution)/shard_map/ppermute | solution.py:509
  10.1 27.6 %collective-permute-start.2 = (f32[464,128]{1,0:T(8,128)S(1)}, f32[464,128]{1,0:T(8,128)S(1)}, u32[]{:S(2)}, u32[]{:S(2)}) collective-permute-start(f32[464,128]{1,0:T(8,128)S(1)} %get-tuple-element.23), channel_id=1, source_target_pairs={{0,8},{8,0},{16,24},{24,16},{32,40},{40,32},{48,56},{56,48},{64,72... | collective-permute-start | bytes 712712 | tf_op jit(solution)/shard_map/ppermute | solution.py:520
  14.1 23.6 %collective-permute-start.3 = (f32[464,128]{1,0:T(8,128)S(1)}, f32[464,128]{1,0:T(8,128)S(1)}, u32[]{:S(2)}, u32[]{:S(2)}) collective-permute-start(f32[464,128]{1,0:T(8,128)S(1)} %get-tuple-element.24), channel_id=1, source_target_pairs={{8,16},{16,8},{24,32},{32,24},{40,48},{48,40},{56,64},{64,56},{72,... | collective-permute-start | bytes 712712 | tf_op jit(solution)/shard_map/ppermute | solution.py:520
  30.4 7.4 %collective-permute-start.4 = (f32[176,128]{1,0:T(8,128)S(1)}, f32[176,128]{1,0:T(8,128)S(1)}, u32[]{:S(2)}, u32[]{:S(2)}) collective-permute-start(f32[176,128]{1,0:T(8,128)S(1)} %get-tuple-element.25), channel_id=1, source_target_pairs={{0,8},{8,16},{16,24},{24,32},{32,40},{40,48},{48,56},{56,64},{64,7... | collective-permute-start | bytes 270344 | tf_op jit(solution)/shard_map/ppermute | solution.py:509
  32.3 6.1 %collective-permute-start.5 = (f32[176,128]{1,0:T(8,128)S(1)}, f32[176,128]{1,0:T(8,128)S(1)}, u32[]{:S(2)}, u32[]{:S(2)}) collective-permute-start(f32[176,128]{1,0:T(8,128)S(1)} %get-tuple-element.26), channel_id=1, source_target_pairs={{8,0},{16,8},{24,16},{32,24},{40,32},{48,40},{56,48},{64,56},{72,6... | collective-permute-start | bytes 270344 | tf_op jit(solution)/shard_map/ppermute | solution.py:509
  39.2 6.9 %collective-permute-start.6 = (f32[15,16,128]{2,1,0:T(8,128)S(1)}, f32[15,16,128]{2,1,0:T(8,128)S(1)}, u32[]{:S(2)}, u32[]{:S(2)}) collective-permute-start(f32[15,16,128]{2,1,0:T(8,128)S(1)} %get-tuple-element.34), channel_id=1, source_target_pairs={{0,1},{1,2},{2,3},{3,4},{4,5},{5,6},{6,7},{7,0},{8,9},{9,10},{10,1... | collective-permute-start | bytes 368648 | tf_op jit(solution)/shard_map/ppermute | solution.py:509
  43.0 4.3 %collective-permute-start.7 = (f32[15,16,128]{2,1,0:T(8,128)S(1)}, f32[15,16,128]{2,1,0:T(8,128)S(1)}, u32[]{:S(2)}, u32[]{:S(2)}) collective-permute-start(f32[15,16,128]{2,1,0:T(8,128)S(1)} %get-tuple-element.35), channel_id=1, source_target_pairs={{1,0},{2,1},{3,2},{4,3},{5,4},{6,5},{7,6},{0,7},{9,8},{10,9},{11,1... | collective-permute-start | bytes 368648 | tf_op jit(solution)/shard_map/ppermute | solution.py:509
  46.1 12.2 %copy-start = (s32[8]{0:T(128)S(1)}, s32[8]{0:T(128)}, u32[]{:S(2)}) copy-start(s32[8]{0:T(128)} %param.7) | copy-start | bytes 100
